TPU v7x, 32 devices: a whole 2x2x4 slice. The times are simulated.
32 devices in a mesh: dp: 8 (over z, y), fsdp: 4 (over x, core).
Axes of the slice: x: 2, y: 2, z: 4, core: 2. Of those that a mesh axis runs over, the one named last changes fastest.
Arguments:
- tokens: bfloat16 [12288, 1024], P(('dp', 'fsdp')), may hold values from -6 to 6
- cotangent: bfloat16 [12288, 1024], P(('dp', 'fsdp')), may hold values from -6 to 6
- lengths: int32 [32], P(('dp', 'fsdp')), may hold values from 128 to 384, as said below
- expert_ids: int32 [12288], P(('dp', 'fsdp')), may hold values from 0 to 1, as said below
- slot_ids: int32 [12288], P(('dp', 'fsdp')), may hold values from -1 to 111, as said below
- w_qkv: bfloat16 [1024, 3072], P(('dp', 'fsdp')), may hold values from -0.1875 to 0.1875
- w_out: bfloat16 [1024, 1024], P(('dp', 'fsdp')), may hold values from -3 to 3
- gain_one: bfloat16 [1024], P(('dp', 'fsdp')), may hold values from 0.5 to 1.5
- w_in: bfloat16 [1024, 4096], P(('dp', 'fsdp')), may hold values from -0.1875 to 0.1875
- w_down: bfloat16 [4096, 1024], P(('dp', 'fsdp')), may hold values from -0.09375 to 0.09375
- w_expert_in: bfloat16 [2, 1024, 4096], P(None, ('dp', 'fsdp')), may hold values from -0.1875 to 0.1875
- w_expert_out: bfloat16 [2, 4096, 1024], P(None, ('dp', 'fsdp')), may hold values from -0.09375 to 0.09375
- w_mix: bfloat16 [1024, 2], P(('dp', 'fsdp')), may hold values from -0.1875 to 0.1875
- gain_two: bfloat16 [1024], P(('dp', 'fsdp')), may hold values from 0.5 to 1.5
Outputs:
- block_out: bfloat16 [12288, 1024], P(('dp', 'fsdp'))
- grad_tokens: float32 [12288, 1024], P(('dp', 'fsdp'))
- grad_w_qkv: float32 [1024, 3072], P(('dp', 'fsdp'))
- grad_w_out: float32 [1024, 1024], P(('dp', 'fsdp'))
- grad_gain_one: float32 [1024], P(('dp', 'fsdp'))
- grad_w_in: float32 [1024, 4096], P(('dp', 'fsdp'))
- grad_w_down: float32 [4096, 1024], P(('dp', 'fsdp'))
- grad_w_expert_in: float32 [2, 1024, 4096], P(None, ('dp', 'fsdp'))
- grad_w_expert_out: float32 [2, 4096, 1024], P(None, ('dp', 'fsdp'))
- grad_w_mix: float32 [1024, 2], P(('dp', 'fsdp'))
- grad_gain_two: float32 [1024], P(('dp', 'fsdp'))
Inputs may be any that keep to these rules, and one draw needn't show every extreme that they name: `lengths`: each sequence's real tokens; the other positions of its 384 slots are padding. `expert_ids`: each token's expert. `slot_ids`: among the real tokens of one device with the same expert, in order of position, the slots are 0, 1, 2 and so on; tokens whose count reaches 112 and padding tokens have -1.
All inputs are finite; a program needn't handle non-finite values.
Results may differ from a plain program's by a relative error of at most 0.012.
Values may be sent and summed in bfloat16 or wider, within the bound.
A program may use at most 384 MiB of HBM per device.

v0:
```python
import jax
import jax.numpy as jnp
from jax import lax
from jax.sharding import PartitionSpec as P

HEAD_DIM = 64
EXPERTS = 2
CAP = 112


def layer_norm(values_in, gain_vec):
    average = jnp.mean(values_in, axis=-1, keepdims=True)
    centred = values_in - average
    variance = jnp.mean(centred * centred, axis=-1, keepdims=True)
    return centred * lax.rsqrt(variance + 1e-05) * gain_vec


def gelu_tanh(values_in):
    return jax.nn.gelu(values_in, approximate=True)


def gelu_back(values_in, grad_in):
    return jax.vjp(gelu_tanh, values_in)[1](grad_in)[0]


def head_scores(query_h, key_h, allowed, score_scale):
    scores = (
        jnp.einsum("qd,kd->qk", query_h, key_h, preferred_element_type=jnp.float32) * score_scale
    )
    return jnp.where(allowed, scores, -1e30)


def head_forward(entries, allowed, score_scale):
    query_h, key_h, value_h = entries
    scores = head_scores(query_h, key_h, allowed, score_scale)
    row_max = jnp.max(scores, axis=-1, keepdims=True)
    exp_scores = jnp.exp(scores - row_max)
    row_total = jnp.sum(exp_scores, axis=-1, keepdims=True)
    prob_low = (exp_scores / row_total).astype(jnp.bfloat16)
    head_out = jnp.dot(prob_low, value_h, preferred_element_type=jnp.float32)
    return (head_out, (row_max + jnp.log(row_total))[:, 0])


def head_backward(entries, allowed, score_scale):
    query_h, key_h, value_h, grad_head, log_total = entries
    scores = head_scores(query_h, key_h, allowed, score_scale)
    prob_full = jnp.where(allowed, jnp.exp(scores - log_total[:, None]), 0.0)
    prob_low = prob_full.astype(jnp.bfloat16)
    grad_value = jnp.einsum("qk,qd->kd", prob_low, grad_head, preferred_element_type=jnp.float32)
    grad_prob = jnp.einsum("qd,kd->qk", grad_head, value_h, preferred_element_type=jnp.float32)
    grad_score = prob_full * (grad_prob - jnp.sum(prob_full * grad_prob, axis=-1, keepdims=True))
    grad_score = grad_score.astype(jnp.bfloat16)
    grad_query = jnp.dot(grad_score, key_h, preferred_element_type=jnp.float32) * score_scale
    grad_key = (
        jnp.einsum("qk,qd->kd", grad_score, query_h, preferred_element_type=jnp.float32)
        * score_scale
    )
    return (grad_query, grad_key, grad_value)


def per_device(
    tokens,
    cotangent,
    lengths,
    expert_ids,
    slot_ids,
    w_qkv,
    w_out,
    gain_one,
    w_in,
    w_down,
    w_expert_in,
    w_expert_out,
    w_mix,
    gain_two,
):
    row_count, model_width = tokens.shape
    head_count = model_width // HEAD_DIM
    score_scale = HEAD_DIM ** (-0.5)
    full_qkv, full_out, full_gain_one = (
        lax.all_gather(w_qkv, ("dp", "fsdp"), axis=0, tiled=True),
        lax.all_gather(w_out, ("dp", "fsdp"), axis=0, tiled=True),
        lax.all_gather(gain_one, ("dp", "fsdp"), axis=0, tiled=True),
    )
    full_in, full_down, full_expert_in, full_expert_out, full_mix, full_gain_two = (
        lax.all_gather(w_in, ("dp", "fsdp"), axis=0, tiled=True),
        lax.all_gather(w_down, ("dp", "fsdp"), axis=0, tiled=True),
        lax.all_gather(w_expert_in, ("dp", "fsdp"), axis=1, tiled=True),
        lax.all_gather(w_expert_out, ("dp", "fsdp"), axis=1, tiled=True),
        lax.all_gather(w_mix, ("dp", "fsdp"), axis=0, tiled=True),
        lax.all_gather(gain_two, ("dp", "fsdp"), axis=0, tiled=True),
    )
    position = jnp.arange(row_count, dtype=jnp.int32)
    seq_len = lengths[0]
    row_keep = (position < seq_len).astype(jnp.float32)[:, None]
    allowed = (position[None, :] <= position[:, None]) & (position[None, :] < seq_len)

    def to_heads(block):
        return block.reshape(row_count, head_count, HEAD_DIM).transpose(1, 0, 2)

    def from_heads(block):
        return block.transpose(1, 0, 2).reshape(row_count, model_width)

    stream = tokens.astype(jnp.float32)
    gain_first = full_gain_one.astype(jnp.float32)
    normed_one = layer_norm(stream, gain_first).astype(jnp.bfloat16)
    qkv_all = jnp.dot(normed_one, full_qkv, preferred_element_type=jnp.float32).astype(jnp.bfloat16)
    queries = to_heads(qkv_all[:, :model_width])
    key_heads = to_heads(qkv_all[:, model_width : 2 * model_width])
    value_heads = to_heads(qkv_all[:, 2 * model_width :])
    head_out, log_total = lax.map(
        lambda entries: head_forward(entries, allowed, score_scale),
        (queries, key_heads, value_heads),
    )
    attended = from_heads(head_out).astype(jnp.bfloat16)
    stream_two = stream + jnp.dot(attended, full_out, preferred_element_type=jnp.float32)
    gain_second = full_gain_two.astype(jnp.float32)
    normed_two = layer_norm(stream_two, gain_second).astype(jnp.bfloat16)
    dense_up = jnp.dot(normed_two, full_in, preferred_element_type=jnp.float32)
    dense_act = gelu_tanh(dense_up).astype(jnp.bfloat16)
    dense_out = jnp.dot(dense_act, full_down, preferred_element_type=jnp.float32)
    routed = slot_ids >= 0
    table_row = jnp.where(routed, expert_ids * CAP + slot_ids, 0)
    slot_total = EXPERTS * CAP
    dispatch = (
        (table_row[None, :] == jnp.arange(slot_total, dtype=jnp.int32)[:, None]) & routed[None, :]
    ).astype(jnp.bfloat16)
    buffer = jnp.dot(dispatch, normed_two, preferred_element_type=jnp.float32).astype(jnp.bfloat16)
    buffer = buffer.reshape(EXPERTS, CAP, model_width)
    expert_up = jnp.einsum(
        "ecd,edf->ecf", buffer, full_expert_in, preferred_element_type=jnp.float32
    )
    expert_act = gelu_tanh(expert_up).astype(jnp.bfloat16)
    expert_y = jnp.einsum(
        "ecf,efd->ecd", expert_act, full_expert_out, preferred_element_type=jnp.float32
    )
    expert_y = expert_y.reshape(slot_total, model_width)
    expert_mix = jnp.where(routed[:, None], expert_y[table_row], 0.0)
    logits = jnp.dot(normed_two, full_mix, preferred_element_type=jnp.float32)
    mix_coeff = jax.nn.softmax(logits, axis=-1)
    branch = mix_coeff[:, 0:1] * dense_out + mix_coeff[:, 1:2] * expert_mix
    block_out = ((stream_two + branch) * row_keep).astype(jnp.bfloat16)
    grad_out = cotangent.astype(jnp.float32) * row_keep
    grad_dense = (mix_coeff[:, 0:1] * grad_out).astype(jnp.bfloat16)
    grad_expert = (mix_coeff[:, 1:2] * grad_out).astype(jnp.bfloat16)
    grad_coeff = jnp.stack(
        [jnp.sum(grad_out * dense_out, axis=-1), jnp.sum(grad_out * expert_mix, axis=-1)], axis=-1
    )
    grad_logits = jax.vjp(lambda values_in: jax.nn.softmax(values_in, axis=-1), logits)[1](
        grad_coeff
    )[0]
    full_in, full_down, full_expert_in, full_expert_out, full_mix, full_gain_two = (
        lax.all_gather(w_in, ("dp", "fsdp"), axis=0, tiled=True),
        lax.all_gather(w_down, ("dp", "fsdp"), axis=0, tiled=True),
        lax.all_gather(w_expert_in, ("dp", "fsdp"), axis=1, tiled=True),
        lax.all_gather(w_expert_out, ("dp", "fsdp"), axis=1, tiled=True),
        lax.all_gather(w_mix, ("dp", "fsdp"), axis=0, tiled=True),
        lax.all_gather(gain_two, ("dp", "fsdp"), axis=0, tiled=True),
    )
    gain_second = full_gain_two.astype(jnp.float32)
    grad_w_down = jnp.einsum("tf,td->fd", dense_act, grad_dense, preferred_element_type=jnp.float32)
    grad_dense_act = jnp.einsum(
        "td,fd->tf", grad_dense, full_down, preferred_element_type=jnp.float32
    )
    grad_dense_up = gelu_back(dense_up, grad_dense_act).astype(jnp.bfloat16)
    grad_w_in = jnp.einsum(
        "td,tf->df", normed_two, grad_dense_up, preferred_element_type=jnp.float32
    )
    grad_normed_two = jnp.einsum(
        "tf,df->td", grad_dense_up, full_in, preferred_element_type=jnp.float32
    )
    grad_y = jnp.dot(dispatch, grad_expert, preferred_element_type=jnp.float32).astype(jnp.bfloat16)
    grad_y = grad_y.reshape(EXPERTS, CAP, model_width)
    grad_expert_out_lead = jnp.einsum(
        "ecf,ecd->fed", expert_act, grad_y, preferred_element_type=jnp.float32
    )
    grad_expert_act = jnp.einsum(
        "ecd,efd->ecf", grad_y, full_expert_out, preferred_element_type=jnp.float32
    )
    grad_expert_up = gelu_back(expert_up, grad_expert_act).astype(jnp.bfloat16)
    grad_expert_in_lead = jnp.einsum(
        "ecd,ecf->def", buffer, grad_expert_up, preferred_element_type=jnp.float32
    )
    grad_buffer = jnp.einsum(
        "ecf,edf->ecd", grad_expert_up, full_expert_in, preferred_element_type=jnp.float32
    )
    grad_buffer = grad_buffer.reshape(slot_total, model_width)
    grad_normed_two = grad_normed_two + jnp.where(routed[:, None], grad_buffer[table_row], 0.0)
    mix_full = full_mix.astype(jnp.float32)
    normed_full = normed_two.astype(jnp.float32)
    grad_normed_two = grad_normed_two + jnp.dot(
        grad_logits, mix_full.T, precision=lax.Precision.HIGHEST
    )
    grad_w_mix = jnp.dot(normed_full.T, grad_logits, precision=lax.Precision.HIGHEST)
    _, pull_two = jax.vjp(layer_norm, stream_two, gain_second)
    grad_stream_ln, grad_gain_two = pull_two(grad_normed_two)
    grad_stream_two = grad_out + grad_stream_ln
    full_qkv, full_out, full_gain_one = (
        lax.all_gather(w_qkv, ("dp", "fsdp"), axis=0, tiled=True),
        lax.all_gather(w_out, ("dp", "fsdp"), axis=0, tiled=True),
        lax.all_gather(gain_one, ("dp", "fsdp"), axis=0, tiled=True),
    )
    gain_first = full_gain_one.astype(jnp.float32)
    grad_attn = grad_stream_two.astype(jnp.bfloat16)
    grad_w_out = jnp.einsum("td,te->de", attended, grad_attn, preferred_element_type=jnp.float32)
    grad_attended = jnp.einsum(
        "te,de->td", grad_attn, full_out, preferred_element_type=jnp.float32
    ).astype(jnp.bfloat16)
    grad_query, grad_key, grad_value = lax.map(
        lambda entries: head_backward(entries, allowed, score_scale),
        (queries, key_heads, value_heads, to_heads(grad_attended), log_total),
    )
    grad_qkv = jnp.concatenate(
        [from_heads(grad_query), from_heads(grad_key), from_heads(grad_value)], axis=1
    ).astype(jnp.bfloat16)
    grad_w_qkv = jnp.einsum("td,te->de", normed_one, grad_qkv, preferred_element_type=jnp.float32)
    grad_normed_one = jnp.einsum(
        "te,de->td", grad_qkv, full_qkv, preferred_element_type=jnp.float32
    )
    _, pull_one = jax.vjp(layer_norm, stream, gain_first)
    grad_stream_one, grad_gain_one = pull_one(grad_normed_one)
    grad_tokens = grad_stream_two + grad_stream_one
    (
        part_qkv,
        part_out,
        part_gain_one,
        part_in,
        part_down,
        lead_expert_in,
        lead_expert_out,
        part_mix,
        part_gain_two,
    ) = (
        lax.psum_scatter(grad_w_qkv, ("dp", "fsdp"), scatter_dimension=0, tiled=True),
        lax.psum_scatter(grad_w_out, ("dp", "fsdp"), scatter_dimension=0, tiled=True),
        lax.psum_scatter(grad_gain_one, ("dp", "fsdp"), scatter_dimension=0, tiled=True),
        lax.psum_scatter(grad_w_in, ("dp", "fsdp"), scatter_dimension=0, tiled=True),
        lax.psum_scatter(grad_w_down, ("dp", "fsdp"), scatter_dimension=0, tiled=True),
        lax.psum_scatter(grad_expert_in_lead, ("dp", "fsdp"), scatter_dimension=0, tiled=True),
        lax.psum_scatter(grad_expert_out_lead, ("dp", "fsdp"), scatter_dimension=0, tiled=True),
        lax.psum_scatter(grad_w_mix, ("dp", "fsdp"), scatter_dimension=0, tiled=True),
        lax.psum_scatter(grad_gain_two, ("dp", "fsdp"), scatter_dimension=0, tiled=True),
    )
    part_expert_in = lead_expert_in.transpose(1, 0, 2)
    part_expert_out = lead_expert_out.transpose(1, 0, 2)
    return (
        block_out,
        grad_tokens,
        part_qkv,
        part_out,
        part_gain_one,
        part_in,
        part_down,
        part_expert_in,
        part_expert_out,
        part_mix,
        part_gain_two,
    )


def solution(mesh):
    placed = (
        P(("dp", "fsdp"), None),
        P(("dp", "fsdp"), None),
        P(("dp", "fsdp")),
        P(("dp", "fsdp")),
        P(("dp", "fsdp")),
        P(("dp", "fsdp"), None),
        P(("dp", "fsdp"), None),
        P(("dp", "fsdp")),
        P(("dp", "fsdp"), None),
        P(("dp", "fsdp"), None),
        P(None, ("dp", "fsdp"), None),
        P(None, ("dp", "fsdp"), None),
        P(("dp", "fsdp"), None),
        P(("dp", "fsdp")),
    )
    return jax.shard_map(
        per_device,
        mesh=mesh,
        in_specs=placed,
        out_specs=(
            P(("dp", "fsdp"), None),
            P(("dp", "fsdp"), None),
            P(("dp", "fsdp"), None),
            P(("dp", "fsdp"), None),
            P(("dp", "fsdp")),
            P(("dp", "fsdp"), None),
            P(("dp", "fsdp"), None),
            P(None, ("dp", "fsdp"), None),
            P(None, ("dp", "fsdp"), None),
            P(("dp", "fsdp"), None),
            P(("dp", "fsdp")),
        ),
        check_vma=False,
    )
```

profile of v0, /device:TPU:0, one launch (start us, length us, event | category | flops | bytes accessed | tf_op | source)
XLA Modules:
  0.0 2222.5 jit_solution(11892626151616188621)
XLA Ops:
  13.6 42.2 %all-reduce.6 = (bf16[1024]{0:T(1024)(128)(2,1)S(1)}, bf16[1024]{0:T(1024)(128)(2,1)S(1)}) all-reduce(bf16[1024]{0:T(1024)(128)(2,1)S(1)} %dynamic-update-slice, bf16[1024]{0:T(1024)(128)(2,1)S(1)} %dynamic-update-slice.1), channel_id=1, replica_groups=mesh['dp'=8,'fsdp'=4] {'dp','fsdp'}, use_global_device_ids=true, to_apply=%add | all-reduce | flops 2048 | bytes 8192
  56.9 40.2 %all-gather = bf16[32,32,2]{1,2,0:T(2,128)(2,1)S(1)} all-gather(bf16[1,32,2]{1,2,0:T(2,128)(2,1)S(1)} %bitcast.179), channel_id=1, replica_groups=mesh['dp'=8,'fsdp'=4] {'dp','fsdp'}, dimensions={0}, use_global_device_ids=true | all-gather | bytes 4224 | tf_op jit(solution)/shard_map/all_gather | solution.py:90
  111.0 61.8 %while.28 = (s32[]{:T(128)}, bf16[16,384,64]{1,2,0:T(8,128)(2,1)S(1)}, f32[16,384]{1,0:T(8,128)}, bf16[16,384,64]{2,1,0:T(8,128)(2,1)}, bf16[16,384,64]{2,1,0:T(...) while((s32[]{:T(128)}, ...), condition=%wide.region_5.6_spmd.clone, body=%wide.region_2.5_spmd.clone.sunk | while | flops 39222912 | bytes 2184681 | solution.py:111
  177.9 42.5 %all-gather.12.cloned.1.call-done = bf16[1024,4096]{1,0:T(8,128)(2,1)} async-done(((bf16[32,4096]{1,0:T(8,128)(2,1)}), bf16[1024,4096]{1,0:T(8,128)(2,1)}) %all-gather.12.cloned.1.call-update) | async-done | bytes 8388624 | tf_op jit(solution)/shard_map/all_gather | solution.py:86
  229.2 107.3 %all-gather.18.cloned.1.call-done = bf16[2,4096,1024]{2,1,0:T(8,128)(2,1)} async-done(((bf16[2,128,1024]{2,1,0:T(8,128)(2,1)}), bf16[2,4096,1024]{2,1,0:T(8,128)(2,1)}) %all-gather.18.cloned.1.call-update) | async-done | bytes 16777232 | tf_op jit(solution)/shard_map/all_gather | solution.py:89
  336.5 13.0 fusion.107
  349.5 102.7 %all-gather.16.cloned.1.call-done = bf16[2,1024,4096]{2,1,0:T(8,128)(2,1)} async-done(((bf16[2,32,4096]{2,1,0:T(8,128)(2,1)}), bf16[2,1024,4096]{2,1,0:T(8,128)(2,1)}) %all-gather.16.cloned.1.call-update) | async-done | bytes 16777232 | tf_op jit(solution)/shard_map/all_gather | solution.py:88
  452.2 13.2 fusion.63
  471.4 59.2 %all-gather.14.cloned.1.call-done = bf16[4096,1024]{1,0:T(8,128)(2,1)} async-done(((bf16[128,1024]{1,0:T(8,128)(2,1)}), bf16[4096,1024]{1,0:T(8,128)(2,1)}) %all-gather.14.cloned.1.call-update) | async-done | bytes 8388624 | tf_op jit(solution)/shard_map/all_gather | solution.py:87
  530.6 11.0 multiply_reduce_fusion.4
  543.5 14.7 convolution_bitcast_fusion.3
  558.3 49.4 %copy.57 = f32[1024,2,4096]{2,1,0:T(2,128)} copy(f32[1024,2,4096]{0,2,1:T(8,128)} %convolution_bitcast_fusion.3) | data formatting | bytes 67108864 | tf_op jit(solution)/shard_map/ecd,ecf->def/transpose | solution.py:181
  608.7 15.3 convolution_bitcast_fusion.2
  644.0 11.9 fusion.108
  671.7 115.2 %while.29 = (s32[]{:T(128)}, bf16[16,384,64]{1,2,0:T(8,128)(2,1)S(1)}, bf16[16,384,64]{1,2,0:T(8,128)(2,1)S(1)}, bf16[16,384,64]{1,2,0:T(8,128)(2,1)}, bf16[16,3...) while((s32[]{:T(128)}, ...), condition=%wide.region_17.18_spmd.clone, body=%wide.region_15.17_spmd.clone.sunk | while | flops 96190080 | bytes 5321721 | solution.py:209
  794.9 10.5 fusion.110
  806.7 14.4 fusion.93
  830.0 40.3 %all-reduce.5 = (f32[1024]{0:T(1024)S(1)}, f32[1024]{0:T(1024)S(1)}) all-reduce(f32[1024]{0:T(1024)S(1)} %get-tuple-element.217, f32[1024]{0:T(1024)S(1)} %get-tuple-element.215), channel_id=4, replica_groups=mesh['dp'=8,'fsdp'=4] {'dp','fsdp'}, use_global_device_ids=true, to_apply=%region_23.24.clone | all-reduce | flops 2048 | bytes 16384
  876.1 301.8 %all-reduce.9.cloned.1.call-done = f32[1024,2,4096]{2,1,0:T(2,128)} async-done(((f32[1024,2,4096]{2,1,0:T(2,128)}), f32[1024,2,4096]{2,1,0:T(2,128)}) %all-reduce.9.cloned.1.call-update) | async-done | bytes 33554448
  1180.7 353.3 %reduce-scatter.17.cloned.1.call-done = f32[128,2,1024]{0,2,1:T(8,128)} async-done(((f32[4096,2,1024]{0,2,1:T(8,128)}), f32[128,2,1024]{0,2,1:T(8,128)}) %reduce-scatter.17.cloned.1.call-update) | async-done | bytes 1048592 | tf_op jit(solution)/shard_map/reduce_scatter | solution.py:240
  1536.6 148.7 %reduce-scatter.11.cloned.1.call-done = f32[32,1024]{1,0:T(8,128)} async-done(((f32[1024,1024]{1,0:T(8,128)}), f32[32,1024]{1,0:T(8,128)}) %reduce-scatter.11.cloned.1.call-update) | async-done | bytes 131088 | tf_op jit(solution)/shard_map/reduce_scatter | solution.py:235
  1685.3 158.0 %reduce-scatter.9.cloned.1.call-done = f32[32,3072]{1,0:T(8,128)} async-done(((f32[1024,3072]{1,0:T(8,128)}), f32[32,3072]{1,0:T(8,128)}) %reduce-scatter.9.cloned.1.call-update) | async-done | bytes 393232 | tf_op jit(solution)/shard_map/reduce_scatter | solution.py:234
  1843.3 184.8 %reduce-scatter.13.cloned.1.call-done = f32[32,4096]{1,0:T(8,128)} async-done(((f32[1024,4096]{1,0:T(8,128)}), f32[32,4096]{1,0:T(8,128)}) %reduce-scatter.13.cloned.1.call-update) | async-done | bytes 524304 | tf_op jit(solution)/shard_map/reduce_scatter | solution.py:237
  2028.2 187.3 %reduce-scatter.15.cloned.1.call-done = f32[128,1024]{1,0:T(8,128)} async-done(((f32[4096,1024]{1,0:T(8,128)}), f32[128,1024]{1,0:T(8,128)}) %reduce-scatter.15.cloned.1.call-update) | async-done | bytes 524304 | tf_op jit(solution)/shard_map/reduce_scatter | solution.py:238
  (398 shorter events, 284.1 us)
Async XLA Ops:
  7.2 49.7 %copy-start.41 = (bf16[32,2]{0,1:T(2,128)(2,1)S(1)}, bf16[32,2]{0,1:T(2,128)(2,1)}, u32[]{:S(2)}) copy-start(bf16[32,2]{0,1:T(2,128)(2,1)} %param.30) | copy-start | bytes 388
  7.2 90.0 %copy-start.39 = (s32[384]{0:T(512)S(1)}, s32[384]{0:T(512)}, u32[]{:S(2)}) copy-start(s32[384]{0:T(512)} %param.22) | copy-start | bytes 4612
  7.2 90.0 %copy-start.40 = (s32[384]{0:T(512)S(1)}, s32[384]{0:T(512)}, u32[]{:S(2)}) copy-start(s32[384]{0:T(512)} %param.21) | copy-start | bytes 4612
  7.2 90.0 %all-gather.8.cloned.1.call-start = ((), (), s32[]{:S(2)}) async-start(), calls=%async_computation.6 | async-start | bytes 6488064 | tf_op jit(solution)/shard_map/all_gather | solution.py:81
  8.0 164.8 %all-gather.10.cloned.1.call-start = ((), (), s32[]{:S(2)}) async-start(), calls=%async_computation.7 | async-start | bytes 2162688 | tf_op jit(solution)/shard_map/all_gather | solution.py:82
  8.7 211.6 %all-gather.12.cloned.1.call-start = ((), (), s32[]{:S(2)}) async-start(), calls=%async_computation.8 | async-start | bytes 8650752 | tf_op jit(solution)/shard_map/all_gather | solution.py:86
  9.4 327.1 %all-gather.18.cloned.1.call-start = ((), (), s32[]{:S(2)}) async-start(), calls=%async_computation.11 | async-start | bytes 17301504 | tf_op jit(solution)/shard_map/all_gather | solution.py:89
  10.0 442.2 %all-gather.16.cloned.1.call-start = ((), (), s32[]{:S(2)}) async-start(), calls=%async_computation.10 | async-start | bytes 17301504 | tf_op jit(solution)/shard_map/all_gather | solution.py:88
  10.6 520.0 %all-gather.14.cloned.1.call-start = ((), (), s32[]{:S(2)}) async-start(), calls=%async_computation.9 | async-start | bytes 8650752 | tf_op jit(solution)/shard_map/all_gather | solution.py:87
  11.2 863.5 %reduce-scatter.19.cloned.1.call-start = ((), (), s32[]{:S(2)}) async-start(), calls=%async_computation.17 | async-start | bytes 540672
  56.4 119.7 %copy-start.27 = (f32[1024]{0:T(1024)}, f32[1024]{0:T(1024)S(1)}, u32[]{:S(2)}) copy-start(f32[1024]{0:T(1024)S(1)} %convert_element_type.92) | copy-start | bytes 12292
  97.2 79.2 %copy-start.31 = (bf16[1024,2]{0,1:T(2,128)(2,1)}, bf16[1024,2]{0,1:T(2,128)(2,1)S(1)}, u32[]{:S(2)}) copy-start(bf16[1024,2]{0,1:T(2,128)(2,1)S(1)} %reshape.201) | copy-start | bytes 12292
  177.3 275.0 %copy-start.19 = (bf16[224,1024]{1,0:T(8,128)(2,1)}, bf16[224,1024]{1,0:T(8,128)(2,1)S(1)}, u32[]{:S(2)}) copy-start(bf16[224,1024]{1,0:T(8,128)(2,1)S(1)} %convolution_convert_fusion.3) | copy-start | bytes 1376260
  177.9 158.7 %copy-start.8 = (bf16[224,1024]{1,0:T(8,128)(2,1)}, bf16[224,1024]{1,0:T(8,128)(2,1)S(1)}, u32[]{:S(2)}) copy-start(bf16[224,1024]{1,0:T(8,128)(2,1)S(1)} %convolution_convert_fusion.2) | copy-start | bytes 1376260
  543.5 634.4 %all-reduce.9.cloned.1.call-start = ((), (), s32[]{:S(2)}) async-start(), calls=%async_computation.18 | async-start | bytes 67108864
  607.7 926.4 %reduce-scatter.17.cloned.1.call-start = ((), (), s32[]{:S(2)}) async-start(), calls=%async_computation.16 | async-start | bytes 34603008 | tf_op jit(solution)/shard_map/reduce_scatter | solution.py:240
  624.0 1061.3 %reduce-scatter.11.cloned.1.call-start = ((), (), s32[]{:S(2)}) async-start(), calls=%async_computation.13 | async-start | bytes 4325376 | tf_op jit(solution)/shard_map/reduce_scatter | solution.py:235
  670.4 1172.9 %reduce-scatter.9.cloned.1.call-start = ((), (), s32[]{:S(2)}) async-start(), calls=%async_computation.12 | async-start | bytes 12976128 | tf_op jit(solution)/shard_map/reduce_scatter | solution.py:234
  671.7 115.3 %copy-start.1 = (bf16[384,1024]{1,0:T(8,128)(2,1)S(1)}, bf16[384,1024]{1,0:T(8,128)(2,1)}, u32[]{:S(2)}) copy-start(bf16[384,1024]{1,0:T(8,128)(2,1)} %param.18) | copy-start | bytes 2359300
  671.7 115.3 %copy-start.22 = (f32[1024]{0:T(1024)S(1)}, f32[1024]{0:T(1024)}, u32[]{:S(2)}) copy-start(f32[1024]{0:T(1024)} %copy-done.21) | copy-start | bytes 12292
  671.7 115.3 %copy-start.24 = (f32[384]{0:T(512)S(1)}, f32[384]{0:T(512)}, u32[]{:S(2)}) copy-start(f32[384]{0:T(512)} %copy-done.23) | copy-start | bytes 4612
  671.7 115.3 %copy-start.26 = (f32[384]{0:T(512)S(1)}, f32[384]{0:T(512)}, u32[]{:S(2)}) copy-start(f32[384]{0:T(512)} %copy-done.25) | copy-start | bytes 4612
  794.9 1233.3 %reduce-scatter.13.cloned.1.call-start = ((), (), s32[]{:S(2)}) async-start(), calls=%async_computation.14 | async-start | bytes 17301504 | tf_op jit(solution)/shard_map/reduce_scatter | solution.py:237
  805.5 1410.0 %reduce-scatter.15.cloned.1.call-start = ((), (), s32[]{:S(2)}) async-start(), calls=%async_computation.15 | async-start | bytes 17301504 | tf_op jit(solution)/shard_map/reduce_scatter | solution.py:238
  (33 other events, 334.8 us)
Sparse Core Ops, SparseCore 0:
  10.9 72.3 all-gather.7
  86.1 54.9 all-gather.9
  144.0 76.3 all-gather.11
  223.1 113.3 all-gather.17
  339.3 112.9 all-gather.15
  454.9 75.6 all-gather.13
  543.6 132.5 reduce-scatter.18
  683.7 494.1 all-reduce.8
  1180.1 353.8 reduce-scatter.16
  1536.7 148.5 reduce-scatter.10
  1691.9 151.3 reduce-scatter.8
  1846.1 181.9 reduce-scatter.12
  2031.1 184.3 reduce-scatter.14
where the time goes:
time: 2240 us; the launch traced here: 2220 us
  waiting for transfers between devices  1650 us (74%)
  matrix products  306 us (14%)
  blocking collectives  123 us (5%)
  local copies, waits for them, and re-layouts  117 us (5%)
    reduce_scatter x1, waiting for transfers between devices, per_device(): lax.psum_scatter(grad_expert_out_lead, ('dp', 'fsdp'), scatter_dimension=...  353 us
    unnamed x15, waiting for transfers between devices  306 us
    reduce_scatter x1, waiting for transfers between devices, per_device(): lax.psum_scatter(grad_w_down, ('dp', 'fsdp'), scatter_dimension=0, tiled=...  187 us
    reduce_scatter x1, waiting for transfers between devices, per_device(): lax.psum_scatter(grad_w_in, ('dp', 'fsdp'), scatter_dimension=0, tiled=True)  185 us
    reduce_scatter x1, waiting for transfers between devices, per_device(): lax.psum_scatter(grad_w_qkv, ('dp', 'fsdp'), scatter_dimension=0, tiled=T...  158 us
    reduce_scatter x1, waiting for transfers between devices, per_device(): lax.psum_scatter(grad_w_out, ('dp', 'fsdp'), scatter_dimension=0, tiled=T...  149 us
    all_gather x1, waiting for transfers between devices, per_device(): lax.all_gather(w_expert_out, ('dp', 'fsdp'), axis=1, tiled=True)  107 us
    all_gather x1, waiting for transfers between devices, per_device(): lax.all_gather(w_expert_in, ('dp', 'fsdp'), axis=1, tiled=True)  103 us
  transfers between devices with their start and end apart: 13, of which 10 were waited for; matrix products, arithmetic and copies ran while one was open for 18% of the time, Pallas kernels for 0%

commit v1 on v0

--- a/solution.py
+++ b/solution.py
@@ -1,6 +1,8 @@
 import jax
 import jax.numpy as jnp
 from jax import lax
+from jax.experimental import pallas as pl
+from jax.experimental.pallas import tpu as pltpu
 from jax.sharding import PartitionSpec as P
 
 HEAD_DIM = 64
@@ -258,6 +260,789 @@
     )
 
 
+BF = jnp.bfloat16
+F32 = jnp.float32
+MESH = pl.DeviceIdType.MESH
+ANY = pl.BlockSpec(memory_space=pl.ANY)
+VM = pl.BlockSpec(memory_space=pltpu.VMEM)
+SM = pl.BlockSpec(memory_space=pltpu.SMEM)
+MIB = 1024 * 1024
+
+
+def dot_nn(a, b):
+    return lax.dot_general(a, b, (((1,), (0,)), ((), ())), preferred_element_type=F32)
+
+
+def dot_nt(a, b):
+    return lax.dot_general(a, b, (((1,), (1,)), ((), ())), preferred_element_type=F32)
+
+
+def dot_tn(a, b):
+    return lax.dot_general(a, b, (((0,), (0,)), ((), ())), preferred_element_type=F32)
+
+
+class Place:
+    def __init__(self):
+        dp, fs = lax.axis_index("dp"), lax.axis_index("fsdp")
+        z, y, x, c = dp // 2, dp % 2, fs // 2, fs % 2
+        self.z, self.y, self.x, self.c = z, y, x, c
+        self.own = (y, x, c)
+        self.sib = (y, x, 1 - c)
+        self.d1 = ((y + c) % 2, (x + 1 - c) % 2, c)
+        self.d2 = ((y + 1 - c) % 2, (x + c) % 2, c)
+        self.dd = (1 - y, 1 - x, c)
+        self.zk = [z, z + 1 - 2 * (z % 2), (z + 2) % 4, 3 - z]
+        self.t = self.rank(self.own)
+        self.b = z * 8 + self.t
+
+    @staticmethod
+    def rank(p):
+        return p[0] * 4 + p[1] * 2 + p[2]
+
+    def flip(self, p):
+        return (p[0], p[1], 1 - p[2])
+
+    def dev(self, p, z=None):
+        z = self.z if z is None else z
+        return (z * 2 + p[0], p[1] * 2 + p[2])
+
+    def plane_others(self):
+        y, x, c = self.own
+        return [
+            ((y + k // 4) % 2, (x + (k // 2) % 2) % 2, (c + k % 2) % 2) for k in range(1, 8)
+        ]
+
+
+def rcopy(src, dst, send, recv, dev):
+    return pltpu.make_async_remote_copy(
+        src_ref=src, dst_ref=dst, send_sem=send, recv_sem=recv, device_id=dev, device_id_type=MESH
+    )
+
+
+def meet(devs):
+    bar = pltpu.get_barrier_semaphore()
+    for dev in devs:
+        pl.semaphore_signal(bar, inc=1, device_id=dev, device_id_type=MESH)
+    pl.semaphore_wait(bar, len(devs))
+
+
+def norm_parts(v):
+    mean = jnp.mean(v, axis=-1, keepdims=True)
+    cen = v - mean
+    var = jnp.mean(cen * cen, axis=-1, keepdims=True)
+    r = lax.rsqrt(var + 1e-05)
+    return cen * r, r
+
+
+def row_of(extra, lane):
+    pick = (lax.broadcasted_iota(jnp.int32, (8, 128), 1) == lane).astype(BF)
+    return dot_nt(pick, extra)[0:1]
+
+
+PW = 4224
+EX = 3072
+WO = 3200
+
+
+def enter_kernel(
+    len_ref, tok, pack, wia, wdn, gt,
+    qkv, lse, att, s2, nt, n1, wmix, pack_all, wi_all, wd_all, g_all,
+    pack_v, ps, pr, asend, arecv, fsend, fri, frd, gs, gr, lsem,
+):
+    P_ = Place()
+    z, t, b = P_.z, P_.t, P_.b
+    own, sib, d1, d2, dd = P_.own, P_.sib, P_.d1, P_.d2, P_.dd
+    others = P_.plane_others()
+    meet([P_.dev(p) for p in others] + [P_.dev(own, zz) for zz in P_.zk[1:]])
+    sends = []
+
+    def go(cp):
+        cp.start()
+        sends.append(cp)
+
+    lc = pltpu.make_async_copy(pack, pack_v.at[b], lsem.at[0])
+    lc.start()
+    for k in range(1, 4):
+        go(rcopy(pack, pack_v.at[b], ps.at[k - 1], pr.at[b], P_.dev(own, P_.zk[k])))
+    go(rcopy(pack, pack_v.at[b], ps.at[3], pr.at[b], P_.dev(d1)))
+    go(rcopy(pack, pack_v.at[b], ps.at[7], pr.at[b], P_.dev(d2)))
+    go(rcopy(pack, pack_v.at[b], ps.at[15], pr.at[b], P_.dev(sib)))
+    rows = pl.ds(pl.multiple_of(t * 32, 32), 32)
+    lw = pltpu.make_async_copy(wia.at[t], wi_all.at[:, z, rows], lsem.at[1])
+    lw.start()
+    for i, p in enumerate(others):
+        go(rcopy(wia.at[P_.rank(p)], wi_all.at[:, z, rows], asend.at[i], arecv.at[t], P_.dev(p)))
+    ld = pltpu.make_async_copy(wdn, wd_all.at[:, z], lsem.at[2])
+    ld.start()
+
+    def landed(slot):
+        rcopy(pack, pack_v.at[slot], ps.at[0], pr.at[slot], P_.dev(sib)).wait_recv()
+
+    def fwd(slot, sem, p):
+        go(rcopy(pack_v.at[slot], pack_v.at[slot], ps.at[sem], pr.at[slot], P_.dev(p)))
+
+    def slot(k, p):
+        return P_.zk[k] * 8 + P_.rank(p)
+
+    for k in range(0, 6):
+        if 1 <= k <= 3:
+            s = slot(k, own)
+            landed(s)
+            fwd(s, 3 + k, d1)
+            fwd(s, 7 + k, d2)
+            fwd(s, 15 + k, sib)
+        if k == 3:
+            lw.wait()
+            ld.wait()
+            for p in others:
+                rr = P_.rank(p)
+                rq = pl.ds(pl.multiple_of(rr * 32, 32), 32)
+                rcopy(
+                    wia.at[0], wi_all.at[:, z, rq], asend.at[0], arecv.at[rr], P_.dev(sib)
+                ).wait_recv()
+            for kd in range(3):
+                for j in range(1, 4):
+                    zz = P_.dev(own, P_.zk[j])
+                    i = kd * 6 + (j - 1) * 2
+                    go(rcopy(wi_all.at[kd, z], wi_all.at[kd, z], fsend.at[i], fri.at[kd, z], zz))
+                    go(rcopy(wdn.at[kd], wd_all.at[kd, z], fsend.at[i + 1], frd.at[kd, z], zz))
+        if 1 <= k <= 4:
+            s = slot(k - 1, d1)
+            landed(s)
+            fwd(s, 11 + k - 1, d2)
+            fwd(s, 19 + k - 1, sib)
+            s = slot(k - 1, d2)
+            landed(s)
+            fwd(s, 23 + k - 1, sib)
+        if k >= 2:
+            s = slot(k - 2, dd)
+            landed(s)
+            fwd(s, 27 + k - 2, sib)
+    lg = pltpu.make_async_copy(gt, g_all.at[t], lsem.at[3])
+    lg.start()
+    for i, p in enumerate((d1, d2, sib)):
+        go(rcopy(gt, g_all.at[t], gs.at[i], gr.at[t], P_.dev(p)))
+    stream = tok[...].astype(F32)
+    for k in range(4):
+        for p in (own, d1, d2, dd):
+            landed(slot(k, P_.flip(p)))
+    lc.wait()
+    keep_all = pltpu.make_async_copy(pack_v, pack_all, lsem.at[0])
+    keep_all.start()
+
+    extra = pack_v[:, :, EX : EX + 128].reshape(1024, 128)
+    wmix[...] = extra
+    n_one, _ = norm_parts(stream)
+    n1[...] = (n_one * row_of(extra, 2)).astype(BF)
+
+    def qkv_step(j, carry):
+        cols = pl.ds(pl.multiple_of(j * 512, 512), 512)
+        qkv[:, cols] = dot_nn(n1[...], pack_v[:, :, cols].reshape(1024, 512)).astype(BF)
+        return carry
+
+    lax.fori_loop(0, 6, qkv_step, 0)
+
+    def g_landed(p):
+        r = P_.rank(p)
+        rcopy(gt, g_all.at[r], gs.at[0], gr.at[r], P_.dev(sib)).wait_recv()
+        return r
+
+    def g_fwd(r, i, p):
+        go(rcopy(g_all.at[r], g_all.at[r], gs.at[i], gr.at[r], P_.dev(p)))
+
+    r = g_landed(d1)
+    g_fwd(r, 3, d2)
+    g_fwd(r, 4, sib)
+
+    allowed = masks(len_ref[0])
+    lane = lax.broadcasted_iota(jnp.int32, (384, 128), 1)
+    lse[...] = jnp.zeros_like(lse)
+
+    def pair_step(p, carry):
+        q2 = qkv[:, pl.ds(pl.multiple_of(p * 128, 128), 128)]
+        k2 = qkv[:, pl.ds(pl.multiple_of(1024 + p * 128, 128), 128)]
+        v2 = qkv[:, pl.ds(pl.multiple_of(2048 + p * 128, 128), 128)]
+        outs = []
+        for hh in range(2):
+            qm = jnp.where(lane // 64 == hh, q2, jnp.zeros_like(q2))
+            sc = jnp.where(allowed, dot_nt(qm, k2) * 0.125, -1e30)
+            top = jnp.max(sc, axis=-1, keepdims=True)
+            ex = jnp.exp(sc - top)
+            tot = jnp.sum(ex, axis=-1, keepdims=True)
+            outs.append(dot_nn((ex * (1.0 / tot)).astype(BF), v2))
+            lse[...] = jnp.where(lane == 2 * p + hh, top + jnp.log(tot), lse[...])
+        att[:, pl.ds(pl.multiple_of(p * 128, 128), 128)] = jnp.where(
+            lane < 64, outs[0], outs[1]
+        ).astype(BF)
+        return carry
+
+    lax.fori_loop(0, 8, pair_step, 0)
+    r = g_landed(d2)
+    g_fwd(r, 5, sib)
+    for j in range(2):
+        w = pack_v[:, :, WO + j * 512 : WO + (j + 1) * 512].reshape(1024, 512)
+        s2[:, j * 512 : (j + 1) * 512] = stream[:, j * 512 : (j + 1) * 512] + dot_nn(att[...], w)
+    n_two, _ = norm_parts(s2[...])
+    nt[...] = (n_two * row_of(extra, 3)).astype(BF)
+    r = g_landed(dd)
+    g_fwd(r, 6, sib)
+    for p in (own, d1, d2, dd):
+        g_landed(P_.flip(p))
+    for kd in range(3):
+        for j in range(1, 4):
+            zz = P_.zk[j]
+            rcopy(wi_all.at[kd, zz], wi_all.at[kd, zz], fsend.at[0], fri.at[kd, zz], P_.dev(sib)).wait_recv()
+            rcopy(wdn.at[kd], wd_all.at[kd, zz], fsend.at[0], frd.at[kd, zz], P_.dev(sib)).wait_recv()
+    lg.wait()
+    keep_all.wait()
+    for cp in sends:
+        cp.wait_send()
+
+
+def masks(seq_len):
+    row = lax.broadcasted_iota(jnp.int32, (384, 384), 0)
+    col = lax.broadcasted_iota(jnp.int32, (384, 384), 1)
+    return (col <= row) & (col < seq_len)
+
+
+def run_enter(lengths, tok, pack, wia, wdn, gt):
+    sd = jax.ShapeDtypeStruct
+    return pl.pallas_call(
+        enter_kernel,
+        out_shape=(
+            sd((384, 3072), BF), sd((384, 128), F32), sd((384, 1024), BF), sd((384, 1024), F32),
+            sd((384, 1024), BF), sd((384, 1024), BF), sd((1024, 128), BF),
+            sd((32, 32, PW), BF), sd((3, 4, 256, 512), BF), sd((3, 4, 128, 1024), BF),
+            sd((8, 400, 1024), BF),
+        ),
+        in_specs=[SM, VM, ANY, ANY, ANY, ANY],
+        out_specs=(VM,) * 7 + (ANY,) * 4,
+        scratch_shapes=[
+            pltpu.VMEM((32, 32, PW), BF),
+            pltpu.SemaphoreType.DMA((31,)), pltpu.SemaphoreType.DMA((32,)),
+            pltpu.SemaphoreType.DMA((7,)), pltpu.SemaphoreType.DMA((8,)),
+            pltpu.SemaphoreType.DMA((18,)), pltpu.SemaphoreType.DMA((3, 4)),
+            pltpu.SemaphoreType.DMA((3, 4)),
+            pltpu.SemaphoreType.DMA((7,)), pltpu.SemaphoreType.DMA((8,)),
+            pltpu.SemaphoreType.DMA((4,)),
+        ],
+        compiler_params=pltpu.CompilerParams(
+            collective_id=0, has_side_effects=True, vmem_limit_bytes=48 * MIB
+        ),
+    )(lengths, tok, pack, wia, wdn, gt)
+
+
+def mix_of(logits):
+    delta = logits[:, 0:1] - logits[:, 1:2]
+    return 1.0 / (1.0 + jnp.exp(-delta)), 1.0 / (1.0 + jnp.exp(delta))
+
+
+def gelu_both(u):
+    a, bb = 0.7978845608028654, 0.044715
+    u2 = u * u
+    th = jnp.tanh(a * u * (1.0 + bb * u2))
+    half = 0.5 * (1.0 + th)
+    return u * half, half + 0.5 * u * (1.0 - th * th) * a * (1.0 + 3.0 * bb * u2)
+
+
+def ff_kernel(
+    len_ref, nt_own, wmix, s2, g_all, wi_all, wd_all,
+    block, gsum, gl_out, gdo, gx, r1, r2, rin, rdn,
+    nt_all, gbuf, br, gn, xb, yb, logit, wi, wd, ai, ad, gin, gdn, tmp, gc, gcr, dots, tabs,
+    ts, tr, gsem, wsem, fs_, fri, frd, s1s, s1r, s2s, s2r, cs, cr, xsd, xrv, lsem,
+):
+    P_ = Place()
+    z, t = P_.z, P_.t
+    own, sib, d1, d2, dd = P_.own, P_.sib, P_.d1, P_.d2, P_.dd
+    others = P_.plane_others()
+    meet([P_.dev(p) for p in others] + [P_.dev(own, zz) for zz in P_.zk[1:]])
+    sends = []
+
+    def go(cp):
+        cp.start()
+        sends.append(cp)
+
+    ln = pltpu.make_async_copy(nt_own, nt_all.at[t], lsem.at[1])
+    ln.start()
+    for i, p in enumerate((d1, d2, sib)):
+        go(rcopy(nt_own, nt_all.at[t], ts.at[i], tr.at[t], P_.dev(p)))
+    def w_load(kd):
+        return (
+            pltpu.make_async_copy(wi_all.at[kd], wi.at[kd % 2], wsem.at[kd, 0]),
+            pltpu.make_async_copy(wd_all.at[kd], wd.at[kd % 2], wsem.at[kd, 1]),
+        )
+
+    for kd in range(2):
+        for cp in w_load(kd):
+            cp.start()
+
+    g_tab = pltpu.make_async_copy(g_all.at[:, 384:400], tabs, lsem.at[2])
+    g_tab.start()
+    s2_in = pltpu.make_async_copy(s2, gsum, lsem.at[3])
+    s2_in.start()
+
+    def w_landed(kd):
+        for cp in w_load(kd):
+            cp.wait()
+
+    order = (own, sib, d1, P_.flip(d2), d2, P_.flip(d1), dd, P_.flip(dd))
+    ranks = [P_.rank(p) for p in order]
+
+    def seq_at(i):
+        s = ranks[0]
+        for k in range(1, 8):
+            s = jnp.where(i == k, ranks[k], s)
+        return s
+
+    def g_copy(i):
+        return pltpu.make_async_copy(g_all.at[seq_at(i)], gbuf.at[i % 2], gsem.at[i % 2])
+
+    def ff(xv, gv, kd):
+        wiv = wi[kd % 2].reshape(1024, 512)
+        wdv = wd[kd % 2].reshape(512, 1024)
+        act, dact = gelu_both(dot_nn(xv, wiv))
+        act = act.astype(BF)
+        gup = (dact * dot_nt(gv, wdv)).astype(BF)
+        ad[...] += dot_tn(act, gv)
+        ai[...] += dot_tn(xv, gup)
+        return dot_nn(act, wdv), dot_nt(gup, wiv)
+
+    lane = lax.broadcasted_iota(jnp.int32, (448, 128), 1)
+
+    def clear():
+        ad[...] = jnp.zeros_like(ad)
+        ai[...] = jnp.zeros_like(ai)
+
+    def ship(kd):
+        gin[kd] = ai[...].astype(BF).reshape(4, 256, 512)
+        gdn[kd] = ad[...].astype(BF).reshape(4, 128, 1024)
+        for j in range(1, 4):
+            zz = P_.zk[j]
+            i = kd * 6 + (j - 1) * 2
+            go(rcopy(gin.at[kd, zz], rin.at[kd, j - 1], fs_.at[i], fri.at[kd, j - 1], P_.dev(own, zz)))
+            go(rcopy(gdn.at[kd, zz], rdn.at[kd, j - 1], fs_.at[i + 1], frd.at[kd, j - 1], P_.dev(own, zz)))
+
+    def shares(tab, e):
+        slot = lax.broadcasted_iota(jnp.int32, (112, 384), 0) + e * 112
+        return (tab == slot.astype(F32)).astype(BF)
+
+    fwds = {2: (d1, ((3, d2), (4, sib))), 4: (d2, ((5, sib),)), 6: (dd, ((6, sib),))}
+
+    def fwd_copy(p, i, q):
+        r = P_.rank(p)
+        return rcopy(nt_all.at[r], nt_all.at[r], ts.at[i], tr.at[r], P_.dev(q))
+
+    g_copy(0).start()
+    clear()
+    w_landed(0)
+    ln.wait()
+
+    def seq_step(i, carry):
+        s = seq_at(i)
+
+        @pl.when(i + 1 < 8)
+        def _():
+            g_copy(i + 1).start()
+
+        @pl.when(i > 0)
+        def _():
+            rcopy(nt_own, nt_all.at[s], ts.at[0], tr.at[s], P_.dev(sib)).wait_recv()
+
+        for k, (p, dests) in fwds.items():
+
+            @pl.when(i == k)
+            def _():
+                for n, q in dests:
+                    fwd_copy(p, n, q).start()
+
+        g_copy(i).wait()
+        xv = nt_all[s]
+        gv = gbuf[i % 2, :384]
+        tab = gbuf[i % 2, 384:400][0:1, :384].astype(F32)
+        lg = dot_nn(xv, wmix[...])
+        logit[s] = lg
+        m0, m1 = mix_of(lg)
+        gf = gv.astype(F32)
+        out, gxv = ff(xv, (m0 * gf).astype(BF), 0)
+        br[s] = (m0 * out).astype(BF)
+        gn[s] = gxv.astype(BF)
+        col = jnp.broadcast_to(jnp.sum(gf * out, axis=-1, keepdims=True), (384, 128))
+        gc[s, 0:8] = jnp.transpose(col)[0:8]
+        ge = (m1 * gf).astype(BF)
+        for e in range(2):
+            sh = shares(tab, e)
+            xb[e, s] = dot_nn(sh, xv).astype(BF)
+            yb[e, s] = dot_nn(sh, ge).astype(BF)
+        return carry
+
+    lax.fori_loop(0, 8, seq_step, 0)
+    for k, (p, dests) in fwds.items():
+        for n, q in dests:
+            fwd_copy(p, n, q).wait_send()
+    for cp in w_load(2):
+        cp.start()
+    ship(0)
+
+    for e in range(2):
+        clear()
+        w_landed(1 + e)
+
+        def ex_step(q, carry):
+            four = pl.ds(q * 4, 4)
+            gq = yb[e, four].reshape(448, 1024)
+            yv, gb = ff(xb[e, four].reshape(448, 1024), gq, 1 + e)
+            rs = jnp.sum(gq.astype(F32) * yv, axis=-1, keepdims=True)
+            high = rs.astype(BF).astype(F32)
+            dots[e, four] = (
+                jnp.where(lane == 0, high, jnp.where(lane == 1, rs - high, 0.0))
+                .astype(BF)
+                .reshape(4, 112, 128)
+            )
+            xb[e, four] = yv.astype(BF).reshape(4, 112, 1024)
+            yb[e, four] = gb.astype(BF).reshape(4, 112, 1024)
+            return carry
+
+        lax.fori_loop(0, 2, ex_step, 0)
+        ship(1 + e)
+
+    g_tab.wait()
+
+    def mix_step(s, carry):
+        tab = tabs[s][0:1, :384].astype(F32)
+        _, m1 = mix_of(logit[s])
+        s0, s1 = shares(tab, 0), shares(tab, 1)
+        em = dot_tn(s0, xb[0, s]) + dot_tn(s1, xb[1, s])
+        gb = dot_tn(s0, yb[0, s]) + dot_tn(s1, yb[1, s])
+        q1 = dot_tn(s0, dots[0, s]) + dot_tn(s1, dots[1, s])
+        gc[s, 8:16] = jnp.transpose(jnp.broadcast_to(q1[:, 0:1] + q1[:, 1:2], (384, 128)))[0:8]
+        br[s] = (br[s].astype(F32) + m1 * em).astype(BF)
+        gn[s] = (gn[s].astype(F32) + gb).astype(BF)
+        return carry
+
+    lax.fori_loop(0, 8, mix_step, 0)
+    for i, p in enumerate(others):
+        go(rcopy(gc.at[P_.rank(p)], gcr.at[t], cs.at[i], cr.at[t], P_.dev(p)))
+
+    chips = (dd, d1, d2, own)
+    both = (gn, br)
+    for q in range(4):
+        r = P_.rank(P_.flip(chips[q]))
+        for w in range(2):
+            i = w * 4 + q
+            go(rcopy(both[w].at[r], r1.at[w, (0, 2, 1, 3)[q]], s1s.at[i], s1r.at[w, (0, 2, 1, 3)[q]], P_.dev(sib)))
+
+    def add_in(w, r, src):
+        cp = pltpu.make_async_copy(src, tmp, lsem.at[0])
+        cp.start()
+        cp.wait()
+        both[w][r] = (both[w][r].astype(F32) + tmp[...].astype(F32)).astype(BF)
+
+    def in1(w, q):
+        rcopy(nt_own, r1.at[w, q], s1s.at[0], s1r.at[w, q], P_.dev(sib)).wait_recv()
+        add_in(w, P_.rank(chips[q]), r1.at[w, q])
+
+    def out2(w, q, k, p):
+        src = both[w].at[P_.rank(chips[q])]
+        go(rcopy(src, r2.at[w, k], s2s.at[w * 3 + k], s2r.at[w, k], P_.dev(p)))
+
+    def in2(w, k, p):
+        rcopy(nt_own, r2.at[w, k], s2s.at[0], s2r.at[w, k], P_.dev(sib)).wait_recv()
+        add_in(w, P_.rank(p), r2.at[w, k])
+
+    for w in range(2):
+        in1(w, 0)
+        out2(w, 0, 0, d2)
+        in1(w, 2)
+        out2(w, 2, 2, d2)
+        in1(w, 1)
+        in1(w, 3)
+    for w in range(2):
+        in2(w, 0, d1)
+        out2(w, 1, 1, d1)
+    for w in range(2):
+        in2(w, 2, own)
+        in2(w, 1, own)
+    s2_in.wait()
+    branch = br[t].astype(F32)
+    keep = (lax.broadcasted_iota(jnp.int32, (384, 1), 0) < len_ref[0]).astype(F32)
+    block[...] = ((gsum[...] + branch) * keep).astype(BF)
+    gsum[...] = gn[t].astype(F32)
+    for p in others:
+        r = P_.rank(p)
+        rcopy(gc.at[0], gcr.at[r], cs.at[0], cr.at[r], P_.dev(sib)).wait_recv()
+    gcr[t] = gc[t]
+    tot = jnp.sum(gcr[...], axis=0)
+    gc0 = jnp.transpose(jnp.broadcast_to(tot[0:1], (128, 384)))
+    q1 = jnp.transpose(jnp.broadcast_to(tot[8:9], (128, 384)))
+    m0, m1 = mix_of(logit[t])
+    gl_out[...] = m0 * (m1 * gc0 - q1)
+
+    for kd in range(3):
+        acc_i = gin[kd, z].astype(F32)
+        acc_d = gdn[kd, z].astype(F32)
+        for j in range(3):
+            rcopy(gin.at[kd, 0], rin.at[kd, j], fs_.at[0], fri.at[kd, j], P_.dev(sib)).wait_recv()
+            rcopy(gdn.at[kd, 0], rdn.at[kd, j], fs_.at[0], frd.at[kd, j], P_.dev(sib)).wait_recv()
+            li = pltpu.make_async_copy(rin.at[kd, j], nt_all.at[j, 0:256, 0:512], lsem.at[0])
+            lj = pltpu.make_async_copy(rdn.at[kd, j], nt_all.at[3, 0:128], lsem.at[1])
+            li.start()
+            lj.start()
+            li.wait()
+            lj.wait()
+            acc_i += nt_all[j, 0:256, 0:512].astype(F32)
+            acc_d += nt_all[3, 0:128].astype(F32)
+        gin[kd, z] = acc_i.astype(BF)
+        ad[kd * 128 : (kd + 1) * 128] = acc_d
+    lgd = pltpu.make_async_copy(ad.at[0:384], gdo, lsem.at[0])
+    lgd.start()
+
+    def rows(p):
+        return pl.ds(pl.multiple_of(P_.rank(p) * 32, 32), 32)
+
+    lx = pltpu.make_async_copy(gin.at[:, z, rows(own)], gx.at[t], lsem.at[1])
+    lx.start()
+    for i, p in enumerate(others):
+        go(rcopy(gin.at[:, z, rows(p)], gx.at[t], xsd.at[i], xrv.at[t], P_.dev(p)))
+    for p in others:
+        r = P_.rank(p)
+        rcopy(gin.at[:, z, rows(own)], gx.at[r], xsd.at[0], xrv.at[r], P_.dev(sib)).wait_recv()
+    lx.wait()
+    lgd.wait()
+    for cp in sends:
+        cp.wait_send()
+
+
+def run_ff(lengths, nt, wmix, s2, g_all, wi_all, wd_all):
+    sd = jax.ShapeDtypeStruct
+    dma = pltpu.SemaphoreType.DMA
+    out = pl.pallas_call(
+        ff_kernel,
+        out_shape=(
+            sd((384, 1024), BF), sd((384, 1024), F32), sd((384, 128), F32), sd((384, 1024), F32),
+            sd((8, 3, 32, 512), BF), sd((2, 4, 384, 1024), BF), sd((2, 3, 384, 1024), BF),
+            sd((3, 3, 256, 512), BF), sd((3, 3, 128, 1024), BF),
+        ),
+        in_specs=[SM, ANY, VM, ANY, ANY, ANY, ANY],
+        out_specs=(VM,) * 3 + (ANY,) * 6,
+        scratch_shapes=[
+            pltpu.VMEM((8, 384, 1024), BF), pltpu.VMEM((2, 400, 1024), BF),
+            pltpu.VMEM((8, 384, 1024), BF), pltpu.VMEM((8, 384, 1024), BF),
+            pltpu.VMEM((2, 8, 112, 1024), BF), pltpu.VMEM((2, 8, 112, 1024), BF),
+            pltpu.VMEM((8, 384, 128), F32),
+            pltpu.VMEM((2, 4, 256, 512), BF), pltpu.VMEM((2, 4, 128, 1024), BF),
+            pltpu.VMEM((1024, 512), F32), pltpu.VMEM((512, 1024), F32),
+            pltpu.VMEM((3, 4, 256, 512), BF), pltpu.VMEM((3, 4, 128, 1024), BF),
+            pltpu.VMEM((384, 1024), BF),
+            pltpu.VMEM((8, 16, 384), F32), pltpu.VMEM((8, 16, 384), F32), pltpu.VMEM((2, 8, 112, 128), BF),
+            pltpu.VMEM((8, 16, 1024), BF),
+            dma((7,)), dma((8,)), dma((2,)), dma((3, 2)), dma((18,)), dma((3, 3)), dma((3, 3)),
+            dma((8,)), dma((2, 4)), dma((6,)), dma((2, 3)), dma((7,)), dma((8,)),
+            dma((7,)), dma((8,)), dma((4,)),
+        ],
+        compiler_params=pltpu.CompilerParams(
+            collective_id=1, has_side_effects=True, vmem_limit_bytes=63 * MIB
+        ),
+    )(lengths, nt, wmix, s2, g_all, wi_all, wd_all)
+    return out[:5]
+
+
+def back_kernel(
+    len_ref, tok, gt, s2, nt, n1, qkv, lse, att, gsum, gl, pack_all,
+    gtok, gpack,
+    pack_v, gq, gacc, gst, rs1, rs2, rs3, s1s, s1r, s2s, s2r, s3s, s3r, lsem,
+):
+    P_ = Place()
+    z, t, b, c = P_.z, P_.t, P_.b, P_.c
+    own, sib, d1, d2, dd = P_.own, P_.sib, P_.d1, P_.d2, P_.dd
+    meet([P_.dev(p) for p in (d1, d2, sib)] + [P_.dev(own, zz) for zz in P_.zk[1:]])
+    sends = []
+
+    def go(cp):
+        cp.start()
+        sends.append(cp)
+
+    lw = pltpu.make_async_copy(pack_all, pack_v, lsem.at[0])
+    lw.start()
+    lw.wait()
+    extra = pack_v[:, :, EX : EX + 128].reshape(1024, 128)
+    lane = lax.broadcasted_iota(jnp.int32, (384, 128), 1)
+    glv = gl[...]
+    gnt = gsum[...] + glv[:, 0:1] * (row_of(extra, 0) - row_of(extra, 1))
+    two = jnp.where(lane == 0, glv, jnp.where(lane == 1, -glv, 0.0)).astype(BF)
+    n_two, r_two = norm_parts(s2[...])
+    gain_two_row = jnp.sum(gnt * n_two, axis=0, keepdims=True)
+
+    def norm_back(gv, gain, n, r):
+        tt = gv * gain
+        return r * (tt - jnp.mean(tt, -1, keepdims=True) - n * jnp.mean(tt * n, -1, keepdims=True))
+
+    gs2 = gt[0:384].astype(F32) + norm_back(gnt, row_of(extra, 3), n_two, r_two)
+    gtok[...] = gs2
+    ga = gs2.astype(BF)
+    for j in range(2):
+        cols = slice(j * 512, (j + 1) * 512)
+        gst[:, :, WO + j * 512 : WO + (j + 1) * 512] = (
+            dot_tn(att[...], ga[:, cols]).astype(BF).reshape(32, 32, 512)
+        )
+    gatt = dot_nt(ga[:, 0:512], pack_v[:, :, WO : WO + 512].reshape(1024, 512))
+    gatt += dot_nt(ga[:, 512:1024], pack_v[:, :, WO + 512 : WO + 1024].reshape(1024, 512))
+    gq[:, 0:1024] = gatt.astype(BF)
+    allowed = masks(len_ref[0])
+
+    def pair_step(p, carry):
+        lo = pl.ds(pl.multiple_of(p * 128, 128), 128)
+        mid = pl.ds(pl.multiple_of(1024 + p * 128, 128), 128)
+        hi = pl.ds(pl.multiple_of(2048 + p * 128, 128), 128)
+        q2, k2, v2, do = qkv[:, lo], qkv[:, mid], qkv[:, hi], gq[:, lo]
+        dq = dk = dv = None
+        for hh in range(2):
+            mine = lane // 64 == hh
+            zero = jnp.zeros_like(q2)
+            qm, km, dm = (jnp.where(mine, v, zero) for v in (q2, k2, do))
+            total = jnp.sum(jnp.where(lane == 2 * p + hh, lse[...], 0.0), axis=-1, keepdims=True)
+            sc = dot_nt(qm, k2) * 0.125
+            pf = jnp.where(allowed, jnp.exp(sc - total), 0.0)
+            gp = dot_nt(dm, v2)
+            ds = (pf * (gp - jnp.sum(pf * gp, axis=-1, keepdims=True))).astype(BF)
+            terms = (dot_nn(ds, km), dot_tn(ds, qm), dot_tn(pf.astype(BF), dm))
+            dq, dk, dv = terms if hh == 0 else (dq + terms[0], dk + terms[1], dv + terms[2])
+        gq[:, lo] = (dq * 0.125).astype(BF)
+        gq[:, mid] = (dk * 0.125).astype(BF)
+        gq[:, hi] = dv.astype(BF)
+        return carry
+
+    lax.fori_loop(0, 8, pair_step, 0)
+
+    def w_step(j, carry):
+        cols = pl.ds(pl.multiple_of(j * 512, 512), 512)
+        gcols = gq[:, cols]
+        gst[:, :, cols] = dot_tn(n1[...], gcols).astype(BF).reshape(32, 32, 512)
+        gacc[...] += dot_nt(gcols, pack_v[:, :, cols].reshape(1024, 512))
+        return carry
+
+    gacc[...] = jnp.zeros_like(gacc)
+    lax.fori_loop(0, 6, w_step, 0)
+    gn1 = gacc[...]
+    n_one, r_one = norm_parts(tok[...].astype(F32))
+    gain_one_row = jnp.sum(gn1 * n_one, axis=0, keepdims=True)
+    gtok[...] += norm_back(gn1, row_of(extra, 2), n_one, r_one)
+    rowi = lax.broadcasted_iota(jnp.int32, (8, 1024), 0)
+    rows = jnp.where(rowi == 0, gain_one_row, jnp.where(rowi == 1, gain_two_row, 0.0)).astype(BF)
+    sel = (
+        lax.broadcasted_iota(jnp.int32, (8, 128), 1) == lax.broadcasted_iota(jnp.int32, (8, 128), 0) + 2
+    ).astype(BF)
+    gst[:, :, EX : EX + 128] = (
+        (dot_tn(nt[...], two) + dot_tn(rows, sel)).astype(BF).reshape(32, 32, 128)
+    )
+
+    chips = (dd, d1, d2, own)
+    swap = (0, 2, 1, 3)
+    for q in range(4):
+        for k in range(4):
+            src = gst.at[P_.zk[k] * 8 + P_.rank(P_.flip(chips[q]))]
+            i = swap[q] * 4 + k
+            go(rcopy(src, rs1.at[i], s1s.at[i], s1r.at[i], P_.dev(sib)))
+
+    def in1(q, k):
+        i = q * 4 + k
+        rcopy(gst.at[0], rs1.at[i], s1s.at[0], s1r.at[i], P_.dev(sib)).wait_recv()
+        s = P_.zk[k] * 8 + P_.rank(chips[q])
+        gst[s] = (gst[s].astype(F32) + rs1[i].astype(F32)).astype(BF)
+
+    def out2(q, k, n, p):
+        i = n * 4 + k
+        go(rcopy(gst.at[P_.zk[k] * 8 + P_.rank(chips[q])], rs2.at[i], s2s.at[i], s2r.at[i], P_.dev(p)))
+
+    def in2(n, k, p):
+        i = n * 4 + k
+        rcopy(gst.at[0], rs2.at[i], s2s.at[0], s2r.at[i], P_.dev(sib)).wait_recv()
+        s = P_.zk[k] * 8 + P_.rank(p)
+        gst[s] = (gst[s].astype(F32) + rs2[i].astype(F32)).astype(BF)
+
+    for k in (3, 2, 1, 0):
+        in1(0, k)
+        out2(0, k, 0, d2)
+        in1(2, k)
+        out2(2, k, 2, d2)
+    for k in (3, 2, 1, 0):
+        in1(1, k)
+        in1(3, k)
+    for k in (3, 2, 1, 0):
+        in2(0, k, d1)
+        out2(1, k, 1, d1)
+    for k in (3, 2, 1, 0):
+        in2(2, k, own)
+        in2(1, k, own)
+        if k:
+            zz = P_.zk[k]
+            go(rcopy(gst.at[zz * 8 + t], rs3.at[k - 1], s3s.at[k - 1], s3r.at[k - 1], P_.dev(own, zz)))
+    acc = gst[b].astype(F32)
+    for k in (1, 2, 3):
+        rcopy(gst.at[0], rs3.at[k - 1], s3s.at[0], s3r.at[k - 1], P_.dev(sib)).wait_recv()
+        acc += rs3[k - 1].astype(F32)
+    gpack[...] = acc
+    for cp in sends:
+        cp.wait_send()
+
+
+def run_back(lengths, tok, gt, s2, nt, n1, qkv, lse, att, gsum, gl, pack_all):
+    sd = jax.ShapeDtypeStruct
+    dma = pltpu.SemaphoreType.DMA
+    return pl.pallas_call(
+        back_kernel,
+        out_shape=(sd((384, 1024), F32), sd((32, PW), F32)),
+        in_specs=[SM] + [VM] * 10 + [ANY],
+        out_specs=(VM, VM),
+        scratch_shapes=[
+            pltpu.VMEM((32, 32, PW), BF), pltpu.VMEM((384, 3072), BF),
+            pltpu.VMEM((384, 1024), F32), pltpu.VMEM((32, 32, PW), BF),
+            pltpu.VMEM((16, 32, PW), BF), pltpu.VMEM((12, 32, PW), BF), pltpu.VMEM((3, 32, PW), BF),
+            dma((16,)), dma((16,)), dma((12,)), dma((12,)), dma((3,)), dma((3,)), dma((1,)),
+        ],
+        compiler_params=pltpu.CompilerParams(
+            collective_id=2, has_side_effects=True, vmem_limit_bytes=60 * MIB
+        ),
+    )(lengths, tok, gt, s2, nt, n1, qkv, lse, att, gsum, gl, pack_all)
+
+
+def fused_device(
+    tokens, cotangent, lengths, expert_ids, slot_ids, w_qkv, w_out, gain_one, w_in, w_down,
+    w_expert_in, w_expert_out, w_mix, gain_two,
+):
+    keep = jnp.arange(384, dtype=jnp.int32) < lengths[0]
+    table = jnp.where(slot_ids >= 0, expert_ids * CAP + slot_ids, -1).astype(BF)
+    gt = jnp.concatenate(
+        [
+            jnp.where(keep[:, None], cotangent, jnp.zeros_like(cotangent)),
+            jnp.pad(table[None, :], ((0, 15), (0, 640))),
+        ],
+        axis=0,
+    )
+    pack = jnp.concatenate(
+        [
+            w_qkv, w_mix, gain_one[:, None], gain_two[:, None],
+            jnp.zeros((32, 124), BF), w_out,
+        ],
+        axis=1,
+    )
+    wia = jnp.concatenate([w_in[None], w_expert_in], axis=0)
+    wia = wia.reshape(3, 32, 4, 8, 128).transpose(3, 0, 1, 2, 4).reshape(8, 3, 32, 512)
+    wdn = jnp.concatenate([w_down[None], w_expert_out], axis=0)
+    qkv, lse, att, s2, nt, n1, wmix, pack_all, wi_all, wd_all, g_all = run_enter(
+        lengths, tokens, pack, wia, wdn, gt
+    )
+    block, gsum, gl, gdo, gx = run_ff(lengths, nt, wmix, s2, g_all, wi_all, wd_all)
+    gtok, gpack = run_back(
+        lengths, tokens, gt, s2, nt, n1, qkv, lse, att, gsum, gl, pack_all
+    )
+    gdo = gdo.reshape(3, 128, 1024)
+    gwi = gx.reshape(8, 3, 32, 4, 128).transpose(1, 2, 3, 0, 4).reshape(3, 32, 4096).astype(F32)
+    return (
+        block, gtok, gpack[:, 0:3072], gpack[:, WO : WO + 1024], gpack[:, EX + 2],
+        gwi[0], gdo[0], gwi[1:], gdo[1:], gpack[:, EX : EX + 2], gpack[:, EX + 3],
+    )
+
+
 def solution(mesh):
     placed = (
         P(("dp", "fsdp"), None),
@@ -275,8 +1060,9 @@
         P(("dp", "fsdp"), None),
         P(("dp", "fsdp")),
     )
+    fused = (mesh.shape["dp"], mesh.shape["fsdp"]) == (8, 4)
     return jax.shard_map(
-        per_device,
+        fused_device if fused else per_device,
         mesh=mesh,
         in_specs=placed,
         out_specs=(

time: 2240 us -> 487 us (0.22)
  waiting for transfers between devices: 1650 us -> 0 us
  Pallas kernels: 0 us -> 458 us
  matrix products: 306 us -> 0 us
  blocking collectives: 123 us -> 0 us
  local copies, waits for them, and re-layouts: 117 us -> 23.6 us
    reduce_scatter x5 -> x0, waiting for transfers between devices: 1030 us -> none  [the longest x1 353 us: per_device(): lax.psum_scatter(grad_expert_out_lead, ('dp', 'fsdp'), scatter_dimension=...]
    pallas_call x0 -> x3, Pallas kernels: none -> 458 us  [the longest x1 194 us: run_ff(): pl.pallas_call(ff_kernel, out_shape=(sd((384, 1024), BF), sd((384, 1024),...]
    all_gather x6 -> x0, waiting for transfers between devices: 312 us -> none  [the longest x1 107 us: per_device(): lax.all_gather(w_expert_out, ('dp', 'fsdp'), axis=1, tiled=True)]
    unnamed x15 -> x0, waiting for transfers between devices: 306 us -> none
    dot_general x134 -> x0, matrix products: 305 us -> none  [the longest x32 40.3 us: head_scores(): jnp.einsum('qd,kd->qk', query_h, key_h, preferred_element_type=jnp.float32)]
    unnamed x2 -> x0, blocking collectives: 82.4 us -> none
    transpose x2 -> x0, local copies, waits for them, and re-layouts: 50.7 us -> none  [the longest x1 49.4 us: per_device(): jnp.einsum('ecd,ecf->def', buffer, grad_expert_up, preferred_element_type...]
    all_gather x1 -> x0, blocking collectives: 40.2 us -> none  [per_device(): lax.all_gather(w_mix, ('dp', 'fsdp'), axis=0, tiled=True)]
  transfers between devices with their start and end apart: 13 -> 0, of which waited for: 10 -> 0; matrix products, arithmetic and copies ran while one was open for 18% -> 0% of each run, Pallas kernels for 0% -> 0%
where the time goes in v1:
time: 487 us; the launch traced here: 485 us
  Pallas kernels  458 us (94%)
  local copies, waits for them, and re-layouts  23.6 us (5%)
    pallas_call x1, Pallas kernels, run_ff(): pl.pallas_call(ff_kernel, out_shape=(sd((384, 1024), BF), sd((384, 1024),...  194 us
    pallas_call x1, Pallas kernels, run_enter(): pl.pallas_call(enter_kernel, out_shape=(sd((384, 3072), BF), sd((384, 128...  163 us
    pallas_call x1, Pallas kernels, run_back(): pl.pallas_call(back_kernel, out_shape=(sd((384, 1024), F32), sd((32, PW),...  101 us

profile of v1, /device:TPU:0, one launch (start us, length us, event | category | flops | bytes accessed | tf_op | source)
XLA Modules:
  0.0 485.3 jit_solution(8718713187418488103)
XLA Ops:
  1.4 0.7 select_convert_fusion
  2.1 0.7 copy.34
  2.8 0.8 copy.33
  3.6 0.8 copy.35
  4.3 1.0 concatenate.17.pack
  5.4 1.0 copy.41
  8.1 0.9 fusion.1.gt
  9.7 162.6 %shard_map.221 = (bf16[384,3072]{1,0:T(8,128)(2,1)}, f32[384,128]{1,0:T(8,128)S(1)}, bf16[384,1024]{1,0:T(8,128)(2,1)S(1)}, f32[384,1024]{1,0:T(8,128)}, bf16[38...) custom-call(s32[1]{0:T(128)} %copy.45.len_ref, ...), custom_call_target="tpu_custom_call" | custom-call | tf_op jit(solution)/shard_map/pallas_call | solution.py:510
  172.3 0.9 copy-done
  173.2 0.9 copy-done.2
  174.1 0.9 copy-done.3
  175.0 0.7 copy-done.4
  176.3 193.7 %shard_map.222 = (bf16[384,1024]{1,0:T(8,128)(2,1)}, f32[384,1024]{1,0:T(8,128)}, f32[384,128]{1,0:T(8,128)}, f32[384,1024]{1,0:T(8,128)}, bf16[8,3,32,512]{3,2,...) custom-call(s32[1]{0:T(128)} %copy.45.len_ref, ...), custom_call_target="tpu_custom_call" | custom-call | tf_op jit(solution)/shard_map/pallas_call | solution.py:818
  370.1 101.5 %shard_map.223 = (f32[384,1024]{1,0:T(8,128)}, f32[32,4224]{1,0:T(8,128)}) custom-call(s32[1]{0:T(128)} %copy.45.len_ref, bf16[384,1024]{1,0:T(8,128)(2,1)} %tok.3, bf16[400,1024]{1,0:T(8,128)(2,1)} %fusion.1.gt, f32[384,1024]{1,0:T(8,128)} %get-tuple-element.31.s2, bf16[384,1024]{1,0:T(8,128)(2,1)} %copy-done, bf16[384,1024]{1,0:T(8,128)(2,1)} %copy-done.3, ...), custom_call_target="tpu_custom_call" | custom-call | tf_op jit(solution)/shard_map/pallas_call | solution.py:991
  471.5 1.5 slice_reduce_fusion
  473.0 0.7 slice.44
  474.4 1.6 slice.36
  476.0 1.8 slice.35
  477.7 0.8 slice.39
  478.6 1.0 slice.42
  480.9 1.2 slice.41
  482.4 0.9 squeeze.15
  483.3 0.9 copy.46
  484.1 1.1 copy.47
  (40 shorter events, 5.2 us)
Async XLA Ops:
  0.6 5.8 %copy-start.12 = (bf16[2,32,4096]{2,1,0:T(8,128)(2,1)S(1)}, bf16[2,32,4096]{2,1,0:T(8,128)(2,1)}, u32[]{:S(2)}) copy-start(bf16[2,32,4096]{2,1,0:T(8,128)(2,1)} %param.24) | copy-start | bytes 1572868
  6.8 1.1 copy-start.8
  8.0 1.1 copy-start.11
  8.0 1.2 copy-start.13
  8.1 1.6 copy-start.1
  172.3 0.9 copy-start
  173.2 0.9 copy-start.2
  174.1 0.9 copy-start.3
  175.0 0.7 copy-start.4
  175.7 0.7 copy-start.5
  370.0 107.7 %copy-start.7 = (f32[384,1024]{1,0:T(8,128)S(1)}, f32[384,1024]{1,0:T(8,128)}, u32[]{:S(2)}) copy-start(f32[384,1024]{1,0:T(8,128)} %get-tuple-element.46) | copy-start | bytes 4718596
  477.7 1.9 copy-start.10
  480.9 2.4 copy-start.9
  482.4 1.8 copy-start.6

commit v2 on v1

--- a/solution.py
+++ b/solution.py
@@ -339,6 +339,125 @@
     return dot_nt(pick, extra)[0:1]
 
 
+class ZSum:
+    def __init__(self, P_, src, land, via, send, recv):
+        self.P, self.src, self.land, self.via = P_, src, land, via
+        self.send, self.recv = send, recv
+        self.mid = (P_.z == 1) | (P_.z == 2)
+
+    def copy(self, n, w, j):
+        P_ = self.P
+        to = P_.dev(P_.own, P_.zk[1 if j == 4 else j])
+        block = self.src[w].at[n, P_.zk[3 if j == 4 else j]]
+        dst = self.via[w].at[n] if j == 4 else self.land[w].at[n, j - 1]
+        i = w * 4 + j - 1
+        return rcopy(block, dst, self.send.at[n, i], self.recv.at[n, i], to)
+
+    def ship(self, n):
+        @pl.when(self.mid)
+        def _():
+            for j in (3, 1):
+                for w in range(2):
+                    self.copy(n, w, j).start()
+
+        @pl.when(jnp.logical_not(self.mid))
+        def _():
+            for j in (4, 2, 1):
+                for w in range(2):
+                    self.copy(n, w, j).start()
+
+    def transit(self, n):
+        @pl.when(self.mid)
+        def _():
+            k2 = self.P.zk[2]
+            for w in range(2):
+                self.copy(n, w, 4).wait_recv()
+                self.src[w][n, k2] = self.src[w][n, k2] + self.via[w][n]
+                self.copy(n, w, 2).start()
+
+    def arrived(self, n):
+        for w in range(2):
+            self.copy(n, w, 1).wait_recv()
+            self.copy(n, w, 2).wait_recv()
+
+        @pl.when(self.mid)
+        def _():
+            for w in range(2):
+                self.copy(n, w, 3).wait_recv()
+
+    def sent(self, n):
+        for w in range(2):
+            self.copy(n, w, 1).wait_send()
+            self.copy(n, w, 2).wait_send()
+
+        @pl.when(self.mid)
+        def _():
+            for w in range(2):
+                self.copy(n, w, 3).wait_send()
+
+        @pl.when(jnp.logical_not(self.mid))
+        def _():
+            for w in range(2):
+                self.copy(n, w, 4).wait_send()
+
+
+class ZGather:
+    def __init__(self, P_, mine, full, send, recv):
+        self.P, self.mine, self.full, self.send, self.recv = P_, mine, full, send, recv
+        self.mid = (P_.z == 1) | (P_.z == 2)
+
+    def copy(self, n, w, j):
+        P_ = self.P
+        zs = P_.zk[2] if j == 4 else P_.z
+        block = self.full[w](n, zs) if j == 4 else self.mine[w](n)
+        to = P_.dev(P_.own, P_.zk[1 if j == 4 else j])
+        return rcopy(
+            block, self.full[w](n, zs), self.send.at[n, w * 4 + j - 1], self.recv.at[n, w * 4 + zs], to
+        )
+
+    def landed(self, n, w, j):
+        P_ = self.P
+        zs = P_.zk[j]
+        rcopy(
+            self.mine[w](n), self.full[w](n, zs), self.send.at[n, 0], self.recv.at[n, w * 4 + zs],
+            P_.dev(P_.sib),
+        ).wait_recv()
+
+    def ship(self, n):
+        for w in range(2):
+            self.copy(n, w, 2).start()
+
+        @pl.when(self.mid)
+        def _():
+            for w in range(2):
+                self.copy(n, w, 3).start()
+
+        for w in range(2):
+            self.copy(n, w, 1).start()
+
+    def relay(self, n):
+        for w in range(2):
+            self.landed(n, w, 2)
+
+        @pl.when(self.mid)
+        def _():
+            for w in range(2):
+                self.copy(n, w, 4).start()
+
+    def finish(self, n):
+        for w in range(2):
+            self.landed(n, w, 1)
+            self.landed(n, w, 3)
+            self.copy(n, w, 1).wait_send()
+            self.copy(n, w, 2).wait_send()
+
+        @pl.when(self.mid)
+        def _():
+            for w in range(2):
+                self.copy(n, w, 3).wait_send()
+                self.copy(n, w, 4).wait_send()
+
+
 PW = 4224
 EX = 3072
 WO = 3200
@@ -347,7 +466,7 @@
 def enter_kernel(
     len_ref, tok, pack, wia, wdn, gt,
     qkv, lse, att, s2, nt, n1, wmix, pack_all, wi_all, wd_all, g_all,
-    pack_v, ps, pr, asend, arecv, fsend, fri, frd, gs, gr, lsem,
+    pack_v, ps, pr, asend, arecv, fsend, frecv, gs, gr, lsem,
 ):
     P_ = Place()
     z, t, b = P_.z, P_.t, P_.b
@@ -360,6 +479,10 @@
         cp.start()
         sends.append(cp)
 
+    experts = ZGather(
+        P_, (lambda n: wi_all.at[1 + n, z], lambda n: wd_all.at[1 + n, z]),
+        (lambda n, zs: wi_all.at[1 + n, zs], lambda n, zs: wd_all.at[1 + n, zs]), fsend, frecv,
+    )
     lc = pltpu.make_async_copy(pack, pack_v.at[b], lsem.at[0])
     lc.start()
     for k in range(1, 4):
@@ -400,12 +523,8 @@
                 rcopy(
                     wia.at[0], wi_all.at[:, z, rq], asend.at[0], arecv.at[rr], P_.dev(sib)
                 ).wait_recv()
-            for kd in range(3):
-                for j in range(1, 4):
-                    zz = P_.dev(own, P_.zk[j])
-                    i = kd * 6 + (j - 1) * 2
-                    go(rcopy(wi_all.at[kd, z], wi_all.at[kd, z], fsend.at[i], fri.at[kd, z], zz))
-                    go(rcopy(wdn.at[kd], wd_all.at[kd, z], fsend.at[i + 1], frd.at[kd, z], zz))
+            for e in range(2):
+                experts.ship(e)
         if 1 <= k <= 4:
             s = slot(k - 1, d1)
             landed(s)
@@ -479,6 +598,7 @@
     lax.fori_loop(0, 8, pair_step, 0)
     r = g_landed(d2)
     g_fwd(r, 5, sib)
+    experts.relay(0)
     for j in range(2):
         w = pack_v[:, :, WO + j * 512 : WO + (j + 1) * 512].reshape(1024, 512)
         s2[:, j * 512 : (j + 1) * 512] = stream[:, j * 512 : (j + 1) * 512] + dot_nn(att[...], w)
@@ -488,11 +608,9 @@
     g_fwd(r, 6, sib)
     for p in (own, d1, d2, dd):
         g_landed(P_.flip(p))
-    for kd in range(3):
-        for j in range(1, 4):
-            zz = P_.zk[j]
-            rcopy(wi_all.at[kd, zz], wi_all.at[kd, zz], fsend.at[0], fri.at[kd, zz], P_.dev(sib)).wait_recv()
-            rcopy(wdn.at[kd], wd_all.at[kd, zz], fsend.at[0], frd.at[kd, zz], P_.dev(sib)).wait_recv()
+    experts.relay(1)
+    for e in range(2):
+        experts.finish(e)
     lg.wait()
     keep_all.wait()
     for cp in sends:
@@ -521,8 +639,7 @@
             pltpu.VMEM((32, 32, PW), BF),
             pltpu.SemaphoreType.DMA((31,)), pltpu.SemaphoreType.DMA((32,)),
             pltpu.SemaphoreType.DMA((7,)), pltpu.SemaphoreType.DMA((8,)),
-            pltpu.SemaphoreType.DMA((18,)), pltpu.SemaphoreType.DMA((3, 4)),
-            pltpu.SemaphoreType.DMA((3, 4)),
+            pltpu.SemaphoreType.DMA((2, 8)), pltpu.SemaphoreType.DMA((2, 8)),
             pltpu.SemaphoreType.DMA((7,)), pltpu.SemaphoreType.DMA((8,)),
             pltpu.SemaphoreType.DMA((4,)),
         ],
@@ -547,9 +664,9 @@
 
 def ff_kernel(
     len_ref, nt_own, wmix, s2, g_all, wi_all, wd_all,
-    block, gsum, gl_out, gdo, gx, r1, r2, rin, rdn,
-    nt_all, gbuf, br, gn, xb, yb, logit, wi, wd, ai, ad, gin, gdn, tmp, gc, gcr, dots, tabs,
-    ts, tr, gsem, wsem, fs_, fri, frd, s1s, s1r, s2s, s2r, cs, cr, xsd, xrv, lsem,
+    block, gsum, gl_out, gde, xe, dgi, dgd, r1, r2, rin, rdn, dwi, dwd,
+    nt_all, gbuf, br, gn, xb, yb, wi, wd, ai, ad, gin, gdn, tri, trd, tmp, gc, gcr, dots,
+    ts, tr, gsem, wsem, zas, zar, zss, zsr, s1s, s1r, s2s, s2r, cs, cr, lsem, tsem,
 ):
     P_ = Place()
     z, t = P_.z, P_.t
@@ -562,28 +679,38 @@
         cp.start()
         sends.append(cp)
 
-    ln = pltpu.make_async_copy(nt_own, nt_all.at[t], lsem.at[1])
+    ln = pltpu.make_async_copy(nt_own, nt_all.at[t], lsem.at[0])
     ln.start()
     for i, p in enumerate((d1, d2, sib)):
         go(rcopy(nt_own, nt_all.at[t], ts.at[i], tr.at[t], P_.dev(p)))
-    def w_load(kd):
-        return (
-            pltpu.make_async_copy(wi_all.at[kd], wi.at[kd % 2], wsem.at[kd, 0]),
-            pltpu.make_async_copy(wd_all.at[kd], wd.at[kd % 2], wsem.at[kd, 1]),
-        )
-
-    for kd in range(2):
-        for cp in w_load(kd):
-            cp.start()
-
-    g_tab = pltpu.make_async_copy(g_all.at[:, 384:400], tabs, lsem.at[2])
-    g_tab.start()
+    dense = ZGather(
+        P_, (lambda n: wi_all.at[0, z], lambda n: wd_all.at[0, z]),
+        (lambda n, zs: dwi.at[zs], lambda n, zs: dwd.at[zs]), zas, zar,
+    )
+    dense.ship(0)
+    l0 = pltpu.make_async_copy(wi_all.at[0, z], dwi.at[z], lsem.at[1])
+    l1 = pltpu.make_async_copy(wd_all.at[0, z], dwd.at[z], lsem.at[2])
+    l0.start()
+    l1.start()
     s2_in = pltpu.make_async_copy(s2, gsum, lsem.at[3])
     s2_in.start()
 
-    def w_landed(kd):
-        for cp in w_load(kd):
-            cp.wait()
+    def w_load(e):
+        return (
+            pltpu.make_async_copy(wi_all.at[1 + e], wi.at[e], wsem.at[e, 0]),
+            pltpu.make_async_copy(wd_all.at[1 + e], wd.at[e], wsem.at[e, 1]),
+        )
+
+    def dense_load():
+        return (
+            pltpu.make_async_copy(dwi, wi.at[0], wsem.at[0, 0]),
+            pltpu.make_async_copy(dwd, wd.at[0], wsem.at[0, 1]),
+        )
+
+    for e in range(2):
+        for cp in w_load(e):
+            cp.start()
+    zsum = ZSum(P_, (gin, gdn), (rin, rdn), (tri, trd), zss, zsr)
 
     order = (own, sib, d1, P_.flip(d2), d2, P_.flip(d1), dd, P_.flip(dd))
     ranks = [P_.rank(p) for p in order]
@@ -597,30 +724,17 @@
     def g_copy(i):
         return pltpu.make_async_copy(g_all.at[seq_at(i)], gbuf.at[i % 2], gsem.at[i % 2])
 
-    def ff(xv, gv, kd):
-        wiv = wi[kd % 2].reshape(1024, 512)
-        wdv = wd[kd % 2].reshape(512, 1024)
+    def ff(xv, gv, k):
+        wiv = wi[k].reshape(1024, 512)
+        wdv = wd[k].reshape(512, 1024)
         act, dact = gelu_both(dot_nn(xv, wiv))
         act = act.astype(BF)
         gup = (dact * dot_nt(gv, wdv)).astype(BF)
-        ad[...] += dot_tn(act, gv)
-        ai[...] += dot_tn(xv, gup)
+        ad[k] += dot_tn(act, gv)
+        ai[k] += dot_tn(xv, gup)
         return dot_nn(act, wdv), dot_nt(gup, wiv)
 
     lane = lax.broadcasted_iota(jnp.int32, (448, 128), 1)
-
-    def clear():
-        ad[...] = jnp.zeros_like(ad)
-        ai[...] = jnp.zeros_like(ai)
-
-    def ship(kd):
-        gin[kd] = ai[...].astype(BF).reshape(4, 256, 512)
-        gdn[kd] = ad[...].astype(BF).reshape(4, 128, 1024)
-        for j in range(1, 4):
-            zz = P_.zk[j]
-            i = kd * 6 + (j - 1) * 2
-            go(rcopy(gin.at[kd, zz], rin.at[kd, j - 1], fs_.at[i], fri.at[kd, j - 1], P_.dev(own, zz)))
-            go(rcopy(gdn.at[kd, zz], rdn.at[kd, j - 1], fs_.at[i + 1], frd.at[kd, j - 1], P_.dev(own, zz)))
 
     def shares(tab, e):
         slot = lax.broadcasted_iota(jnp.int32, (112, 384), 0) + e * 112
@@ -633,11 +747,14 @@
         return rcopy(nt_all.at[r], nt_all.at[r], ts.at[i], tr.at[r], P_.dev(q))
 
     g_copy(0).start()
-    clear()
-    w_landed(0)
+    ai[...] = jnp.zeros_like(ai)
+    ad[...] = jnp.zeros_like(ad)
     ln.wait()
-
-    def seq_step(i, carry):
+    for e in range(2):
+        for cp in w_load(e):
+            cp.wait()
+
+    def arrive(i, carry):
         s = seq_at(i)
 
         @pl.when(i + 1 < 8)
@@ -659,38 +776,25 @@
         xv = nt_all[s]
         gv = gbuf[i % 2, :384]
         tab = gbuf[i % 2, 384:400][0:1, :384].astype(F32)
-        lg = dot_nn(xv, wmix[...])
-        logit[s] = lg
-        m0, m1 = mix_of(lg)
-        gf = gv.astype(F32)
-        out, gxv = ff(xv, (m0 * gf).astype(BF), 0)
-        br[s] = (m0 * out).astype(BF)
-        gn[s] = gxv.astype(BF)
-        col = jnp.broadcast_to(jnp.sum(gf * out, axis=-1, keepdims=True), (384, 128))
-        gc[s, 0:8] = jnp.transpose(col)[0:8]
-        ge = (m1 * gf).astype(BF)
+        _, m1 = mix_of(dot_nn(xv, wmix[...]))
+        ge = (m1 * gv.astype(F32)).astype(BF)
         for e in range(2):
             sh = shares(tab, e)
-            xb[e, s] = dot_nn(sh, xv).astype(BF)
-            yb[e, s] = dot_nn(sh, ge).astype(BF)
+            xb[e, i] = dot_nn(sh, xv).astype(BF)
+            yb[e, i] = dot_nn(sh, ge).astype(BF)
         return carry
 
-    lax.fori_loop(0, 8, seq_step, 0)
-    for k, (p, dests) in fwds.items():
-        for n, q in dests:
-            fwd_copy(p, n, q).wait_send()
-    for cp in w_load(2):
-        cp.start()
-    ship(0)
-
-    for e in range(2):
-        clear()
-        w_landed(1 + e)
-
-        def ex_step(q, carry):
-            four = pl.ds(q * 4, 4)
+    def half(b, carry):
+        lax.fori_loop(b * 4, b * 4 + 4, arrive, 0)
+
+        @pl.when(b == 1)
+        def _():
+            dense.relay(0)
+
+        def expert(e, carry):
+            four = pl.ds(b * 4, 4)
             gq = yb[e, four].reshape(448, 1024)
-            yv, gb = ff(xb[e, four].reshape(448, 1024), gq, 1 + e)
+            yv, gb = ff(xb[e, four].reshape(448, 1024), gq, e)
             rs = jnp.sum(gq.astype(F32) * yv, axis=-1, keepdims=True)
             high = rs.astype(BF).astype(F32)
             dots[e, four] = (
@@ -700,68 +804,148 @@
             )
             xb[e, four] = yv.astype(BF).reshape(4, 112, 1024)
             yb[e, four] = gb.astype(BF).reshape(4, 112, 1024)
+
+            @pl.when(b == 1)
+            def _():
+                gin[e] = ai[e].astype(BF).reshape(4, 256, 512)
+                gdn[e] = ad[e].astype(BF).reshape(4, 128, 1024)
+                zsum.ship(e)
+
             return carry
 
-        lax.fori_loop(0, 2, ex_step, 0)
-        ship(1 + e)
-
-    g_tab.wait()
-
-    def mix_step(s, carry):
-        tab = tabs[s][0:1, :384].astype(F32)
-        _, m1 = mix_of(logit[s])
+        lax.fori_loop(0, 2, expert, 0)
+        return carry
+
+    lax.fori_loop(0, 2, half, 0)
+    g_copy(7).start()
+    l0.wait()
+    l1.wait()
+    dense.finish(0)
+    for cp in dense_load():
+        cp.start()
+    ai[0] = jnp.zeros_like(ai[0])
+    ad[0] = jnp.zeros_like(ad[0])
+    for cp in dense_load():
+        cp.wait()
+
+    chips = (dd, d1, d2, own)
+    both = (gn, br)
+
+    def give1(q, w):
+        r = P_.rank(P_.flip(chips[q]))
+        k = (0, 2, 1, 3)[q]
+        return rcopy(both[w].at[r], r1.at[w, k], s1s.at[w, k], s1r.at[w, k], P_.dev(sib))
+
+    def load1(q, w, start):
+        cp = pltpu.make_async_copy(r1.at[w, q], tmp.at[w], tsem.at[w])
+        if start:
+            rcopy(nt_own, r1.at[w, q], s1s.at[0, 0], s1r.at[w, q], P_.dev(sib)).wait_recv()
+            cp.start()
+        else:
+            cp.wait()
+            add_tmp(w, P_.rank(chips[q]))
+
+    def load2(k, p, w, start):
+        cp = pltpu.make_async_copy(r2.at[w, k], tmp.at[w], tsem.at[w])
+        if start:
+            rcopy(nt_own, r2.at[w, k], s2s.at[0, 0], s2r.at[w, k], P_.dev(sib)).wait_recv()
+            cp.start()
+        else:
+            cp.wait()
+            add_tmp(w, P_.rank(p))
+
+    def add_tmp(w, r):
+        both[w][r] = both[w][r] + tmp[w]
+
+    def give2(q, k, p, w):
+        src = both[w].at[P_.rank(chips[q])]
+        return rcopy(src, r2.at[w, k], s2s.at[w, k], s2r.at[w, k], P_.dev(p))
+
+    def dense_step(k, carry):
+        i = 7 - k
+        s = seq_at(i)
+
+        @pl.when(i > 0)
+        def _():
+            g_copy(i - 1).start()
+
+        g_copy(i).wait()
+        xv = nt_all[s]
+        gf = gbuf[i % 2, :384].astype(F32)
+        tab = gbuf[i % 2, 384:400][0:1, :384].astype(F32)
+        m0, m1 = mix_of(dot_nn(xv, wmix[...]))
+        out, gxv = ff(xv, (m0 * gf).astype(BF), 0)
+        col = jnp.broadcast_to(jnp.sum(gf * out, axis=-1, keepdims=True), (384, 128))
+        gc[s, 0:8] = jnp.transpose(col)[0:8]
         s0, s1 = shares(tab, 0), shares(tab, 1)
-        em = dot_tn(s0, xb[0, s]) + dot_tn(s1, xb[1, s])
-        gb = dot_tn(s0, yb[0, s]) + dot_tn(s1, yb[1, s])
-        q1 = dot_tn(s0, dots[0, s]) + dot_tn(s1, dots[1, s])
+        q1 = dot_tn(s0, dots[0, i]) + dot_tn(s1, dots[1, i])
         gc[s, 8:16] = jnp.transpose(jnp.broadcast_to(q1[:, 0:1] + q1[:, 1:2], (384, 128)))[0:8]
-        br[s] = (br[s].astype(F32) + m1 * em).astype(BF)
-        gn[s] = (gn[s].astype(F32) + gb).astype(BF)
+        br[s] = (m0 * out + m1 * (dot_tn(s0, xb[0, i]) + dot_tn(s1, xb[1, i]))).astype(BF)
+        gn[s] = (gxv + dot_tn(s0, yb[0, i]) + dot_tn(s1, yb[1, i])).astype(BF)
+
+        for step, q in ((0, 0), (2, 1), (4, 2), (6, 3)):
+
+            @pl.when(k == step)
+            def _():
+                for w in range(2):
+                    give1(q, w).start()
+
+        @pl.when(k == 1)
+        def _():
+            for w in range(2):
+                load1(0, w, True)
+
+        @pl.when(k == 2)
+        def _():
+            for w in range(2):
+                load1(0, w, False)
+                give2(0, 0, d2, w).start()
+            zsum.transit(0)
+
+        @pl.when(k == 3)
+        def _():
+            for w in range(2):
+                load1(2, w, True)
+
+        @pl.when(k == 4)
+        def _():
+            for w in range(2):
+                load1(2, w, False)
+                give2(2, 2, d2, w).start()
+
+        @pl.when(k == 5)
+        def _():
+            for w in range(2):
+                load1(1, w, True)
+            zsum.transit(1)
+
+        @pl.when(k == 6)
+        def _():
+            for w in range(2):
+                load1(1, w, False)
+                load2(0, d1, w, True)
+
         return carry
 
-    lax.fori_loop(0, 8, mix_step, 0)
+    lax.fori_loop(0, 8, dense_step, 0)
+    for w in range(2):
+        load2(0, d1, w, False)
+        give2(1, 1, d1, w).start()
+        load1(3, w, True)
     for i, p in enumerate(others):
         go(rcopy(gc.at[P_.rank(p)], gcr.at[t], cs.at[i], cr.at[t], P_.dev(p)))
-
-    chips = (dd, d1, d2, own)
-    both = (gn, br)
-    for q in range(4):
-        r = P_.rank(P_.flip(chips[q]))
-        for w in range(2):
-            i = w * 4 + q
-            go(rcopy(both[w].at[r], r1.at[w, (0, 2, 1, 3)[q]], s1s.at[i], s1r.at[w, (0, 2, 1, 3)[q]], P_.dev(sib)))
-
-    def add_in(w, r, src):
-        cp = pltpu.make_async_copy(src, tmp, lsem.at[0])
-        cp.start()
-        cp.wait()
-        both[w][r] = (both[w][r].astype(F32) + tmp[...].astype(F32)).astype(BF)
-
-    def in1(w, q):
-        rcopy(nt_own, r1.at[w, q], s1s.at[0], s1r.at[w, q], P_.dev(sib)).wait_recv()
-        add_in(w, P_.rank(chips[q]), r1.at[w, q])
-
-    def out2(w, q, k, p):
-        src = both[w].at[P_.rank(chips[q])]
-        go(rcopy(src, r2.at[w, k], s2s.at[w * 3 + k], s2r.at[w, k], P_.dev(p)))
-
-    def in2(w, k, p):
-        rcopy(nt_own, r2.at[w, k], s2s.at[0], s2r.at[w, k], P_.dev(sib)).wait_recv()
-        add_in(w, P_.rank(p), r2.at[w, k])
-
+    o0 = pltpu.make_async_copy(ai.at[0], dgi, lsem.at[0])
+    o1 = pltpu.make_async_copy(ad.at[0], dgd, lsem.at[1])
+    o0.start()
+    o1.start()
     for w in range(2):
-        in1(w, 0)
-        out2(w, 0, 0, d2)
-        in1(w, 2)
-        out2(w, 2, 2, d2)
-        in1(w, 1)
-        in1(w, 3)
+        load1(3, w, False)
+        load2(2, own, w, True)
     for w in range(2):
-        in2(w, 0, d1)
-        out2(w, 1, 1, d1)
+        load2(2, own, w, False)
     for w in range(2):
-        in2(w, 2, own)
-        in2(w, 1, own)
+        load2(1, own, w, True)
+        load2(1, own, w, False)
     s2_in.wait()
     branch = br[t].astype(F32)
     keep = (lax.broadcasted_iota(jnp.int32, (384, 1), 0) < len_ref[0]).astype(F32)
@@ -774,40 +958,64 @@
     tot = jnp.sum(gcr[...], axis=0)
     gc0 = jnp.transpose(jnp.broadcast_to(tot[0:1], (128, 384)))
     q1 = jnp.transpose(jnp.broadcast_to(tot[8:9], (128, 384)))
-    m0, m1 = mix_of(logit[t])
+    m0, m1 = mix_of(dot_nn(nt_all[t], wmix[...]))
     gl_out[...] = m0 * (m1 * gc0 - q1)
 
-    for kd in range(3):
-        acc_i = gin[kd, z].astype(F32)
-        acc_d = gdn[kd, z].astype(F32)
-        for j in range(3):
-            rcopy(gin.at[kd, 0], rin.at[kd, j], fs_.at[0], fri.at[kd, j], P_.dev(sib)).wait_recv()
-            rcopy(gdn.at[kd, 0], rdn.at[kd, j], fs_.at[0], frd.at[kd, j], P_.dev(sib)).wait_recv()
-            li = pltpu.make_async_copy(rin.at[kd, j], nt_all.at[j, 0:256, 0:512], lsem.at[0])
-            lj = pltpu.make_async_copy(rdn.at[kd, j], nt_all.at[3, 0:128], lsem.at[1])
-            li.start()
-            lj.start()
-            li.wait()
-            lj.wait()
-            acc_i += nt_all[j, 0:256, 0:512].astype(F32)
-            acc_d += nt_all[3, 0:128].astype(F32)
-        gin[kd, z] = acc_i.astype(BF)
-        ad[kd * 128 : (kd + 1) * 128] = acc_d
-    lgd = pltpu.make_async_copy(ad.at[0:384], gdo, lsem.at[0])
-    lgd.start()
-
-    def rows(p):
-        return pl.ds(pl.multiple_of(P_.rank(p) * 32, 32), 32)
-
-    lx = pltpu.make_async_copy(gin.at[:, z, rows(own)], gx.at[t], lsem.at[1])
-    lx.start()
-    for i, p in enumerate(others):
-        go(rcopy(gin.at[:, z, rows(p)], gx.at[t], xsd.at[i], xrv.at[t], P_.dev(p)))
-    for p in others:
-        r = P_.rank(p)
-        rcopy(gin.at[:, z, rows(own)], gx.at[r], xsd.at[0], xrv.at[r], P_.dev(sib)).wait_recv()
-    lx.wait()
-    lgd.wait()
+    for k, (p, dests) in fwds.items():
+        for n, q in dests:
+            fwd_copy(p, n, q).wait_send()
+    mids = zsum.mid
+
+    def third(e):
+        return (
+            pltpu.make_async_copy(rin.at[e, 2], nt_all.at[2, 0:256, 0:512], lsem.at[4]),
+            pltpu.make_async_copy(rdn.at[e, 2], nt_all.at[3, 0:128], lsem.at[5]),
+        )
+
+    for e in range(2):
+        zsum.arrived(e)
+        loads = (
+            (rin.at[e, 0], nt_all.at[0, 0:256, 0:512]), (rin.at[e, 1], nt_all.at[0, 0:256, 512:1024]),
+            (rdn.at[e, 0], nt_all.at[1, 0:128]), (rdn.at[e, 1], nt_all.at[1, 128:256]),
+        )
+        loads = [pltpu.make_async_copy(u, v, lsem.at[6 + n]) for n, (u, v) in enumerate(loads)]
+
+        @pl.when(mids)
+        def _():
+            for cp in third(e):
+                cp.start()
+
+        for cp in loads:
+            cp.start()
+        for cp in loads:
+            cp.wait()
+        two = nt_all[0, 0:256]
+        ai[1, 0:256] = gin[e, z].astype(F32) + two[:, 0:512].astype(F32) + two[:, 512:1024].astype(F32)
+        at = slice(e * 128, (e + 1) * 128)
+        ad[1, at] = gdn[e, z].astype(F32) + nt_all[1, 0:128].astype(F32) + nt_all[1, 128:256].astype(F32)
+
+        @pl.when(mids)
+        def _():
+            for cp in third(e):
+                cp.wait()
+            ai[1, 0:256] += nt_all[2, 0:256, 0:512].astype(F32)
+            ad[1, at] += nt_all[3, 0:128].astype(F32)
+
+        gin[e, z] = ai[1, 0:256].astype(BF)
+    o2 = pltpu.make_async_copy(gin.at[:, z], xe, lsem.at[2])
+    o3 = pltpu.make_async_copy(ad.at[1, 0:256], gde, lsem.at[3])
+    o2.start()
+    o3.start()
+    for w in range(2):
+        for q in range(4):
+            give1(q, w).wait_send()
+        give2(0, 0, d2, w).wait_send()
+        give2(1, 1, d1, w).wait_send()
+        give2(2, 2, d2, w).wait_send()
+    for e in range(2):
+        zsum.sent(e)
+    for cp in (o0, o1, o2, o3):
+        cp.wait()
     for cp in sends:
         cp.wait_send()
 
@@ -818,51 +1026,162 @@
     out = pl.pallas_call(
         ff_kernel,
         out_shape=(
-            sd((384, 1024), BF), sd((384, 1024), F32), sd((384, 128), F32), sd((384, 1024), F32),
-            sd((8, 3, 32, 512), BF), sd((2, 4, 384, 1024), BF), sd((2, 3, 384, 1024), BF),
-            sd((3, 3, 256, 512), BF), sd((3, 3, 128, 1024), BF),
+            sd((384, 1024), BF), sd((384, 1024), F32), sd((384, 128), F32),
+            sd((256, 1024), F32), sd((2, 256, 512), BF), sd((1024, 512), F32), sd((512, 1024), F32),
+            sd((2, 4, 384, 1024), BF), sd((2, 3, 384, 1024), BF),
+            sd((2, 3, 256, 512), BF), sd((2, 3, 128, 1024), BF),
+            sd((4, 256, 512), BF), sd((4, 128, 1024), BF),
         ),
         in_specs=[SM, ANY, VM, ANY, ANY, ANY, ANY],
-        out_specs=(VM,) * 3 + (ANY,) * 6,
+        out_specs=(VM,) * 3 + (ANY,) * 10,
         scratch_shapes=[
             pltpu.VMEM((8, 384, 1024), BF), pltpu.VMEM((2, 400, 1024), BF),
             pltpu.VMEM((8, 384, 1024), BF), pltpu.VMEM((8, 384, 1024), BF),
             pltpu.VMEM((2, 8, 112, 1024), BF), pltpu.VMEM((2, 8, 112, 1024), BF),
-            pltpu.VMEM((8, 384, 128), F32),
             pltpu.VMEM((2, 4, 256, 512), BF), pltpu.VMEM((2, 4, 128, 1024), BF),
-            pltpu.VMEM((1024, 512), F32), pltpu.VMEM((512, 1024), F32),
-            pltpu.VMEM((3, 4, 256, 512), BF), pltpu.VMEM((3, 4, 128, 1024), BF),
-            pltpu.VMEM((384, 1024), BF),
+            pltpu.VMEM((2, 1024, 512), F32), pltpu.VMEM((2, 512, 1024), F32),
+            pltpu.VMEM((2, 4, 256, 512), BF), pltpu.VMEM((2, 4, 128, 1024), BF),
+            pltpu.VMEM((2, 256, 512), BF), pltpu.VMEM((2, 128, 1024), BF),
+            pltpu.VMEM((2, 384, 1024), BF),
             pltpu.VMEM((8, 16, 384), F32), pltpu.VMEM((8, 16, 384), F32), pltpu.VMEM((2, 8, 112, 128), BF),
-            pltpu.VMEM((8, 16, 1024), BF),
-            dma((7,)), dma((8,)), dma((2,)), dma((3, 2)), dma((18,)), dma((3, 3)), dma((3, 3)),
-            dma((8,)), dma((2, 4)), dma((6,)), dma((2, 3)), dma((7,)), dma((8,)),
-            dma((7,)), dma((8,)), dma((4,)),
+            dma((7,)), dma((8,)), dma((2,)), dma((2, 2)), dma((1, 8)), dma((1, 8)), dma((2, 8)), dma((2, 8)),
+            dma((2, 4)), dma((2, 4)), dma((2, 3)), dma((2, 3)), dma((7,)), dma((8,)), dma((10,)), dma((2,)),
         ],
         compiler_params=pltpu.CompilerParams(
             collective_id=1, has_side_effects=True, vmem_limit_bytes=63 * MIB
         ),
     )(lengths, nt, wmix, s2, g_all, wi_all, wd_all)
-    return out[:5]
+    return out[:7]
+
+
+class RowSum:
+    swap = (0, 2, 1, 3)
+
+    def __init__(self, P_, g, r1, r2, r3, sems):
+        self.P, self.g, self.r1, self.r2, self.r3 = P_, g, r1, r2, r3
+        self.s1s, self.s1r, self.s2s, self.s2r, self.s3s, self.s3r = sems
+        self.chips = (P_.dd, P_.d1, P_.d2, P_.own)
+
+    def rank(self, q):
+        return self.P.rank(self.chips[q])
+
+    def copy1(self, n, q):
+        k = self.swap[q]
+        src = self.g.at[n, self.P.rank(self.P.flip(self.chips[q]))]
+        return rcopy(src, self.r1.at[n, k], self.s1s.at[n, k], self.s1r.at[n, k], self.P.dev(self.P.sib))
+
+    def copy2(self, n, q, k, p):
+        src = self.g.at[n, self.rank(q)]
+        return rcopy(src, self.r2.at[n, k], self.s2s.at[n, k], self.s2r.at[n, k], self.P.dev(p))
+
+    def copy3(self, n, k):
+        P_ = self.P
+        return rcopy(
+            self.g.at[n, P_.t, P_.zk[k]], self.r3.at[n, k - 1], self.s3s.at[n, k - 1],
+            self.s3r.at[n, k - 1], P_.dev(P_.own, P_.zk[k]),
+        )
+
+    def in1(self, n, q):
+        rcopy(
+            self.g.at[n, 0], self.r1.at[n, q], self.s1s.at[n, 0], self.s1r.at[n, q], self.P.dev(self.P.sib)
+        ).wait_recv()
+        r = self.rank(q)
+        self.g[n, r] = self.g[n, r] + self.r1[n, q]
+
+    def in2(self, n, k, q):
+        rcopy(
+            self.g.at[n, 0], self.r2.at[n, k], self.s2s.at[n, 0], self.s2r.at[n, k], self.P.dev(self.P.sib)
+        ).wait_recv()
+        r = self.rank(q)
+        self.g[n, r] = self.g[n, r] + self.r2[n, k]
+
+    def step1(self, n):
+        for q in (0, 1, 2, 3):
+            self.copy1(n, q).start()
+
+    def step2(self, n):
+        P_ = self.P
+        self.in1(n, 0)
+        self.copy2(n, 0, 0, P_.d2).start()
+        self.in1(n, 2)
+        self.copy2(n, 2, 2, P_.d2).start()
+        self.in1(n, 1)
+
+    def step3(self, n):
+        self.in2(n, 0, 1)
+        self.copy2(n, 1, 1, self.P.d1).start()
+        self.in1(n, 3)
+
+    def step4(self, n):
+        self.in2(n, 2, 3)
+        self.in2(n, 1, 3)
+        for k in (3, 2, 1):
+            self.copy3(n, k).start()
+
+    def step5(self, n):
+        P_ = self.P
+        for k in (1, 2, 3):
+            rcopy(
+                self.g.at[n, 0, 0], self.r3.at[n, k - 1], self.s3s.at[n, 0], self.s3r.at[n, k - 1],
+                P_.dev(P_.sib),
+            ).wait_recv()
+        total = self.g[n, P_.t, P_.z].astype(F32)
+        for k in range(3):
+            total += self.r3[n, k].astype(F32)
+        return total
+
+    def sent(self, n):
+        P_ = self.P
+        for q in range(4):
+            self.copy1(n, q).wait_send()
+        self.copy2(n, 0, 0, P_.d2).wait_send()
+        self.copy2(n, 2, 2, P_.d2).wait_send()
+        self.copy2(n, 1, 1, P_.d1).wait_send()
+        for k in (1, 2, 3):
+            self.copy3(n, k).wait_send()
 
 
 def back_kernel(
-    len_ref, tok, gt, s2, nt, n1, qkv, lse, att, gsum, gl, pack_all,
-    gtok, gpack,
-    pack_v, gq, gacc, gst, rs1, rs2, rs3, s1s, s1r, s2s, s2r, s3s, s3r, lsem,
+    len_ref, tok, gt, s2, nt, n1, qkv, lse, att, gsum, gl, pack_all, dgi, dgd, xe,
+    gtok, gqkv, gwo, gex, gdd, gx,
+    pack_v, gq, gacc, n1t, ga_, gb_, gc_, ra1, ra2, ra3, rb1, rb2, rb3, rc1, rc2, rc3,
+    di, dj, gin, gdn, rin, rdn, tri, trd, *sems,
 ):
     P_ = Place()
-    z, t, b, c = P_.z, P_.t, P_.b, P_.c
+    z, t = P_.z, P_.t
     own, sib, d1, d2, dd = P_.own, P_.sib, P_.d1, P_.d2, P_.dd
-    meet([P_.dev(p) for p in (d1, d2, sib)] + [P_.dev(own, zz) for zz in P_.zk[1:]])
+    others = P_.plane_others()
+    zss, zsr, xs, xr, lsem = sems[18:]
+    sum_a = RowSum(P_, ga_, ra1, ra2, ra3, sems[0:6])
+    sum_b = RowSum(P_, gb_, rb1, rb2, rb3, sems[6:12])
+    sum_c = RowSum(P_, gc_, rc1, rc2, rc3, sems[12:18])
+    lw = pltpu.make_async_copy(pack_all, pack_v, lsem.at[0])
+    li = pltpu.make_async_copy(dgi, di, lsem.at[1])
+    lj = pltpu.make_async_copy(dgd, dj, lsem.at[2])
+    li.start()
+    lj.start()
+    lw.start()
+    meet([P_.dev(p) for p in others] + [P_.dev(own, zz) for zz in P_.zk[1:]])
     sends = []
 
     def go(cp):
         cp.start()
         sends.append(cp)
 
-    lw = pltpu.make_async_copy(pack_all, pack_v, lsem.at[0])
-    lw.start()
+    def rows(p):
+        return pl.ds(pl.multiple_of(P_.rank(p) * 32, 32), 32)
+
+    zsum = ZSum(P_, (gin, gdn), (rin, rdn), (tri, trd), zss, zsr)
+    li.wait()
+    lj.wait()
+    gin[0] = di[...].astype(BF).reshape(4, 256, 512)
+    gdn[0] = dj[...].astype(BF).reshape(4, 128, 1024)
+    zsum.ship(0)
+    le = pltpu.make_async_copy(xe.at[:, rows(own)], gx.at[t, 1:3], lsem.at[3])
+    le.start()
+    for i, p in enumerate(others):
+        go(rcopy(xe.at[:, rows(p)], gx.at[t, 1:3], xs.at[i], xr.at[t, 0], P_.dev(p)))
+
     lw.wait()
     extra = pack_v[:, :, EX : EX + 128].reshape(1024, 128)
     lane = lax.broadcasted_iota(jnp.int32, (384, 128), 1)
@@ -879,15 +1198,23 @@
     gs2 = gt[0:384].astype(F32) + norm_back(gnt, row_of(extra, 3), n_two, r_two)
     gtok[...] = gs2
     ga = gs2.astype(BF)
+
+    def put(ref, n, cols, val):
+        low = val.astype(BF)
+        for zz in range(4):
+            ref[n, :, zz, :, cols] = low[zz * 256 : (zz + 1) * 256].reshape(8, 32, low.shape[1])
+
     for j in range(2):
         cols = slice(j * 512, (j + 1) * 512)
-        gst[:, :, WO + j * 512 : WO + (j + 1) * 512] = (
-            dot_tn(att[...], ga[:, cols]).astype(BF).reshape(32, 32, 512)
-        )
+        put(ga_, 0, cols, dot_tn(att[...], ga[:, cols]))
+    sum_a.step1(0)
     gatt = dot_nt(ga[:, 0:512], pack_v[:, :, WO : WO + 512].reshape(1024, 512))
     gatt += dot_nt(ga[:, 512:1024], pack_v[:, :, WO + 512 : WO + 1024].reshape(1024, 512))
     gq[:, 0:1024] = gatt.astype(BF)
+    n1t[...] = jnp.transpose(n1[...])
+    gacc[...] = jnp.zeros_like(gacc)
     allowed = masks(len_ref[0])
+    sum_a.step2(0)
 
     def pair_step(p, carry):
         lo = pl.ds(pl.multiple_of(p * 128, 128), 128)
@@ -911,98 +1238,130 @@
         gq[:, hi] = dv.astype(BF)
         return carry
 
-    lax.fori_loop(0, 8, pair_step, 0)
-
-    def w_step(j, carry):
-        cols = pl.ds(pl.multiple_of(j * 512, 512), 512)
-        gcols = gq[:, cols]
-        gst[:, :, cols] = dot_tn(n1[...], gcols).astype(BF).reshape(32, 32, 512)
-        gacc[...] += dot_nt(gcols, pack_v[:, :, cols].reshape(1024, 512))
+    def chunk_step(j, carry):
+        lax.fori_loop(2 * j, 2 * j + 2, pair_step, 0)
+        for seg in range(3):
+            cols = pl.ds(pl.multiple_of(seg * 1024 + j * 256, 256), 256)
+            gcols = gq[:, cols]
+            put(gb_, j, slice(seg * 256, (seg + 1) * 256), dot_nn(n1t[...], gcols))
+            gacc[...] += dot_nt(gcols, pack_v[:, :, cols].reshape(1024, 256))
+        sum_b.step1(j)
+
+        @pl.when(j == 0)
+        def _():
+            zsum.transit(0)
+            sum_a.step3(0)
+
+        @pl.when(j == 1)
+        def _():
+            sum_a.step4(0)
+
+        @pl.when(j >= 1)
+        def _():
+            sum_b.step2(j - 1)
+
+        @pl.when(j >= 2)
+        def _():
+            sum_b.step3(j - 2)
+
+        @pl.when(j >= 3)
+        def _():
+            sum_b.step4(j - 3)
+
         return carry
 
-    gacc[...] = jnp.zeros_like(gacc)
-    lax.fori_loop(0, 6, w_step, 0)
+    lax.fori_loop(0, 4, chunk_step, 0)
     gn1 = gacc[...]
     n_one, r_one = norm_parts(tok[...].astype(F32))
     gain_one_row = jnp.sum(gn1 * n_one, axis=0, keepdims=True)
-    gtok[...] += norm_back(gn1, row_of(extra, 2), n_one, r_one)
     rowi = lax.broadcasted_iota(jnp.int32, (8, 1024), 0)
-    rows = jnp.where(rowi == 0, gain_one_row, jnp.where(rowi == 1, gain_two_row, 0.0)).astype(BF)
+    rws = jnp.where(rowi == 0, gain_one_row, jnp.where(rowi == 1, gain_two_row, 0.0)).astype(BF)
     sel = (
         lax.broadcasted_iota(jnp.int32, (8, 128), 1) == lax.broadcasted_iota(jnp.int32, (8, 128), 0) + 2
     ).astype(BF)
-    gst[:, :, EX : EX + 128] = (
-        (dot_tn(nt[...], two) + dot_tn(rows, sel)).astype(BF).reshape(32, 32, 128)
-    )
-
-    chips = (dd, d1, d2, own)
-    swap = (0, 2, 1, 3)
-    for q in range(4):
-        for k in range(4):
-            src = gst.at[P_.zk[k] * 8 + P_.rank(P_.flip(chips[q]))]
-            i = swap[q] * 4 + k
-            go(rcopy(src, rs1.at[i], s1s.at[i], s1r.at[i], P_.dev(sib)))
-
-    def in1(q, k):
-        i = q * 4 + k
-        rcopy(gst.at[0], rs1.at[i], s1s.at[0], s1r.at[i], P_.dev(sib)).wait_recv()
-        s = P_.zk[k] * 8 + P_.rank(chips[q])
-        gst[s] = (gst[s].astype(F32) + rs1[i].astype(F32)).astype(BF)
-
-    def out2(q, k, n, p):
-        i = n * 4 + k
-        go(rcopy(gst.at[P_.zk[k] * 8 + P_.rank(chips[q])], rs2.at[i], s2s.at[i], s2r.at[i], P_.dev(p)))
-
-    def in2(n, k, p):
-        i = n * 4 + k
-        rcopy(gst.at[0], rs2.at[i], s2s.at[0], s2r.at[i], P_.dev(sib)).wait_recv()
-        s = P_.zk[k] * 8 + P_.rank(p)
-        gst[s] = (gst[s].astype(F32) + rs2[i].astype(F32)).astype(BF)
-
-    for k in (3, 2, 1, 0):
-        in1(0, k)
-        out2(0, k, 0, d2)
-        in1(2, k)
-        out2(2, k, 2, d2)
-    for k in (3, 2, 1, 0):
-        in1(1, k)
-        in1(3, k)
-    for k in (3, 2, 1, 0):
-        in2(0, k, d1)
-        out2(1, k, 1, d1)
-    for k in (3, 2, 1, 0):
-        in2(2, k, own)
-        in2(1, k, own)
-        if k:
-            zz = P_.zk[k]
-            go(rcopy(gst.at[zz * 8 + t], rs3.at[k - 1], s3s.at[k - 1], s3r.at[k - 1], P_.dev(own, zz)))
-    acc = gst[b].astype(F32)
-    for k in (1, 2, 3):
-        rcopy(gst.at[0], rs3.at[k - 1], s3s.at[0], s3r.at[k - 1], P_.dev(sib)).wait_recv()
-        acc += rs3[k - 1].astype(F32)
-    gpack[...] = acc
+    put(gc_, 0, slice(0, 128), dot_tn(nt[...], two) + dot_tn(rws, sel))
+    sum_c.step1(0)
+    sum_b.step2(3)
+    sum_b.step3(2)
+    sum_c.step2(0)
+    gtok[...] += norm_back(gn1, row_of(extra, 2), n_one, r_one)
+    sum_b.step3(3)
+    sum_b.step4(1)
+    sum_c.step3(0)
+
+    zsum.arrived(0)
+    di[0:256] = gin[0, z].astype(F32) + rin[0, 0].astype(F32) + rin[0, 1].astype(F32)
+    gdd[...] = gdn[0, z].astype(F32) + rdn[0, 0].astype(F32) + rdn[0, 1].astype(F32)
+
+    @pl.when(zsum.mid)
+    def _():
+        di[0:256] += rin[0, 2].astype(F32)
+        gdd[...] += rdn[0, 2].astype(F32)
+
+    gin[0, z] = di[0:256].astype(BF)
+    lx = pltpu.make_async_copy(gin.at[:, z, rows(own)], gx.at[t, 0:1], lsem.at[4])
+    lx.start()
+    for i, p in enumerate(others):
+        go(rcopy(gin.at[:, z, rows(p)], gx.at[t, 0:1], xs.at[7 + i], xr.at[t, 1], P_.dev(p)))
+
+    sum_b.step4(2)
+    sum_b.step4(3)
+    sum_c.step4(0)
+    gwo[...] = sum_a.step5(0)
+    for j in range(4):
+        total = sum_b.step5(j)
+        for seg in range(3):
+            at = seg * 1024 + j * 256
+            gqkv[:, at : at + 256] = total[:, seg * 256 : (seg + 1) * 256]
+    gex[...] = sum_c.step5(0)
+    for p in others:
+        r = P_.rank(p)
+        rcopy(xe.at[:, rows(own)], gx.at[r, 1:3], xs.at[0], xr.at[r, 0], P_.dev(sib)).wait_recv()
+        rcopy(gin.at[:, 0, rows(own)], gx.at[r, 0:1], xs.at[0], xr.at[r, 1], P_.dev(sib)).wait_recv()
+    le.wait()
+    lx.wait()
+    zsum.sent(0)
+    sum_a.sent(0)
+    for j in range(4):
+        sum_b.sent(j)
+    sum_c.sent(0)
     for cp in sends:
         cp.wait_send()
 
 
-def run_back(lengths, tok, gt, s2, nt, n1, qkv, lse, att, gsum, gl, pack_all):
+def run_back(lengths, tok, gt, s2, nt, n1, qkv, lse, att, gsum, gl, pack_all, dgi, dgd, xe):
     sd = jax.ShapeDtypeStruct
     dma = pltpu.SemaphoreType.DMA
+    sizes = ((1, 1024), (4, 768), (1, 128))
+    blocks = [pltpu.VMEM((n, 8, 4, 32, w), BF) for n, w in sizes]
+    for n, w in sizes:
+        blocks += [
+            pltpu.VMEM((n, 4, 4, 32, w), BF), pltpu.VMEM((n, 3, 4, 32, w), BF), pltpu.VMEM((n, 3, 32, w), BF),
+        ]
+    sems = []
+    for n, _ in sizes:
+        sems += [dma((n, 4)), dma((n, 4)), dma((n, 3)), dma((n, 3)), dma((n, 3)), dma((n, 3))]
     return pl.pallas_call(
         back_kernel,
-        out_shape=(sd((384, 1024), F32), sd((32, PW), F32)),
-        in_specs=[SM] + [VM] * 10 + [ANY],
-        out_specs=(VM, VM),
+        out_shape=(
+            sd((384, 1024), F32), sd((32, 3072), F32), sd((32, 1024), F32), sd((32, 128), F32),
+            sd((128, 1024), F32), sd((8, 3, 32, 512), BF),
+        ),
+        in_specs=[SM] + [VM] * 10 + [ANY] * 4,
+        out_specs=(VM,) * 5 + (ANY,),
         scratch_shapes=[
-            pltpu.VMEM((32, 32, PW), BF), pltpu.VMEM((384, 3072), BF),
-            pltpu.VMEM((384, 1024), F32), pltpu.VMEM((32, 32, PW), BF),
-            pltpu.VMEM((16, 32, PW), BF), pltpu.VMEM((12, 32, PW), BF), pltpu.VMEM((3, 32, PW), BF),
-            dma((16,)), dma((16,)), dma((12,)), dma((12,)), dma((3,)), dma((3,)), dma((1,)),
+            pltpu.VMEM((32, 32, PW), BF), pltpu.VMEM((384, 3072), BF), pltpu.VMEM((384, 1024), F32),
+            pltpu.VMEM((1024, 384), BF), *blocks,
+            pltpu.VMEM((1024, 512), F32), pltpu.VMEM((512, 1024), F32),
+            pltpu.VMEM((1, 4, 256, 512), BF), pltpu.VMEM((1, 4, 128, 1024), BF),
+            pltpu.VMEM((1, 3, 256, 512), BF), pltpu.VMEM((1, 3, 128, 1024), BF),
+            pltpu.VMEM((1, 256, 512), BF), pltpu.VMEM((1, 128, 1024), BF),
+            *sems, dma((1, 8)), dma((1, 8)), dma((14,)), dma((8, 2)), dma((5,)),
         ],
         compiler_params=pltpu.CompilerParams(
-            collective_id=2, has_side_effects=True, vmem_limit_bytes=60 * MIB
+            collective_id=2, has_side_effects=True, vmem_limit_bytes=63 * MIB
         ),
-    )(lengths, tok, gt, s2, nt, n1, qkv, lse, att, gsum, gl, pack_all)
+    )(lengths, tok, gt, s2, nt, n1, qkv, lse, att, gsum, gl, pack_all, dgi, dgd, xe)
 
 
 def fused_device(
@@ -1031,15 +1390,14 @@
     qkv, lse, att, s2, nt, n1, wmix, pack_all, wi_all, wd_all, g_all = run_enter(
         lengths, tokens, pack, wia, wdn, gt
     )
-    block, gsum, gl, gdo, gx = run_ff(lengths, nt, wmix, s2, g_all, wi_all, wd_all)
-    gtok, gpack = run_back(
-        lengths, tokens, gt, s2, nt, n1, qkv, lse, att, gsum, gl, pack_all
-    )
-    gdo = gdo.reshape(3, 128, 1024)
+    block, gsum, gl, gde, xe, dgi, dgd = run_ff(lengths, nt, wmix, s2, g_all, wi_all, wd_all)
+    gtok, gqkv, gwo, gex, gdd, gx = run_back(
+        lengths, tokens, gt, s2, nt, n1, qkv, lse, att, gsum, gl, pack_all, dgi, dgd, xe
+    )
     gwi = gx.reshape(8, 3, 32, 4, 128).transpose(1, 2, 3, 0, 4).reshape(3, 32, 4096).astype(F32)
     return (
-        block, gtok, gpack[:, 0:3072], gpack[:, WO : WO + 1024], gpack[:, EX + 2],
-        gwi[0], gdo[0], gwi[1:], gdo[1:], gpack[:, EX : EX + 2], gpack[:, EX + 3],
+        block, gtok, gqkv, gwo, gex[:, 2], gwi[0], gdd, gwi[1:], gde.reshape(2, 128, 1024),
+        gex[:, 0:2], gex[:, 3],
     )
 
 

time: 487 us -> 341 us (0.70)
  Pallas kernels: 458 us -> 313 us
    pallas_call x1, Pallas kernels: 194 us -> 128 us  [run_ff(): pl.pallas_call(ff_kernel, out_shape=(sd((384, 1024), BF), sd((384, 1024),...]
    pallas_call x1, Pallas kernels: 163 us -> 117 us  [run_enter(): pl.pallas_call(enter_kernel, out_shape=(sd((384, 3072), BF), sd((384, 128...]
    pallas_call x1, Pallas kernels: 101 us -> 68.6 us  [run_back(): pl.pallas_call(back_kernel, out_shape=(sd((384, 1024), F32), sd((32, 3072...]
    slice x6 -> x1, local copies, waits for them, and re-layouts: 7.42 us -> 1.49 us  [fused_device(): gex[:, 3]]
    unnamed x34 -> x42, local copies, waits for them, and re-layouts: 9.37 us -> 13.3 us
where the time goes in v2:
time: 341 us; the launch traced here: 340 us
  Pallas kernels  313 us (92%)
  local copies, waits for them, and re-layouts  22.8 us (7%)
    pallas_call x1, Pallas kernels, run_ff(): pl.pallas_call(ff_kernel, out_shape=(sd((384, 1024), BF), sd((384, 1024),...  128 us
    pallas_call x1, Pallas kernels, run_enter(): pl.pallas_call(enter_kernel, out_shape=(sd((384, 3072), BF), sd((384, 128...  117 us
    pallas_call x1, Pallas kernels, run_back(): pl.pallas_call(back_kernel, out_shape=(sd((384, 1024), F32), sd((32, 3072...  68.6 us
    unnamed x42, local copies, waits for them, and re-layouts  13.3 us

profile of v2, /device:TPU:0, one launch (start us, length us, event | category | flops | bytes accessed | tf_op | source)
XLA Modules:
  0.0 340.0 jit_solution(6438623750640192599)
XLA Ops:
  1.4 0.7 select_convert_fusion
  2.1 0.7 copy.34
  2.8 0.8 copy.33
  3.6 0.8 copy.35
  4.3 1.0 concatenate.17.pack
  5.4 1.0 copy.41
  8.1 0.9 fusion.1.gt
  9.7 116.5 %shard_map.221 = (bf16[384,3072]{1,0:T(8,128)(2,1)}, f32[384,128]{1,0:T(8,128)S(1)}, bf16[384,1024]{1,0:T(8,128)(2,1)S(1)}, f32[384,1024]{1,0:T(8,128)}, bf16[38...) custom-call(s32[1]{0:T(128)} %copy.49.len_ref, ...), custom_call_target="tpu_custom_call" | custom-call | tf_op jit(solution)/shard_map/pallas_call | solution.py:628
  126.2 0.9 copy-done
  127.1 0.9 copy-done.2
  128.0 0.9 copy-done.3
  128.9 0.7 copy-done.4
  130.2 128.1 %shard_map.222 = (bf16[384,1024]{1,0:T(8,128)(2,1)}, f32[384,1024]{1,0:T(8,128)}, f32[384,128]{1,0:T(8,128)}, f32[256,1024]{1,0:T(8,128)}, bf16[2,256,512]{2,1,0...) custom-call(s32[1]{0:T(128)} %copy.49.len_ref, ...), custom_call_target="tpu_custom_call" | custom-call | tf_op jit(solution)/shard_map/pallas_call | solution.py:1026
  258.3 68.6 %shard_map.223 = (f32[384,1024]{1,0:T(8,128)}, f32[32,3072]{1,0:T(8,128)}, f32[32,1024]{1,0:T(8,128)}, f32[32,128]{1,0:T(8,128)}, f32[128,1024]{1,0:T(8,128)}, /*index=5*/bf16[8,3,32,512]{3,2,1,0:T(8,128)(2,1)}) custom-call(s32[1]{0:T(128)} %copy.49.len_ref, bf16[384,1024]{1,0:T(8,128)(2,1)} %tok.3, bf16[400,1024]{1,0:T(8,128)(2,1)} %fusion.1.gt, ...), custom_call_target="tpu_custom_call" | custom-call | tf_op jit(solution)/shard_map/pallas_call | solution.py:1344
  327.0 1.4 copy.40
  328.4 1.5 slice_reduce_fusion
  329.8 1.7 reshape.46
  332.4 1.2 slice.22
  333.8 0.9 squeeze.14
  334.7 0.9 copy.50
  335.6 1.1 copy.51
  336.8 0.7 copy.52
  338.2 0.8 copy.54
  339.0 1.0 copy.55
  (43 shorter events, 4.8 us)
Async XLA Ops:
  0.6 5.8 %copy-start.11 = (bf16[2,32,4096]{2,1,0:T(8,128)(2,1)S(1)}, bf16[2,32,4096]{2,1,0:T(8,128)(2,1)}, u32[]{:S(2)}) copy-start(bf16[2,32,4096]{2,1,0:T(8,128)(2,1)} %param.24) | copy-start | bytes 1572868
  6.8 1.1 copy-start.8
  8.0 1.1 copy-start.10
  8.0 1.2 copy-start.14
  8.1 1.6 copy-start.1
  126.2 0.9 copy-start
  127.1 0.9 copy-start.2
  128.0 0.9 copy-start.3
  128.9 0.7 copy-start.4
  129.6 0.7 copy-start.5
  332.4 2.4 copy-start.9
  333.8 1.8 copy-start.6
  335.6 1.2 copy-start.13
  335.6 2.0 copy-start.15
  335.6 2.6 copy-start.12
  336.8 2.2 copy-start.7

commit v3 on v2

--- a/solution.py
+++ b/solution.py
@@ -405,57 +405,55 @@
     def __init__(self, P_, mine, full, send, recv):
         self.P, self.mine, self.full, self.send, self.recv = P_, mine, full, send, recv
         self.mid = (P_.z == 1) | (P_.z == 2)
-
-    def copy(self, n, w, j):
+        self.all = range(len(mine))
+
+    def copy(self, w, j):
         P_ = self.P
         zs = P_.zk[2] if j == 4 else P_.z
-        block = self.full[w](n, zs) if j == 4 else self.mine[w](n)
+        block = self.full[w](zs) if j == 4 else self.mine[w]
         to = P_.dev(P_.own, P_.zk[1 if j == 4 else j])
-        return rcopy(
-            block, self.full[w](n, zs), self.send.at[n, w * 4 + j - 1], self.recv.at[n, w * 4 + zs], to
-        )
-
-    def landed(self, n, w, j):
+        return rcopy(block, self.full[w](zs), self.send.at[w * 4 + j - 1], self.recv.at[w * 4 + zs], to)
+
+    def landed(self, w, j):
         P_ = self.P
         zs = P_.zk[j]
         rcopy(
-            self.mine[w](n), self.full[w](n, zs), self.send.at[n, 0], self.recv.at[n, w * 4 + zs],
-            P_.dev(P_.sib),
+            self.mine[w], self.full[w](zs), self.send.at[0], self.recv.at[w * 4 + zs], P_.dev(P_.sib)
         ).wait_recv()
 
-    def ship(self, n):
-        for w in range(2):
-            self.copy(n, w, 2).start()
+    def ship(self):
+        for w in self.all:
+            self.copy(w, 2).start()
 
         @pl.when(self.mid)
         def _():
-            for w in range(2):
-                self.copy(n, w, 3).start()
-
-        for w in range(2):
-            self.copy(n, w, 1).start()
-
-    def relay(self, n):
-        for w in range(2):
-            self.landed(n, w, 2)
+            for w in self.all:
+                self.copy(w, 3).start()
+
+        for w in self.all:
+            self.copy(w, 1).start()
+
+    def relay(self):
+        for w in self.all:
+            self.landed(w, 2)
 
         @pl.when(self.mid)
         def _():
-            for w in range(2):
-                self.copy(n, w, 4).start()
-
-    def finish(self, n):
-        for w in range(2):
-            self.landed(n, w, 1)
-            self.landed(n, w, 3)
-            self.copy(n, w, 1).wait_send()
-            self.copy(n, w, 2).wait_send()
+            for w in self.all:
+                self.copy(w, 4).start()
+
+    def finish(self):
+        for w in self.all:
+            self.landed(w, 1)
+            self.landed(w, 3)
+            self.copy(w, 1).wait_send()
+            self.copy(w, 2).wait_send()
 
         @pl.when(self.mid)
         def _():
-            for w in range(2):
-                self.copy(n, w, 3).wait_send()
-                self.copy(n, w, 4).wait_send()
+            for w in self.all:
+                self.copy(w, 3).wait_send()
+                self.copy(w, 4).wait_send()
 
 
 PW = 4224
@@ -464,39 +462,73 @@
 
 
 def enter_kernel(
-    len_ref, tok, pack, wia, wdn, gt,
-    qkv, lse, att, s2, nt, n1, wmix, pack_all, wi_all, wd_all, g_all,
-    pack_v, ps, pr, asend, arecv, fsend, frecv, gs, gr, lsem,
+    len_ref, tok, cot, tab, w_qkv, w_out, small, w_in, w_ein, w_down, w_eout,
+    qkv_o, lse_o, att_o, s2_o, n1_o, wmix_o, pack_all, wi_all, wd_all, g_all, nt_all,
+    pack_v, wia, gt, qkv, lse, att, s2, nt, n1,
+    pz, ps, pr, asend, arecv, fsend, frecv, gs, gr, ts, tr, lsem, osem,
 ):
     P_ = Place()
     z, t, b = P_.z, P_.t, P_.b
     own, sib, d1, d2, dd = P_.own, P_.sib, P_.d1, P_.d2, P_.dd
     others = P_.plane_others()
+    pack = pack_v.at[b]
+    pack_v[b, :, 0:3072] = w_qkv[...]
+    pack_v[b, :, EX : EX + 128] = small[...]
+    pack_v[b, :, WO : WO + 1024] = w_out[...]
     meet([P_.dev(p) for p in others] + [P_.dev(own, zz) for zz in P_.zk[1:]])
     sends = []
+    keeps = []
 
     def go(cp):
         cp.start()
         sends.append(cp)
 
-    experts = ZGather(
-        P_, (lambda n: wi_all.at[1 + n, z], lambda n: wd_all.at[1 + n, z]),
-        (lambda n, zs: wi_all.at[1 + n, zs], lambda n, zs: wd_all.at[1 + n, zs]), fsend, frecv,
-    )
-    lc = pltpu.make_async_copy(pack, pack_v.at[b], lsem.at[0])
-    lc.start()
-    for k in range(1, 4):
-        go(rcopy(pack, pack_v.at[b], ps.at[k - 1], pr.at[b], P_.dev(own, P_.zk[k])))
-    go(rcopy(pack, pack_v.at[b], ps.at[3], pr.at[b], P_.dev(d1)))
-    go(rcopy(pack, pack_v.at[b], ps.at[7], pr.at[b], P_.dev(d2)))
-    go(rcopy(pack, pack_v.at[b], ps.at[15], pr.at[b], P_.dev(sib)))
+    def store(src, dst):
+        cp = pltpu.make_async_copy(src, dst, osem.at[len(keeps)])
+        cp.start()
+        keeps.append(cp)
+
+    def gather(n, mine, full):
+        return ZGather(P_, (mine,), (full,), fsend.at[n], frecv.at[n])
+
+    out_a = gather(0, w_eout.at[0], lambda zs: wd_all.at[1, zs])
+    out_b = gather(1, w_eout.at[1], lambda zs: wd_all.at[2, zs])
+    in_a = gather(2, wi_all.at[1, z], lambda zs: wi_all.at[1, zs])
+    in_b = gather(3, wi_all.at[2, z], lambda zs: wi_all.at[2, zs])
+    out_d = gather(4, w_down, lambda zs: wd_all.at[0, zs])
+    mid = in_a.mid
+
+    def z_copy(k, s, to):
+        return rcopy(pack_v.at[s], pack_v.at[s], pz.at[k - 1], pr.at[s], P_.dev(own, P_.zk[to]))
+
+    z_copy(2, b, 2).start()
+
+    @pl.when(mid)
+    def _():
+        z_copy(3, b, 3).start()
+
+    z_copy(1, b, 1).start()
+    go(rcopy(pack, pack, ps.at[3], pr.at[b], P_.dev(d1)))
+    go(rcopy(pack, pack, ps.at[7], pr.at[b], P_.dev(d2)))
+    go(rcopy(pack, pack, ps.at[15], pr.at[b], P_.dev(sib)))
+    out_a.ship()
+    for r in range(8):
+        for zz in range(4):
+            at = slice((zz * 8 + r) * 128, (zz * 8 + r + 1) * 128)
+            to = slice(zz * 128, (zz + 1) * 128)
+            wia[r, 0, :, to] = w_in[:, at]
+            wia[r, 1:3, :, to] = w_ein[:, :, at]
     rows = pl.ds(pl.multiple_of(t * 32, 32), 32)
     lw = pltpu.make_async_copy(wia.at[t], wi_all.at[:, z, rows], lsem.at[1])
     lw.start()
     for i, p in enumerate(others):
         go(rcopy(wia.at[P_.rank(p)], wi_all.at[:, z, rows], asend.at[i], arecv.at[t], P_.dev(p)))
-    ld = pltpu.make_async_copy(wdn, wd_all.at[:, z], lsem.at[2])
-    ld.start()
+    store(w_down, wd_all.at[0, z])
+    store(w_eout, wd_all.at[1:3, z])
+    keep = lax.broadcasted_iota(jnp.int32, (384, 1), 0) < len_ref[0]
+    gt[0:384] = jnp.where(keep, cot[...], jnp.zeros_like(cot[...]))
+    gt[384:400] = jnp.zeros((16, 1024), BF)
+    gt[384:385, 0:384] = tab[...].astype(BF)
 
     def landed(slot):
         rcopy(pack, pack_v.at[slot], ps.at[0], pr.at[slot], P_.dev(sib)).wait_recv()
@@ -508,23 +540,34 @@
         return P_.zk[k] * 8 + P_.rank(p)
 
     for k in range(0, 6):
+        if k == 2:
+            out_b.ship()
         if 1 <= k <= 3:
             s = slot(k, own)
             landed(s)
+            if k == 2:
+
+                @pl.when(mid)
+                def _():
+                    z_copy(4, s, 1).start()
+
             fwd(s, 3 + k, d1)
             fwd(s, 7 + k, d2)
             fwd(s, 15 + k, sib)
         if k == 3:
             lw.wait()
-            ld.wait()
             for p in others:
                 rr = P_.rank(p)
                 rq = pl.ds(pl.multiple_of(rr * 32, 32), 32)
                 rcopy(
                     wia.at[0], wi_all.at[:, z, rq], asend.at[0], arecv.at[rr], P_.dev(sib)
                 ).wait_recv()
-            for e in range(2):
-                experts.ship(e)
+            out_a.relay()
+            in_a.ship()
+        if k == 4:
+            store(gt, g_all.at[t])
+            for i, p in enumerate((d1, d2, sib)):
+                go(rcopy(gt, g_all.at[t], gs.at[i], gr.at[t], P_.dev(p)))
         if 1 <= k <= 4:
             s = slot(k - 1, d1)
             landed(s)
@@ -537,22 +580,19 @@
             s = slot(k - 2, dd)
             landed(s)
             fwd(s, 27 + k - 2, sib)
-    lg = pltpu.make_async_copy(gt, g_all.at[t], lsem.at[3])
-    lg.start()
-    for i, p in enumerate((d1, d2, sib)):
-        go(rcopy(gt, g_all.at[t], gs.at[i], gr.at[t], P_.dev(p)))
+    out_b.relay()
+    in_b.ship()
     stream = tok[...].astype(F32)
     for k in range(4):
         for p in (own, d1, d2, dd):
             landed(slot(k, P_.flip(p)))
-    lc.wait()
-    keep_all = pltpu.make_async_copy(pack_v, pack_all, lsem.at[0])
-    keep_all.start()
+    store(pack_v, pack_all)
+    store(pack_v.at[:, :, EX : EX + 128], wmix_o)
 
     extra = pack_v[:, :, EX : EX + 128].reshape(1024, 128)
-    wmix[...] = extra
     n_one, _ = norm_parts(stream)
     n1[...] = (n_one * row_of(extra, 2)).astype(BF)
+    store(n1, n1_o)
 
     def qkv_step(j, carry):
         cols = pl.ds(pl.multiple_of(j * 512, 512), 512)
@@ -560,18 +600,24 @@
         return carry
 
     lax.fori_loop(0, 6, qkv_step, 0)
-
-    def g_landed(p):
-        r = P_.rank(p)
-        rcopy(gt, g_all.at[r], gs.at[0], gr.at[r], P_.dev(sib)).wait_recv()
-        return r
-
-    def g_fwd(r, i, p):
-        go(rcopy(g_all.at[r], g_all.at[r], gs.at[i], gr.at[r], P_.dev(p)))
-
-    r = g_landed(d1)
-    g_fwd(r, 3, d2)
-    g_fwd(r, 4, sib)
+    store(qkv, qkv_o)
+
+    def plane(src_own, full, send, recv):
+        def landed_at(p):
+            r = P_.rank(p)
+            rcopy(src_own, full.at[r], send.at[0], recv.at[r], P_.dev(sib)).wait_recv()
+            return r
+
+        def pass_on(p, *dests):
+            r = landed_at(p)
+            for i, q in dests:
+                go(rcopy(full.at[r], full.at[r], send.at[i], recv.at[r], P_.dev(q)))
+
+        return landed_at, pass_on
+
+    g_landed, g_pass = plane(gt, g_all, gs, gr)
+    n_landed, n_pass = plane(nt, nt_all, ts, tr)
+    g_pass(d1, (3, d2), (4, sib))
 
     allowed = masks(len_ref[0])
     lane = lax.broadcasted_iota(jnp.int32, (384, 128), 1)
@@ -593,26 +639,49 @@
         att[:, pl.ds(pl.multiple_of(p * 128, 128), 128)] = jnp.where(
             lane < 64, outs[0], outs[1]
         ).astype(BF)
+
+        @pl.when(p == 4)
+        def _():
+            in_a.relay()
+            out_d.ship()
+
         return carry
 
     lax.fori_loop(0, 8, pair_step, 0)
-    r = g_landed(d2)
-    g_fwd(r, 5, sib)
-    experts.relay(0)
+    store(lse, lse_o)
+    store(att, att_o)
     for j in range(2):
         w = pack_v[:, :, WO + j * 512 : WO + (j + 1) * 512].reshape(1024, 512)
         s2[:, j * 512 : (j + 1) * 512] = stream[:, j * 512 : (j + 1) * 512] + dot_nn(att[...], w)
+    store(s2, s2_o)
     n_two, _ = norm_parts(s2[...])
     nt[...] = (n_two * row_of(extra, 3)).astype(BF)
-    r = g_landed(dd)
-    g_fwd(r, 6, sib)
+    store(nt, nt_all.at[t])
+    for i, p in enumerate((d1, d2, sib)):
+        go(rcopy(nt, nt_all.at[t], ts.at[i], tr.at[t], P_.dev(p)))
+    g_pass(d2, (5, sib))
+    g_pass(dd, (6, sib))
+    in_b.relay()
+    n_pass(d1, (3, d2), (4, sib))
+    n_pass(d2, (5, sib))
+    out_d.relay()
+    n_pass(dd, (6, sib))
     for p in (own, d1, d2, dd):
         g_landed(P_.flip(p))
-    experts.relay(1)
-    for e in range(2):
-        experts.finish(e)
-    lg.wait()
-    keep_all.wait()
+    for p in (own, d2, d1, dd):
+        n_landed(P_.flip(p))
+    for part in (out_a, out_b, in_a, in_b, out_d):
+        part.finish()
+    z_copy(1, b, 1).wait_send()
+    z_copy(2, b, 2).wait_send()
+
+    @pl.when(mid)
+    def _():
+        z_copy(3, b, 3).wait_send()
+        z_copy(4, b, 1).wait_send()
+
+    for cp in keeps:
+        cp.wait()
     for cp in sends:
         cp.wait_send()
 
@@ -623,34 +692,33 @@
     return (col <= row) & (col < seq_len)
 
 
-def run_enter(lengths, tok, pack, wia, wdn, gt):
+def run_enter(*args):
     sd = jax.ShapeDtypeStruct
+    dma = pltpu.SemaphoreType.DMA
     return pl.pallas_call(
         enter_kernel,
         out_shape=(
             sd((384, 3072), BF), sd((384, 128), F32), sd((384, 1024), BF), sd((384, 1024), F32),
-            sd((384, 1024), BF), sd((384, 1024), BF), sd((1024, 128), BF),
+            sd((384, 1024), BF), sd((32, 32, 128), BF),
             sd((32, 32, PW), BF), sd((3, 4, 256, 512), BF), sd((3, 4, 128, 1024), BF),
-            sd((8, 400, 1024), BF),
+            sd((8, 400, 1024), BF), sd((8, 384, 1024), BF),
         ),
-        in_specs=[SM, VM, ANY, ANY, ANY, ANY],
-        out_specs=(VM,) * 7 + (ANY,) * 4,
+        in_specs=[SM] + [VM] * 10,
+        out_specs=(ANY,) * 11,
         scratch_shapes=[
-            pltpu.VMEM((32, 32, PW), BF),
-            pltpu.SemaphoreType.DMA((31,)), pltpu.SemaphoreType.DMA((32,)),
-            pltpu.SemaphoreType.DMA((7,)), pltpu.SemaphoreType.DMA((8,)),
-            pltpu.SemaphoreType.DMA((2, 8)), pltpu.SemaphoreType.DMA((2, 8)),
-            pltpu.SemaphoreType.DMA((7,)), pltpu.SemaphoreType.DMA((8,)),
-            pltpu.SemaphoreType.DMA((4,)),
+            pltpu.VMEM((32, 32, PW), BF), pltpu.VMEM((8, 3, 32, 512), BF), pltpu.VMEM((400, 1024), BF),
+            pltpu.VMEM((384, 3072), BF), pltpu.VMEM((384, 128), F32), pltpu.VMEM((384, 1024), BF),
+            pltpu.VMEM((384, 1024), F32), pltpu.VMEM((384, 1024), BF), pltpu.VMEM((384, 1024), BF),
+            dma((4,)), dma((31,)), dma((32,)), dma((7,)), dma((8,)), dma((5, 4)), dma((5, 4)),
+            dma((7,)), dma((8,)), dma((7,)), dma((8,)), dma((4,)), dma((12,)),
         ],
         compiler_params=pltpu.CompilerParams(
-            collective_id=0, has_side_effects=True, vmem_limit_bytes=48 * MIB
+            collective_id=0, has_side_effects=True, vmem_limit_bytes=63 * MIB
         ),
-    )(lengths, tok, pack, wia, wdn, gt)
-
-
-def mix_of(logits):
-    delta = logits[:, 0:1] - logits[:, 1:2]
+    )(*args)
+
+
+def mix_of(delta):
     return 1.0 / (1.0 + jnp.exp(-delta)), 1.0 / (1.0 + jnp.exp(delta))
 
 
@@ -663,10 +731,10 @@
 
 
 def ff_kernel(
-    len_ref, nt_own, wmix, s2, g_all, wi_all, wd_all,
-    block, gsum, gl_out, gde, xe, dgi, dgd, r1, r2, rin, rdn, dwi, dwd,
-    nt_all, gbuf, br, gn, xb, yb, wi, wd, ai, ad, gin, gdn, tri, trd, tmp, gc, gcr, dots,
-    ts, tr, gsem, wsem, zas, zar, zss, zsr, s1s, s1r, s2s, s2r, cs, cr, lsem, tsem,
+    len_ref, nt_hbm, wmix, s2, g_all, wi_all, wd_all,
+    block, gsum, gl_out, gde, xe, dgi, dgd, r1, r2, rin, rdn, dwi,
+    nt_all, gbuf, br, gn, xb, yb, wi, wd, ai, ad, gin, gdn, tri, trd, tmp, gc, gcr, dots, gaps,
+    tr, gsem, wsem, dsem, zas, zar, zss, zsr, s1s, s1r, s2s, s2r, cs, cr, lsem, tsem,
 ):
     P_ = Place()
     z, t = P_.z, P_.t
@@ -679,37 +747,30 @@
         cp.start()
         sends.append(cp)
 
-    ln = pltpu.make_async_copy(nt_own, nt_all.at[t], lsem.at[0])
-    ln.start()
-    for i, p in enumerate((d1, d2, sib)):
-        go(rcopy(nt_own, nt_all.at[t], ts.at[i], tr.at[t], P_.dev(p)))
     dense = ZGather(
-        P_, (lambda n: wi_all.at[0, z], lambda n: wd_all.at[0, z]),
-        (lambda n, zs: dwi.at[zs], lambda n, zs: dwd.at[zs]), zas, zar,
-    )
-    dense.ship(0)
-    l0 = pltpu.make_async_copy(wi_all.at[0, z], dwi.at[z], lsem.at[1])
-    l1 = pltpu.make_async_copy(wd_all.at[0, z], dwd.at[z], lsem.at[2])
-    l0.start()
-    l1.start()
+        P_, (wi_all.at[0, z],), (lambda zs: dwi.at[zs],), zas, zar
+    )
+    dense.ship()
     s2_in = pltpu.make_async_copy(s2, gsum, lsem.at[3])
     s2_in.start()
 
-    def w_load(e):
-        return (
-            pltpu.make_async_copy(wi_all.at[1 + e], wi.at[e], wsem.at[e, 0]),
-            pltpu.make_async_copy(wd_all.at[1 + e], wd.at[e], wsem.at[e, 1]),
-        )
+    expert_load = (
+        pltpu.make_async_copy(wi_all.at[1], wi.at[0], wsem.at[0, 0]),
+        pltpu.make_async_copy(wd_all.at[1], wd.at[0], wsem.at[0, 1]),
+        pltpu.make_async_copy(wi_all.at[2], wi.at[1], wsem.at[1, 0]),
+        pltpu.make_async_copy(wd_all.at[2], wd.at[1], wsem.at[1, 1]),
+    )
+    for cp in expert_load:
+        cp.start()
 
     def dense_load():
-        return (
-            pltpu.make_async_copy(dwi, wi.at[0], wsem.at[0, 0]),
-            pltpu.make_async_copy(dwd, wd.at[0], wsem.at[0, 1]),
-        )
-
-    for e in range(2):
-        for cp in w_load(e):
-            cp.start()
+        copies = [pltpu.make_async_copy(wd_all.at[0], wd.at[0], dsem.at[4])]
+        for k in range(4):
+            zz = P_.zk[k]
+            src = wi_all.at[0, z] if k == 0 else dwi.at[zz]
+            copies.append(pltpu.make_async_copy(src, wi.at[0, zz], dsem.at[k]))
+        return copies
+
     zsum = ZSum(P_, (gin, gdn), (rin, rdn), (tri, trd), zss, zsr)
 
     order = (own, sib, d1, P_.flip(d2), d2, P_.flip(d1), dd, P_.flip(dd))
@@ -736,23 +797,20 @@
 
     lane = lax.broadcasted_iota(jnp.int32, (448, 128), 1)
 
-    def shares(tab, e):
-        slot = lax.broadcasted_iota(jnp.int32, (112, 384), 0) + e * 112
+    def shares(tab):
+        slot = lax.broadcasted_iota(jnp.int32, (224, 384), 0)
         return (tab == slot.astype(F32)).astype(BF)
 
-    fwds = {2: (d1, ((3, d2), (4, sib))), 4: (d2, ((5, sib),)), 6: (dd, ((6, sib),))}
-
-    def fwd_copy(p, i, q):
-        r = P_.rank(p)
-        return rcopy(nt_all.at[r], nt_all.at[r], ts.at[i], tr.at[r], P_.dev(q))
-
+    def n_copy(s):
+        return pltpu.make_async_copy(nt_hbm.at[s], nt_all.at[s], tr.at[s])
+
+    for s in ranks:
+        n_copy(s).start()
     g_copy(0).start()
     ai[...] = jnp.zeros_like(ai)
     ad[...] = jnp.zeros_like(ad)
-    ln.wait()
-    for e in range(2):
-        for cp in w_load(e):
-            cp.wait()
+    for cp in expert_load:
+        cp.wait()
 
     def arrive(i, carry):
         s = seq_at(i)
@@ -761,66 +819,56 @@
         def _():
             g_copy(i + 1).start()
 
-        @pl.when(i > 0)
-        def _():
-            rcopy(nt_own, nt_all.at[s], ts.at[0], tr.at[s], P_.dev(sib)).wait_recv()
-
-        for k, (p, dests) in fwds.items():
-
-            @pl.when(i == k)
-            def _():
-                for n, q in dests:
-                    fwd_copy(p, n, q).start()
-
+        n_copy(s).wait()
         g_copy(i).wait()
         xv = nt_all[s]
         gv = gbuf[i % 2, :384]
         tab = gbuf[i % 2, 384:400][0:1, :384].astype(F32)
-        _, m1 = mix_of(dot_nn(xv, wmix[...]))
+        lg = dot_nn(xv, wmix[...])
+        gap = lg[:, 0:1] - lg[:, 1:2]
+        gaps[i] = jnp.transpose(jnp.broadcast_to(gap, (384, 128)))[0:8]
+        _, m1 = mix_of(gap)
         ge = (m1 * gv.astype(F32)).astype(BF)
-        for e in range(2):
-            sh = shares(tab, e)
-            xb[e, i] = dot_nn(sh, xv).astype(BF)
-            yb[e, i] = dot_nn(sh, ge).astype(BF)
+        sh = shares(tab)
+        xb[i] = dot_nn(sh, xv).astype(BF).reshape(2, 112, 1024)
+        yb[i] = dot_nn(sh, ge).astype(BF).reshape(2, 112, 1024)
         return carry
+
+    def expert(b, e):
+        four = pl.ds(b * 4, 4)
+        gq = yb[four, e].reshape(448, 1024)
+        yv, gb = ff(xb[four, e].reshape(448, 1024), gq, e)
+        rs = jnp.sum(gq.astype(F32) * yv, axis=-1, keepdims=True)
+        high = rs.astype(BF).astype(F32)
+        dots[four, e] = (
+            jnp.where(lane == 0, high, jnp.where(lane == 1, rs - high, 0.0))
+            .astype(BF)
+            .reshape(4, 112, 128)
+        )
+        xb[four, e] = yv.astype(BF).reshape(4, 112, 1024)
+        yb[four, e] = gb.astype(BF).reshape(4, 112, 1024)
+
+    def stage(e):
+        gin[e] = ai[e].astype(BF).reshape(4, 256, 512)
+        gdn[e] = ad[e].astype(BF).reshape(4, 128, 1024)
+        zsum.ship(e)
 
     def half(b, carry):
         lax.fori_loop(b * 4, b * 4 + 4, arrive, 0)
-
-        @pl.when(b == 1)
-        def _():
-            dense.relay(0)
-
-        def expert(e, carry):
-            four = pl.ds(b * 4, 4)
-            gq = yb[e, four].reshape(448, 1024)
-            yv, gb = ff(xb[e, four].reshape(448, 1024), gq, e)
-            rs = jnp.sum(gq.astype(F32) * yv, axis=-1, keepdims=True)
-            high = rs.astype(BF).astype(F32)
-            dots[e, four] = (
-                jnp.where(lane == 0, high, jnp.where(lane == 1, rs - high, 0.0))
-                .astype(BF)
-                .reshape(4, 112, 128)
-            )
-            xb[e, four] = yv.astype(BF).reshape(4, 112, 1024)
-            yb[e, four] = gb.astype(BF).reshape(4, 112, 1024)
-
-            @pl.when(b == 1)
-            def _():
-                gin[e] = ai[e].astype(BF).reshape(4, 256, 512)
-                gdn[e] = ad[e].astype(BF).reshape(4, 128, 1024)
-                zsum.ship(e)
-
-            return carry
-
-        lax.fori_loop(0, 2, expert, 0)
+        expert(b, 0)
         return carry
 
+    def half_two(b, carry):
+        expert(b, 1)
+        return carry
+
     lax.fori_loop(0, 2, half, 0)
+    stage(0)
+    dense.relay()
+    lax.fori_loop(0, 2, half_two, 0)
+    stage(1)
     g_copy(7).start()
-    l0.wait()
-    l1.wait()
-    dense.finish(0)
+    dense.finish()
     for cp in dense_load():
         cp.start()
     ai[0] = jnp.zeros_like(ai[0])
@@ -839,7 +887,7 @@
     def load1(q, w, start):
         cp = pltpu.make_async_copy(r1.at[w, q], tmp.at[w], tsem.at[w])
         if start:
-            rcopy(nt_own, r1.at[w, q], s1s.at[0, 0], s1r.at[w, q], P_.dev(sib)).wait_recv()
+            rcopy(tmp.at[0], r1.at[w, q], s1s.at[0, 0], s1r.at[w, q], P_.dev(sib)).wait_recv()
             cp.start()
         else:
             cp.wait()
@@ -848,7 +896,7 @@
     def load2(k, p, w, start):
         cp = pltpu.make_async_copy(r2.at[w, k], tmp.at[w], tsem.at[w])
         if start:
-            rcopy(nt_own, r2.at[w, k], s2s.at[0, 0], s2r.at[w, k], P_.dev(sib)).wait_recv()
+            rcopy(tmp.at[0], r2.at[w, k], s2s.at[0, 0], s2r.at[w, k], P_.dev(sib)).wait_recv()
             cp.start()
         else:
             cp.wait()
@@ -861,6 +909,12 @@
         src = both[w].at[P_.rank(chips[q])]
         return rcopy(src, r2.at[w, k], s2s.at[w, k], s2r.at[w, k], P_.dev(p))
 
+    def at_step(step, k, fn):
+        @pl.when(step == k)
+        def _():
+            for w in range(2):
+                fn(w)
+
     def dense_step(k, carry):
         i = 7 - k
         s = seq_at(i)
@@ -873,65 +927,54 @@
         xv = nt_all[s]
         gf = gbuf[i % 2, :384].astype(F32)
         tab = gbuf[i % 2, 384:400][0:1, :384].astype(F32)
-        m0, m1 = mix_of(dot_nn(xv, wmix[...]))
+        gap = jnp.transpose(jnp.broadcast_to(gaps[i][0:1], (128, 384)))[:, 0:1]
+        m0, m1 = mix_of(gap)
         out, gxv = ff(xv, (m0 * gf).astype(BF), 0)
+        at_step(k, 1, lambda w: load1(0, w, True))
+        at_step(k, 3, lambda w: load1(2, w, True))
+        at_step(k, 5, lambda w: load1(1, w, True))
+        at_step(k, 7, lambda w: load1(3, w, True))
         col = jnp.broadcast_to(jnp.sum(gf * out, axis=-1, keepdims=True), (384, 128))
         gc[s, 0:8] = jnp.transpose(col)[0:8]
-        s0, s1 = shares(tab, 0), shares(tab, 1)
-        q1 = dot_tn(s0, dots[0, i]) + dot_tn(s1, dots[1, i])
+        sh = shares(tab)
+        q1 = dot_tn(sh, dots[i].reshape(224, 128))
         gc[s, 8:16] = jnp.transpose(jnp.broadcast_to(q1[:, 0:1] + q1[:, 1:2], (384, 128)))[0:8]
-        br[s] = (m0 * out + m1 * (dot_tn(s0, xb[0, i]) + dot_tn(s1, xb[1, i]))).astype(BF)
-        gn[s] = (gxv + dot_tn(s0, yb[0, i]) + dot_tn(s1, yb[1, i])).astype(BF)
-
-        for step, q in ((0, 0), (2, 1), (4, 2), (6, 3)):
-
-            @pl.when(k == step)
-            def _():
-                for w in range(2):
-                    give1(q, w).start()
-
-        @pl.when(k == 1)
-        def _():
-            for w in range(2):
-                load1(0, w, True)
+        gn[s] = (gxv + dot_tn(sh, yb[i].reshape(224, 1024))).astype(BF)
+        br[s] = (m0 * out + m1 * dot_tn(sh, xb[i].reshape(224, 1024))).astype(BF)
+
+        for q in range(4):
+            at_step(k, 2 * q, lambda w, q=q: give1(q, w).start())
+
+        def pass_on(q, n, p):
+            def fn(w):
+                load1(q, w, False)
+                give2(q, n, p, w).start()
+
+            return fn
+
+        at_step(k, 1, pass_on(0, 0, d2))
+        at_step(k, 3, pass_on(2, 2, d2))
+        at_step(k, 5, lambda w: load1(1, w, False))
+        at_step(k, 5, lambda w: load2(0, d1, w, True))
+
+        def turn(w):
+            load2(0, d1, w, False)
+            give2(1, 1, d1, w).start()
+
+        at_step(k, 5, turn)
+        at_step(k, 7, lambda w: load1(3, w, False))
 
         @pl.when(k == 2)
         def _():
-            for w in range(2):
-                load1(0, w, False)
-                give2(0, 0, d2, w).start()
             zsum.transit(0)
 
-        @pl.when(k == 3)
-        def _():
-            for w in range(2):
-                load1(2, w, True)
-
-        @pl.when(k == 4)
-        def _():
-            for w in range(2):
-                load1(2, w, False)
-                give2(2, 2, d2, w).start()
-
         @pl.when(k == 5)
         def _():
-            for w in range(2):
-                load1(1, w, True)
             zsum.transit(1)
 
-        @pl.when(k == 6)
-        def _():
-            for w in range(2):
-                load1(1, w, False)
-                load2(0, d1, w, True)
-
         return carry
 
     lax.fori_loop(0, 8, dense_step, 0)
-    for w in range(2):
-        load2(0, d1, w, False)
-        give2(1, 1, d1, w).start()
-        load1(3, w, True)
     for i, p in enumerate(others):
         go(rcopy(gc.at[P_.rank(p)], gcr.at[t], cs.at[i], cr.at[t], P_.dev(p)))
     o0 = pltpu.make_async_copy(ai.at[0], dgi, lsem.at[0])
@@ -939,7 +982,6 @@
     o0.start()
     o1.start()
     for w in range(2):
-        load1(3, w, False)
         load2(2, own, w, True)
     for w in range(2):
         load2(2, own, w, False)
@@ -958,12 +1000,9 @@
     tot = jnp.sum(gcr[...], axis=0)
     gc0 = jnp.transpose(jnp.broadcast_to(tot[0:1], (128, 384)))
     q1 = jnp.transpose(jnp.broadcast_to(tot[8:9], (128, 384)))
-    m0, m1 = mix_of(dot_nn(nt_all[t], wmix[...]))
+    m0, m1 = mix_of(jnp.transpose(jnp.broadcast_to(gaps[0][0:1], (128, 384))))
     gl_out[...] = m0 * (m1 * gc0 - q1)
 
-    for k, (p, dests) in fwds.items():
-        for n, q in dests:
-            fwd_copy(p, n, q).wait_send()
     mids = zsum.mid
 
     def third(e):
@@ -1030,21 +1069,22 @@
             sd((256, 1024), F32), sd((2, 256, 512), BF), sd((1024, 512), F32), sd((512, 1024), F32),
             sd((2, 4, 384, 1024), BF), sd((2, 3, 384, 1024), BF),
             sd((2, 3, 256, 512), BF), sd((2, 3, 128, 1024), BF),
-            sd((4, 256, 512), BF), sd((4, 128, 1024), BF),
+            sd((4, 256, 512), BF),
         ),
         in_specs=[SM, ANY, VM, ANY, ANY, ANY, ANY],
-        out_specs=(VM,) * 3 + (ANY,) * 10,
+        out_specs=(VM,) * 3 + (ANY,) * 9,
         scratch_shapes=[
             pltpu.VMEM((8, 384, 1024), BF), pltpu.VMEM((2, 400, 1024), BF),
             pltpu.VMEM((8, 384, 1024), BF), pltpu.VMEM((8, 384, 1024), BF),
-            pltpu.VMEM((2, 8, 112, 1024), BF), pltpu.VMEM((2, 8, 112, 1024), BF),
+            pltpu.VMEM((8, 2, 112, 1024), BF), pltpu.VMEM((8, 2, 112, 1024), BF),
             pltpu.VMEM((2, 4, 256, 512), BF), pltpu.VMEM((2, 4, 128, 1024), BF),
             pltpu.VMEM((2, 1024, 512), F32), pltpu.VMEM((2, 512, 1024), F32),
             pltpu.VMEM((2, 4, 256, 512), BF), pltpu.VMEM((2, 4, 128, 1024), BF),
             pltpu.VMEM((2, 256, 512), BF), pltpu.VMEM((2, 128, 1024), BF),
             pltpu.VMEM((2, 384, 1024), BF),
-            pltpu.VMEM((8, 16, 384), F32), pltpu.VMEM((8, 16, 384), F32), pltpu.VMEM((2, 8, 112, 128), BF),
-            dma((7,)), dma((8,)), dma((2,)), dma((2, 2)), dma((1, 8)), dma((1, 8)), dma((2, 8)), dma((2, 8)),
+            pltpu.VMEM((8, 16, 384), F32), pltpu.VMEM((8, 16, 384), F32), pltpu.VMEM((8, 2, 112, 128), BF),
+            pltpu.VMEM((8, 8, 384), F32),
+            dma((8,)), dma((2,)), dma((2, 2)), dma((5,)), dma((4,)), dma((4,)), dma((2, 8)), dma((2, 8)),
             dma((2, 4)), dma((2, 4)), dma((2, 3)), dma((2, 3)), dma((7,)), dma((8,)), dma((10,)), dma((2,)),
         ],
         compiler_params=pltpu.CompilerParams(
@@ -1142,8 +1182,9 @@
 
 
 def back_kernel(
-    len_ref, tok, gt, s2, nt, n1, qkv, lse, att, gsum, gl, pack_all, dgi, dgd, xe,
-    gtok, gqkv, gwo, gex, gdd, gx,
+    len_ref, tok, s2, n1, qkv, lse, att, gsum, gl, g_all, nt_all, pack_all, dgi, dgd, xe,
+    gtok, gqkv, gwo, gex, gdd, gwi, gwe,
+    gx, gt, nt,
     pack_v, gq, gacc, n1t, ga_, gb_, gc_, ra1, ra2, ra3, rb1, rb2, rb3, rc1, rc2, rc3,
     di, dj, gin, gdn, rin, rdn, tri, trd, *sems,
 ):
@@ -1161,6 +1202,12 @@
     li.start()
     lj.start()
     lw.start()
+    own_in = (
+        pltpu.make_async_copy(g_all.at[t], gt, lsem.at[5]),
+        pltpu.make_async_copy(nt_all.at[t], nt, lsem.at[6]),
+    )
+    for cp in own_in:
+        cp.start()
     meet([P_.dev(p) for p in others] + [P_.dev(own, zz) for zz in P_.zk[1:]])
     sends = []
 
@@ -1183,6 +1230,8 @@
         go(rcopy(xe.at[:, rows(p)], gx.at[t, 1:3], xs.at[i], xr.at[t, 0], P_.dev(p)))
 
     lw.wait()
+    for cp in own_in:
+        cp.wait()
     extra = pack_v[:, :, EX : EX + 128].reshape(1024, 128)
     lane = lax.broadcasted_iota(jnp.int32, (384, 128), 1)
     glv = gl[...]
@@ -1320,6 +1369,12 @@
         rcopy(gin.at[:, 0, rows(own)], gx.at[r, 0:1], xs.at[0], xr.at[r, 1], P_.dev(sib)).wait_recv()
     le.wait()
     lx.wait()
+    for r in range(8):
+        for zz in range(4):
+            to = slice((zz * 8 + r) * 128, (zz * 8 + r + 1) * 128)
+            at = slice(zz * 128, (zz + 1) * 128)
+            gwi[:, to] = gx[r, 0, :, at].astype(F32)
+            gwe[:, :, to] = gx[r, 1:3, :, at].astype(F32)
     zsum.sent(0)
     sum_a.sent(0)
     for j in range(4):
@@ -1329,7 +1384,7 @@
         cp.wait_send()
 
 
-def run_back(lengths, tok, gt, s2, nt, n1, qkv, lse, att, gsum, gl, pack_all, dgi, dgd, xe):
+def run_back(*args):
     sd = jax.ShapeDtypeStruct
     dma = pltpu.SemaphoreType.DMA
     sizes = ((1, 1024), (4, 768), (1, 128))
@@ -1345,59 +1400,47 @@
         back_kernel,
         out_shape=(
             sd((384, 1024), F32), sd((32, 3072), F32), sd((32, 1024), F32), sd((32, 128), F32),
-            sd((128, 1024), F32), sd((8, 3, 32, 512), BF),
+            sd((128, 1024), F32), sd((32, 4096), F32), sd((2, 32, 4096), F32),
         ),
-        in_specs=[SM] + [VM] * 10 + [ANY] * 4,
-        out_specs=(VM,) * 5 + (ANY,),
+        in_specs=[SM] + [VM] * 8 + [ANY] * 6,
+        out_specs=(VM,) * 7,
         scratch_shapes=[
+            pltpu.VMEM((8, 3, 32, 512), BF), pltpu.VMEM((400, 1024), BF), pltpu.VMEM((384, 1024), BF),
             pltpu.VMEM((32, 32, PW), BF), pltpu.VMEM((384, 3072), BF), pltpu.VMEM((384, 1024), F32),
             pltpu.VMEM((1024, 384), BF), *blocks,
             pltpu.VMEM((1024, 512), F32), pltpu.VMEM((512, 1024), F32),
             pltpu.VMEM((1, 4, 256, 512), BF), pltpu.VMEM((1, 4, 128, 1024), BF),
             pltpu.VMEM((1, 3, 256, 512), BF), pltpu.VMEM((1, 3, 128, 1024), BF),
             pltpu.VMEM((1, 256, 512), BF), pltpu.VMEM((1, 128, 1024), BF),
-            *sems, dma((1, 8)), dma((1, 8)), dma((14,)), dma((8, 2)), dma((5,)),
+            *sems, dma((1, 8)), dma((1, 8)), dma((14,)), dma((8, 2)), dma((7,)),
         ],
         compiler_params=pltpu.CompilerParams(
             collective_id=2, has_side_effects=True, vmem_limit_bytes=63 * MIB
         ),
-    )(lengths, tok, gt, s2, nt, n1, qkv, lse, att, gsum, gl, pack_all, dgi, dgd, xe)
+    )(*args)
 
 
 def fused_device(
     tokens, cotangent, lengths, expert_ids, slot_ids, w_qkv, w_out, gain_one, w_in, w_down,
     w_expert_in, w_expert_out, w_mix, gain_two,
 ):
-    keep = jnp.arange(384, dtype=jnp.int32) < lengths[0]
-    table = jnp.where(slot_ids >= 0, expert_ids * CAP + slot_ids, -1).astype(BF)
-    gt = jnp.concatenate(
-        [
-            jnp.where(keep[:, None], cotangent, jnp.zeros_like(cotangent)),
-            jnp.pad(table[None, :], ((0, 15), (0, 640))),
-        ],
-        axis=0,
-    )
-    pack = jnp.concatenate(
-        [
-            w_qkv, w_mix, gain_one[:, None], gain_two[:, None],
-            jnp.zeros((32, 124), BF), w_out,
-        ],
-        axis=1,
-    )
-    wia = jnp.concatenate([w_in[None], w_expert_in], axis=0)
-    wia = wia.reshape(3, 32, 4, 8, 128).transpose(3, 0, 1, 2, 4).reshape(8, 3, 32, 512)
-    wdn = jnp.concatenate([w_down[None], w_expert_out], axis=0)
-    qkv, lse, att, s2, nt, n1, wmix, pack_all, wi_all, wd_all, g_all = run_enter(
-        lengths, tokens, pack, wia, wdn, gt
-    )
-    block, gsum, gl, gde, xe, dgi, dgd = run_ff(lengths, nt, wmix, s2, g_all, wi_all, wd_all)
-    gtok, gqkv, gwo, gex, gdd, gx = run_back(
-        lengths, tokens, gt, s2, nt, n1, qkv, lse, att, gsum, gl, pack_all, dgi, dgd, xe
-    )
-    gwi = gx.reshape(8, 3, 32, 4, 128).transpose(1, 2, 3, 0, 4).reshape(3, 32, 4096).astype(F32)
+    table = jnp.where(slot_ids >= 0, expert_ids * CAP + slot_ids, -1).astype(F32)
+    lane = jnp.arange(128, dtype=jnp.int32)[None, :]
+    small = jnp.zeros((32, 128), BF)
+    for k, col in enumerate((w_mix[:, 0], w_mix[:, 1], gain_one, gain_two)):
+        small = jnp.where(lane == k, col[:, None], small)
+    qkv, lse, att, s2, n1, wmix, pack_all, wi_all, wd_all, g_all, nt_all = run_enter(
+        lengths, tokens, cotangent, table.reshape(1, 384),
+        w_qkv, w_out, small, w_in, w_expert_in, w_down, w_expert_out,
+    )
+    block, gsum, gl, gde, xe, dgi, dgd = run_ff(
+        lengths, nt_all, wmix.reshape(1024, 128), s2, g_all, wi_all, wd_all
+    )
+    gtok, gqkv, gwo, gex, gdd, gwi, gwe = run_back(
+        lengths, tokens, s2, n1, qkv, lse, att, gsum, gl, g_all, nt_all, pack_all, dgi, dgd, xe
+    )
     return (
-        block, gtok, gqkv, gwo, gex[:, 2], gwi[0], gdd, gwi[1:], gde.reshape(2, 128, 1024),
-        gex[:, 0:2], gex[:, 3],
+        block, gtok, gqkv, gwo, gex[:, 2], gwi, gdd, gwe, gde.reshape(2, 128, 1024), gex[:, 0:2], gex[:, 3],
     )
 
 

time: 341 us -> 318 us (0.933)
  local copies, waits for them, and re-layouts: 22.8 us -> 11.3 us
  Pallas kernels: 313 us -> 303 us
    pallas_call x1, Pallas kernels: 128 us -> 115 us  [run_ff(): pl.pallas_call(ff_kernel, out_shape=(sd((384, 1024), BF), sd((384, 1024),...]
    unnamed x42 -> x25, local copies, waits for them, and re-layouts: 13.3 us -> 8.45 us
where the time goes in v3:
time: 318 us; the launch traced here: 317 us
  Pallas kernels  303 us (95%)
  local copies, waits for them, and re-layouts  11.3 us (4%)
    pallas_call x1, Pallas kernels, run_enter(): pl.pallas_call(enter_kernel, out_shape=(sd((384, 3072), BF), sd((384, 128...  119 us
    pallas_call x1, Pallas kernels, run_ff(): pl.pallas_call(ff_kernel, out_shape=(sd((384, 1024), BF), sd((384, 1024),...  115 us
    pallas_call x1, Pallas kernels, run_back(): pl.pallas_call(back_kernel, out_shape=(sd((384, 1024), F32), sd((32, 3072...  69 us
    unnamed x25, local copies, waits for them, and re-layouts  8.45 us

profile of v3, /device:TPU:0, one launch (start us, length us, event | category | flops | bytes accessed | tf_op | source)
XLA Modules:
  0.0 317.2 jit_solution(17742265732851847085)
XLA Ops:
  1.3 0.7 slice_bitcast_fusion.1
  2.0 0.7 select_convert_fusion
  2.7 0.6 reshape.53.tab
  3.3 1.4 select_select_fusion.small
  4.7 118.8 %shard_map.221 = (bf16[384,3072]{1,0:T(8,128)(2,1)}, f32[384,128]{1,0:T(8,128)}, bf16[384,1024]{1,0:T(8,128)(2,1)}, f32[384,1024]{1,0:T(8,128)}, bf16[384,1024]{...) custom-call(s32[1]{0:T(128)S(6)} %copy.35.len_ref, ...), custom_call_target="tpu_custom_call" | custom-call | tf_op jit(solution)/shard_map/pallas_call | solution.py:698
  123.5 114.8 %shard_map.222 = (bf16[384,1024]{1,0:T(8,128)(2,1)}, f32[384,1024]{1,0:T(8,128)}, f32[384,128]{1,0:T(8,128)}, f32[256,1024]{1,0:T(8,128)}, bf16[2,256,512]{2,1,0...) custom-call(s32[1]{0:T(128)S(6)} %copy.35.len_ref, ...), custom_call_target="tpu_custom_call" | custom-call | tf_op jit(solution)/shard_map/pallas_call | solution.py:1065
  238.3 0.0 copy-start.3
  238.3 69.0 %shard_map.223 = (f32[384,1024]{1,0:T(8,128)}, f32[32,3072]{1,0:T(8,128)}, f32[32,1024]{1,0:T(8,128)}, f32[32,128]{1,0:T(8,128)}, f32[128,1024]{1,0:T(8,128)}, /...) custom-call(s32[1]{0:T(128)S(6)} %copy.35.len_ref, bf16[384,1024]{1,0:T(8,128)(2,1)} %tok.3, f32[384,1024]{1,0:T(8,128)} %get-tuple-element.38.s2, ...), custom_call_target="tpu_custom_call" | custom-call | tf_op jit(solution)/shard_map/pallas_call | solution.py:1399
  307.3 0.0 copy-start
  307.3 1.5 copy.26
  308.7 1.5 slice_reduce_fusion
  310.2 0.0 copy-done.3
  310.2 0.9 copy.36
  311.1 0.0 copy-done
  311.1 1.1 copy.37
  312.3 0.0 copy-done.6
  312.3 0.7 copy.38
  313.0 0.0 copy-done.7
  313.0 0.7 copy.39
  313.7 0.8 copy.40
  314.5 0.0 copy-done.4
  314.5 0.8 copy.41
  315.3 1.0 copy.42
  316.3 1.0 copy.43
  (11 shorter events, 0.0 us)
Async XLA Ops:
  238.3 72.0 %copy-start.3 = (bf16[384,1024]{1,0:T(8,128)(2,1)S(1)}, bf16[384,1024]{1,0:T(8,128)(2,1)}, u32[]{:S(2)}) copy-start(bf16[384,1024]{1,0:T(8,128)(2,1)} %get-tuple-element.102) | copy-start | bytes 2359300
  307.3 3.9 %copy-start = (f32[384,1024]{1,0:T(8,128)S(1)}, f32[384,1024]{1,0:T(8,128)}, u32[]{:S(2)}) copy-start(f32[384,1024]{1,0:T(8,128)} %get-tuple-element.103) | copy-start | bytes 4718596
  310.2 2.0 copy-start.6
  311.1 1.9 copy-start.7
  311.1 2.6 copy-start.5
  311.1 3.4 %copy-start.4 = (f32[128,1024]{1,0:T(8,128)S(1)}, f32[128,1024]{1,0:T(8,128)}, u32[]{:S(2)}) copy-start(f32[128,1024]{1,0:T(8,128)} %get-tuple-element.108) | copy-start | bytes 1572868
  312.3 3.0 copy-start.2
  313.0 3.2 %copy-start.1 = (f32[256,1024]{1,0:T(8,128)S(1)}, f32[256,1024]{1,0:T(8,128)}, u32[]{:S(2)}) copy-start(f32[256,1024]{1,0:T(8,128)} %get-tuple-element.60) | copy-start | bytes 3145732

commit v4 on v3

--- a/solution.py
+++ b/solution.py
@@ -353,51 +353,51 @@
         i = w * 4 + j - 1
         return rcopy(block, dst, self.send.at[n, i], self.recv.at[n, i], to)
 
-    def ship(self, n):
+    def ship(self, n, ws=(0, 1)):
         @pl.when(self.mid)
         def _():
             for j in (3, 1):
-                for w in range(2):
+                for w in ws:
                     self.copy(n, w, j).start()
 
         @pl.when(jnp.logical_not(self.mid))
         def _():
             for j in (4, 2, 1):
-                for w in range(2):
+                for w in ws:
                     self.copy(n, w, j).start()
 
-    def transit(self, n):
+    def transit(self, n, ws=(0, 1)):
         @pl.when(self.mid)
         def _():
             k2 = self.P.zk[2]
-            for w in range(2):
+            for w in ws:
                 self.copy(n, w, 4).wait_recv()
                 self.src[w][n, k2] = self.src[w][n, k2] + self.via[w][n]
                 self.copy(n, w, 2).start()
 
-    def arrived(self, n):
-        for w in range(2):
+    def arrived(self, n, ws=(0, 1)):
+        for w in ws:
             self.copy(n, w, 1).wait_recv()
             self.copy(n, w, 2).wait_recv()
 
         @pl.when(self.mid)
         def _():
-            for w in range(2):
+            for w in ws:
                 self.copy(n, w, 3).wait_recv()
 
-    def sent(self, n):
-        for w in range(2):
+    def sent(self, n, ws=(0, 1)):
+        for w in ws:
             self.copy(n, w, 1).wait_send()
             self.copy(n, w, 2).wait_send()
 
         @pl.when(self.mid)
         def _():
-            for w in range(2):
+            for w in ws:
                 self.copy(n, w, 3).wait_send()
 
         @pl.when(jnp.logical_not(self.mid))
         def _():
-            for w in range(2):
+            for w in ws:
                 self.copy(n, w, 4).wait_send()
 
 
@@ -495,7 +495,6 @@
     out_b = gather(1, w_eout.at[1], lambda zs: wd_all.at[2, zs])
     in_a = gather(2, wi_all.at[1, z], lambda zs: wi_all.at[1, zs])
     in_b = gather(3, wi_all.at[2, z], lambda zs: wi_all.at[2, zs])
-    out_d = gather(4, w_down, lambda zs: wd_all.at[0, zs])
     mid = in_a.mid
 
     def z_copy(k, s, to):
@@ -617,7 +616,7 @@
 
     g_landed, g_pass = plane(gt, g_all, gs, gr)
     n_landed, n_pass = plane(nt, nt_all, ts, tr)
-    g_pass(d1, (3, d2), (4, sib))
+    g_pass(d1, (4, sib))
 
     allowed = masks(len_ref[0])
     lane = lax.broadcasted_iota(jnp.int32, (384, 128), 1)
@@ -643,7 +642,6 @@
         @pl.when(p == 4)
         def _():
             in_a.relay()
-            out_d.ship()
 
         return carry
 
@@ -660,17 +658,14 @@
     for i, p in enumerate((d1, d2, sib)):
         go(rcopy(nt, nt_all.at[t], ts.at[i], tr.at[t], P_.dev(p)))
     g_pass(d2, (5, sib))
-    g_pass(dd, (6, sib))
     in_b.relay()
-    n_pass(d1, (3, d2), (4, sib))
+    n_pass(d1, (4, sib))
     n_pass(d2, (5, sib))
-    out_d.relay()
-    n_pass(dd, (6, sib))
-    for p in (own, d1, d2, dd):
+    for p in (own, d1, d2):
         g_landed(P_.flip(p))
-    for p in (own, d2, d1, dd):
+    for p in (own, d2, d1):
         n_landed(P_.flip(p))
-    for part in (out_a, out_b, in_a, in_b, out_d):
+    for part in (out_a, out_b, in_a, in_b):
         part.finish()
     z_copy(1, b, 1).wait_send()
     z_copy(2, b, 2).wait_send()
@@ -709,7 +704,7 @@
             pltpu.VMEM((32, 32, PW), BF), pltpu.VMEM((8, 3, 32, 512), BF), pltpu.VMEM((400, 1024), BF),
             pltpu.VMEM((384, 3072), BF), pltpu.VMEM((384, 128), F32), pltpu.VMEM((384, 1024), BF),
             pltpu.VMEM((384, 1024), F32), pltpu.VMEM((384, 1024), BF), pltpu.VMEM((384, 1024), BF),
-            dma((4,)), dma((31,)), dma((32,)), dma((7,)), dma((8,)), dma((5, 4)), dma((5, 4)),
+            dma((4,)), dma((31,)), dma((32,)), dma((7,)), dma((8,)), dma((4, 4)), dma((4, 4)),
             dma((7,)), dma((8,)), dma((7,)), dma((8,)), dma((4,)), dma((12,)),
         ],
         compiler_params=pltpu.CompilerParams(
@@ -731,10 +726,10 @@
 
 
 def ff_kernel(
-    len_ref, nt_hbm, wmix, s2, g_all, wi_all, wd_all,
-    block, gsum, gl_out, gde, xe, dgi, dgd, r1, r2, rin, rdn, dwi,
+    nt_hbm, wmix, g_all, wi_all, wd_all,
+    gsum, gl_out, bnext, bown, eoi, eod, dgi, dgd, r1, r2, rin, rdn, dwi, dwd, gfar,
     nt_all, gbuf, br, gn, xb, yb, wi, wd, ai, ad, gin, gdn, tri, trd, tmp, gc, gcr, dots, gaps,
-    tr, gsem, wsem, dsem, zas, zar, zss, zsr, s1s, s1r, s2s, s2r, cs, cr, lsem, tsem,
+    ts, tr, gs, gr, gsem, wsem, dsem, zas, zar, zss, zsr, s1s, s1r, s2s, s2r, cs, cr, lsem, tsem,
 ):
     P_ = Place()
     z, t = P_.z, P_.t
@@ -747,13 +742,17 @@
         cp.start()
         sends.append(cp)
 
+    keeps = []
+
+    def keep(src, dst):
+        cp = pltpu.make_async_copy(src, dst, lsem.at[len(keeps)])
+        cp.start()
+        keeps.append(cp)
+
     dense = ZGather(
-        P_, (wi_all.at[0, z],), (lambda zs: dwi.at[zs],), zas, zar
+        P_, (wi_all.at[0, z], wd_all.at[0, z]), (lambda zs: dwi.at[zs], lambda zs: dwd.at[zs]), zas, zar
     )
     dense.ship()
-    s2_in = pltpu.make_async_copy(s2, gsum, lsem.at[3])
-    s2_in.start()
-
     expert_load = (
         pltpu.make_async_copy(wi_all.at[1], wi.at[0], wsem.at[0, 0]),
         pltpu.make_async_copy(wd_all.at[1], wd.at[0], wsem.at[0, 1]),
@@ -764,11 +763,12 @@
         cp.start()
 
     def dense_load():
-        copies = [pltpu.make_async_copy(wd_all.at[0], wd.at[0], dsem.at[4])]
+        copies = []
         for k in range(4):
             zz = P_.zk[k]
-            src = wi_all.at[0, z] if k == 0 else dwi.at[zz]
-            copies.append(pltpu.make_async_copy(src, wi.at[0, zz], dsem.at[k]))
+            for n, (full, far, dst) in enumerate(((wi_all, dwi, wi), (wd_all, dwd, wd))):
+                src = full.at[0, z] if k == 0 else far.at[zz]
+                copies.append(pltpu.make_async_copy(src, dst.at[0, zz], dsem.at[n, k]))
         return copies
 
     zsum = ZSum(P_, (gin, gdn), (rin, rdn), (tri, trd), zss, zsr)
@@ -782,8 +782,46 @@
             s = jnp.where(i == k, ranks[k], s)
         return s
 
+    r1st, rdd = P_.rank(d1), P_.rank(dd)
+    go(rcopy(nt_hbm.at[r1st], nt_all.at[r1st], ts.at[0], tr.at[r1st], P_.dev(d2)))
+    go(rcopy(g_all.at[r1st], gfar.at[0], gs.at[0], gr.at[0], P_.dev(d2)))
+
+    def far_on(start):
+        cps = (
+            rcopy(nt_all.at[rdd], nt_all.at[rdd], ts.at[1], tr.at[rdd], P_.dev(sib)),
+            rcopy(gfar.at[0], gfar.at[1], gs.at[1], gr.at[1], P_.dev(sib)),
+        )
+        for cp in cps:
+            if start:
+                cp.start()
+            else:
+                cp.wait_send()
+
+    def far_here(s, k):
+        rcopy(gfar.at[0], gfar.at[k], gs.at[0], gr.at[k], P_.dev(sib)).wait_recv()
+        rcopy(tmp.at[0], nt_all.at[s], ts.at[0], tr.at[s], P_.dev(sib)).wait_recv()
+
+    class GCopy:
+        def __init__(self, i):
+            self.i = i
+
+        def make(self, src):
+            return pltpu.make_async_copy(src, gbuf.at[self.i % 2], gsem.at[self.i % 2])
+
+        def start(self):
+            @pl.when(self.i < 6)
+            def _():
+                self.make(g_all.at[seq_at(self.i)]).start()
+
+            @pl.when(self.i >= 6)
+            def _():
+                self.make(gfar.at[jnp.maximum(self.i - 6, 0)]).start()
+
+        def wait(self):
+            self.make(g_all.at[0]).wait()
+
     def g_copy(i):
-        return pltpu.make_async_copy(g_all.at[seq_at(i)], gbuf.at[i % 2], gsem.at[i % 2])
+        return GCopy(i)
 
     def ff(xv, gv, k):
         wiv = wi[k].reshape(1024, 512)
@@ -804,7 +842,7 @@
     def n_copy(s):
         return pltpu.make_async_copy(nt_hbm.at[s], nt_all.at[s], tr.at[s])
 
-    for s in ranks:
+    for s in ranks[:6]:
         n_copy(s).start()
     g_copy(0).start()
     ai[...] = jnp.zeros_like(ai)
@@ -815,11 +853,23 @@
     def arrive(i, carry):
         s = seq_at(i)
 
+        @pl.when(i == 5)
+        def _():
+            far_here(rdd, 0)
+            far_on(True)
+
+        @pl.when(i == 6)
+        def _():
+            far_here(P_.rank(P_.flip(dd)), 1)
+
         @pl.when(i + 1 < 8)
         def _():
             g_copy(i + 1).start()
 
-        n_copy(s).wait()
+        @pl.when(i < 6)
+        def _():
+            n_copy(s).wait()
+
         g_copy(i).wait()
         xv = nt_all[s]
         gv = gbuf[i % 2, :384]
@@ -852,21 +902,23 @@
         gin[e] = ai[e].astype(BF).reshape(4, 256, 512)
         gdn[e] = ad[e].astype(BF).reshape(4, 128, 1024)
         zsum.ship(e)
+        keep(gin.at[e, z], eoi.at[e])
+        keep(gdn.at[e, z], eod.at[e])
 
     def half(b, carry):
         lax.fori_loop(b * 4, b * 4 + 4, arrive, 0)
+        @pl.when(b == 1)
+        def _():
+            dense.relay()
+
         expert(b, 0)
-        return carry
-
-    def half_two(b, carry):
         expert(b, 1)
         return carry
 
     lax.fori_loop(0, 2, half, 0)
     stage(0)
-    dense.relay()
-    lax.fori_loop(0, 2, half_two, 0)
     stage(1)
+    far_on(False)
     g_copy(7).start()
     dense.finish()
     for cp in dense_load():
@@ -959,7 +1011,8 @@
 
         def turn(w):
             load2(0, d1, w, False)
-            give2(1, 1, d1, w).start()
+            if w == 0:
+                give2(1, 1, d1, w).start()
 
         at_step(k, 5, turn)
         at_step(k, 7, lambda w: load1(3, w, False))
@@ -977,22 +1030,13 @@
     lax.fori_loop(0, 8, dense_step, 0)
     for i, p in enumerate(others):
         go(rcopy(gc.at[P_.rank(p)], gcr.at[t], cs.at[i], cr.at[t], P_.dev(p)))
-    o0 = pltpu.make_async_copy(ai.at[0], dgi, lsem.at[0])
-    o1 = pltpu.make_async_copy(ad.at[0], dgd, lsem.at[1])
-    o0.start()
-    o1.start()
+    keep(br.at[P_.rank(d1)], bnext)
     for w in range(2):
         load2(2, own, w, True)
     for w in range(2):
         load2(2, own, w, False)
-    for w in range(2):
-        load2(1, own, w, True)
-        load2(1, own, w, False)
-    s2_in.wait()
-    branch = br[t].astype(F32)
-    keep = (lax.broadcasted_iota(jnp.int32, (384, 1), 0) < len_ref[0]).astype(F32)
-    block[...] = ((gsum[...] + branch) * keep).astype(BF)
-    gsum[...] = gn[t].astype(F32)
+    keep(br.at[t], bown)
+    load2(1, own, 0, True)
     for p in others:
         r = P_.rank(p)
         rcopy(gc.at[0], gcr.at[r], cs.at[0], cr.at[r], P_.dev(sib)).wait_recv()
@@ -1002,77 +1046,45 @@
     q1 = jnp.transpose(jnp.broadcast_to(tot[8:9], (128, 384)))
     m0, m1 = mix_of(jnp.transpose(jnp.broadcast_to(gaps[0][0:1], (128, 384))))
     gl_out[...] = m0 * (m1 * gc0 - q1)
-
-    mids = zsum.mid
-
-    def third(e):
-        return (
-            pltpu.make_async_copy(rin.at[e, 2], nt_all.at[2, 0:256, 0:512], lsem.at[4]),
-            pltpu.make_async_copy(rdn.at[e, 2], nt_all.at[3, 0:128], lsem.at[5]),
-        )
-
-    for e in range(2):
-        zsum.arrived(e)
-        loads = (
-            (rin.at[e, 0], nt_all.at[0, 0:256, 0:512]), (rin.at[e, 1], nt_all.at[0, 0:256, 512:1024]),
-            (rdn.at[e, 0], nt_all.at[1, 0:128]), (rdn.at[e, 1], nt_all.at[1, 128:256]),
-        )
-        loads = [pltpu.make_async_copy(u, v, lsem.at[6 + n]) for n, (u, v) in enumerate(loads)]
-
-        @pl.when(mids)
-        def _():
-            for cp in third(e):
-                cp.start()
-
-        for cp in loads:
-            cp.start()
-        for cp in loads:
-            cp.wait()
-        two = nt_all[0, 0:256]
-        ai[1, 0:256] = gin[e, z].astype(F32) + two[:, 0:512].astype(F32) + two[:, 512:1024].astype(F32)
-        at = slice(e * 128, (e + 1) * 128)
-        ad[1, at] = gdn[e, z].astype(F32) + nt_all[1, 0:128].astype(F32) + nt_all[1, 128:256].astype(F32)
-
-        @pl.when(mids)
-        def _():
-            for cp in third(e):
-                cp.wait()
-            ai[1, 0:256] += nt_all[2, 0:256, 0:512].astype(F32)
-            ad[1, at] += nt_all[3, 0:128].astype(F32)
-
-        gin[e, z] = ai[1, 0:256].astype(BF)
-    o2 = pltpu.make_async_copy(gin.at[:, z], xe, lsem.at[2])
-    o3 = pltpu.make_async_copy(ad.at[1, 0:256], gde, lsem.at[3])
-    o2.start()
-    o3.start()
+    load2(1, own, 0, False)
+    gsum[...] = gn[t].astype(F32)
+    zsum.sent(0)
+    for cp in keeps[0:2]:
+        cp.wait()
+    gin[0] = ai[0].astype(BF).reshape(4, 256, 512)
+    gdn[0] = ad[0].astype(BF).reshape(4, 128, 1024)
+    keep(gin.at[0], dgi)
+    keep(gdn.at[0], dgd)
     for w in range(2):
         for q in range(4):
             give1(q, w).wait_send()
         give2(0, 0, d2, w).wait_send()
-        give2(1, 1, d1, w).wait_send()
         give2(2, 2, d2, w).wait_send()
-    for e in range(2):
-        zsum.sent(e)
-    for cp in (o0, o1, o2, o3):
+    give2(1, 1, d1, 0).wait_send()
+    zsum.arrived(0)
+    zsum.arrived(1)
+    zsum.sent(1)
+    for cp in keeps[2:]:
         cp.wait()
     for cp in sends:
         cp.wait_send()
 
 
-def run_ff(lengths, nt, wmix, s2, g_all, wi_all, wd_all):
+def run_ff(*args):
     sd = jax.ShapeDtypeStruct
     dma = pltpu.SemaphoreType.DMA
     out = pl.pallas_call(
         ff_kernel,
         out_shape=(
-            sd((384, 1024), BF), sd((384, 1024), F32), sd((384, 128), F32),
-            sd((256, 1024), F32), sd((2, 256, 512), BF), sd((1024, 512), F32), sd((512, 1024), F32),
+            sd((384, 1024), F32), sd((384, 128), F32), sd((384, 1024), BF), sd((384, 1024), BF),
+            sd((2, 256, 512), BF), sd((2, 128, 1024), BF),
+            sd((4, 256, 512), BF), sd((4, 128, 1024), BF),
             sd((2, 4, 384, 1024), BF), sd((2, 3, 384, 1024), BF),
             sd((2, 3, 256, 512), BF), sd((2, 3, 128, 1024), BF),
-            sd((4, 256, 512), BF),
+            sd((4, 256, 512), BF), sd((4, 128, 1024), BF), sd((2, 400, 1024), BF),
         ),
-        in_specs=[SM, ANY, VM, ANY, ANY, ANY, ANY],
-        out_specs=(VM,) * 3 + (ANY,) * 9,
+        in_specs=[ANY, VM, ANY, ANY, ANY],
+        out_specs=(VM,) * 2 + (ANY,) * 13,
         scratch_shapes=[
             pltpu.VMEM((8, 384, 1024), BF), pltpu.VMEM((2, 400, 1024), BF),
             pltpu.VMEM((8, 384, 1024), BF), pltpu.VMEM((8, 384, 1024), BF),
@@ -1084,14 +1096,15 @@
             pltpu.VMEM((2, 384, 1024), BF),
             pltpu.VMEM((8, 16, 384), F32), pltpu.VMEM((8, 16, 384), F32), pltpu.VMEM((8, 2, 112, 128), BF),
             pltpu.VMEM((8, 8, 384), F32),
-            dma((8,)), dma((2,)), dma((2, 2)), dma((5,)), dma((4,)), dma((4,)), dma((2, 8)), dma((2, 8)),
+            dma((2,)), dma((8,)), dma((2,)), dma((2,)), dma((2,)), dma((2, 2)), dma((2, 4)), dma((8,)), dma((8,)),
+            dma((2, 8)), dma((2, 8)),
             dma((2, 4)), dma((2, 4)), dma((2, 3)), dma((2, 3)), dma((7,)), dma((8,)), dma((10,)), dma((2,)),
         ],
         compiler_params=pltpu.CompilerParams(
             collective_id=1, has_side_effects=True, vmem_limit_bytes=63 * MIB
         ),
-    )(lengths, nt, wmix, s2, g_all, wi_all, wd_all)
-    return out[:7]
+    )(*args)
+    return (*out[:8], out[10], out[11])
 
 
 class RowSum:
@@ -1182,31 +1195,37 @@
 
 
 def back_kernel(
-    len_ref, tok, s2, n1, qkv, lse, att, gsum, gl, g_all, nt_all, pack_all, dgi, dgd, xe,
-    gtok, gqkv, gwo, gex, gdd, gwi, gwe,
-    gx, gt, nt,
+    len_ref, tok, s2, n1, qkv, lse, att, gsum, gl, g_all, nt_all, pack_all,
+    bnext, bown, eoi, eod, dgi, dgd, ein, edr,
+    block, gtok, gqkv, gwo, gex, gdd, gde, gwi, gwe,
+    gx, gt, nt, bin_, xe, er, ed, eo,
     pack_v, gq, gacc, n1t, ga_, gb_, gc_, ra1, ra2, ra3, rb1, rb2, rb3, rc1, rc2, rc3,
-    di, dj, gin, gdn, rin, rdn, tri, trd, *sems,
+    gin, gdn, rin, rdn, tri, trd, *sems,
 ):
     P_ = Place()
     z, t = P_.z, P_.t
     own, sib, d1, d2, dd = P_.own, P_.sib, P_.d1, P_.d2, P_.dd
     others = P_.plane_others()
-    zss, zsr, xs, xr, lsem = sems[18:]
+    zss, zsr, xs, xr, bs, lsem = sems[18:]
     sum_a = RowSum(P_, ga_, ra1, ra2, ra3, sems[0:6])
     sum_b = RowSum(P_, gb_, rb1, rb2, rb3, sems[6:12])
     sum_c = RowSum(P_, gc_, rc1, rc2, rc3, sems[12:18])
     lw = pltpu.make_async_copy(pack_all, pack_v, lsem.at[0])
-    li = pltpu.make_async_copy(dgi, di, lsem.at[1])
-    lj = pltpu.make_async_copy(dgd, dj, lsem.at[2])
-    li.start()
-    lj.start()
-    lw.start()
+    z_in = (
+        pltpu.make_async_copy(dgi, gin.at[0], lsem.at[2]),
+        pltpu.make_async_copy(dgd, gdn.at[0], lsem.at[7]),
+    )
     own_in = (
         pltpu.make_async_copy(g_all.at[t], gt, lsem.at[5]),
         pltpu.make_async_copy(nt_all.at[t], nt, lsem.at[6]),
     )
-    for cp in own_in:
+    e_in = (
+        pltpu.make_async_copy(eoi, xe, lsem.at[8]),
+        pltpu.make_async_copy(ein, er, lsem.at[9]),
+        pltpu.make_async_copy(eod, eo, lsem.at[10]),
+        pltpu.make_async_copy(edr, ed, lsem.at[11]),
+    )
+    for cp in (*z_in, lw, *own_in, *e_in):
         cp.start()
     meet([P_.dev(p) for p in others] + [P_.dev(own, zz) for zz in P_.zk[1:]])
     sends = []
@@ -1219,15 +1238,10 @@
         return pl.ds(pl.multiple_of(P_.rank(p) * 32, 32), 32)
 
     zsum = ZSum(P_, (gin, gdn), (rin, rdn), (tri, trd), zss, zsr)
-    li.wait()
-    lj.wait()
-    gin[0] = di[...].astype(BF).reshape(4, 256, 512)
-    gdn[0] = dj[...].astype(BF).reshape(4, 128, 1024)
+    for cp in z_in:
+        cp.wait()
     zsum.ship(0)
-    le = pltpu.make_async_copy(xe.at[:, rows(own)], gx.at[t, 1:3], lsem.at[3])
-    le.start()
-    for i, p in enumerate(others):
-        go(rcopy(xe.at[:, rows(p)], gx.at[t, 1:3], xs.at[i], xr.at[t, 0], P_.dev(p)))
+    go(rcopy(bnext, bin_, bs.at[0], bs.at[1], P_.dev(d1)))
 
     lw.wait()
     for cp in own_in:
@@ -1257,6 +1271,18 @@
         cols = slice(j * 512, (j + 1) * 512)
         put(ga_, 0, cols, dot_tn(att[...], ga[:, cols]))
     sum_a.step1(0)
+    for cp in e_in:
+        cp.wait()
+    mid = zsum.mid
+    for e in range(2):
+        total = xe[e].astype(F32) + er[e, 0].astype(F32) + er[e, 1].astype(F32)
+        xe[e] = (total + jnp.where(mid, er[e, 2].astype(F32), 0.0)).astype(BF)
+        total = eo[e].astype(F32) + ed[e, 0].astype(F32) + ed[e, 1].astype(F32)
+        gde[e] = total + jnp.where(mid, ed[e, 2].astype(F32), 0.0)
+    le = pltpu.make_async_copy(xe.at[:, rows(own)], gx.at[t, 1:3], lsem.at[3])
+    le.start()
+    for i, p in enumerate(others):
+        go(rcopy(xe.at[:, rows(p)], gx.at[t, 1:3], xs.at[i], xr.at[t, 0], P_.dev(p)))
     gatt = dot_nt(ga[:, 0:512], pack_v[:, :, WO : WO + 512].reshape(1024, 512))
     gatt += dot_nt(ga[:, 512:1024], pack_v[:, :, WO + 512 : WO + 1024].reshape(1024, 512))
     gq[:, 0:1024] = gatt.astype(BF)
@@ -1339,15 +1365,15 @@
     sum_c.step3(0)
 
     zsum.arrived(0)
-    di[0:256] = gin[0, z].astype(F32) + rin[0, 0].astype(F32) + rin[0, 1].astype(F32)
+    gacc[0:256, 0:512] = gin[0, z].astype(F32) + rin[0, 0].astype(F32) + rin[0, 1].astype(F32)
     gdd[...] = gdn[0, z].astype(F32) + rdn[0, 0].astype(F32) + rdn[0, 1].astype(F32)
 
-    @pl.when(zsum.mid)
+    @pl.when(mid)
     def _():
-        di[0:256] += rin[0, 2].astype(F32)
+        gacc[0:256, 0:512] += rin[0, 2].astype(F32)
         gdd[...] += rdn[0, 2].astype(F32)
 
-    gin[0, z] = di[0:256].astype(BF)
+    gin[0, z] = gacc[0:256, 0:512].astype(BF)
     lx = pltpu.make_async_copy(gin.at[:, z, rows(own)], gx.at[t, 0:1], lsem.at[4])
     lx.start()
     for i, p in enumerate(others):
@@ -1356,6 +1382,12 @@
     sum_b.step4(2)
     sum_b.step4(3)
     sum_c.step4(0)
+    rcopy(bnext, bin_, bs.at[0], bs.at[1], P_.dev(sib)).wait_recv()
+    b_in = pltpu.make_async_copy(bown, nt, lsem.at[6])
+    b_in.start()
+    b_in.wait()
+    keep = (lax.broadcasted_iota(jnp.int32, (384, 1), 0) < len_ref[0]).astype(F32)
+    block[...] = ((s2[...] + (nt[...].astype(F32) + bin_[...].astype(F32))) * keep).astype(BF)
     gwo[...] = sum_a.step5(0)
     for j in range(4):
         total = sum_b.step5(j)
@@ -1391,33 +1423,67 @@
     blocks = [pltpu.VMEM((n, 8, 4, 32, w), BF) for n, w in sizes]
     for n, w in sizes:
         blocks += [
-            pltpu.VMEM((n, 4, 4, 32, w), BF), pltpu.VMEM((n, 3, 4, 32, w), BF), pltpu.VMEM((n, 3, 32, w), BF),
+            pltpu.VMEM((n, 4, 4, 32, w), BF), pltpu.VMEM((n, 3, 4, 32, w), BF), pltpu.VMEM((n, 4, 32, w), BF),
         ]
     sems = []
     for n, _ in sizes:
-        sems += [dma((n, 4)), dma((n, 4)), dma((n, 3)), dma((n, 3)), dma((n, 3)), dma((n, 3))]
+        sems += [dma((n, 4)), dma((n, 4)), dma((n, 3)), dma((n, 3)), dma((n, 4)), dma((n, 4))]
     return pl.pallas_call(
         back_kernel,
         out_shape=(
-            sd((384, 1024), F32), sd((32, 3072), F32), sd((32, 1024), F32), sd((32, 128), F32),
-            sd((128, 1024), F32), sd((32, 4096), F32), sd((2, 32, 4096), F32),
+            sd((384, 1024), BF), sd((384, 1024), F32), sd((32, 3072), F32), sd((32, 1024), F32),
+            sd((32, 128), F32), sd((128, 1024), F32), sd((2, 128, 1024), F32), sd((32, 4096), F32),
+            sd((2, 32, 4096), F32),
         ),
-        in_specs=[SM] + [VM] * 8 + [ANY] * 6,
-        out_specs=(VM,) * 7,
+        in_specs=[SM] + [VM] * 8 + [ANY] * 11,
+        out_specs=(VM,) * 9,
         scratch_shapes=[
             pltpu.VMEM((8, 3, 32, 512), BF), pltpu.VMEM((400, 1024), BF), pltpu.VMEM((384, 1024), BF),
+            pltpu.VMEM((384, 1024), BF), pltpu.VMEM((2, 256, 512), BF), pltpu.VMEM((2, 3, 256, 512), BF),
+            pltpu.VMEM((2, 3, 128, 1024), BF), pltpu.VMEM((2, 128, 1024), BF),
             pltpu.VMEM((32, 32, PW), BF), pltpu.VMEM((384, 3072), BF), pltpu.VMEM((384, 1024), F32),
             pltpu.VMEM((1024, 384), BF), *blocks,
-            pltpu.VMEM((1024, 512), F32), pltpu.VMEM((512, 1024), F32),
             pltpu.VMEM((1, 4, 256, 512), BF), pltpu.VMEM((1, 4, 128, 1024), BF),
             pltpu.VMEM((1, 3, 256, 512), BF), pltpu.VMEM((1, 3, 128, 1024), BF),
             pltpu.VMEM((1, 256, 512), BF), pltpu.VMEM((1, 128, 1024), BF),
-            *sems, dma((1, 8)), dma((1, 8)), dma((14,)), dma((8, 2)), dma((7,)),
+            *sems, dma((1, 8)), dma((1, 8)), dma((14,)), dma((8, 2)), dma((2,)),
+            dma((12,)),
         ],
         compiler_params=pltpu.CompilerParams(
             collective_id=2, has_side_effects=True, vmem_limit_bytes=63 * MIB
         ),
     )(*args)
+
+
+def leave_kernel(*refs):
+    n = 8
+    srcs, gex, dsts, rows = refs[:n], refs[n], refs[n + 1 : 2 * n + 1], refs[2 * n + 1]
+    bufs, sin, sout = refs[2 * n + 2 : 3 * n + 2], refs[3 * n + 2], refs[3 * n + 3]
+    ins = [pltpu.make_async_copy(s, v, sin.at[i]) for i, (s, v) in enumerate(zip(srcs, bufs))]
+    outs = [pltpu.make_async_copy(v, d, sout.at[i]) for i, (v, d) in enumerate(zip(bufs, dsts))]
+    for cp in ins:
+        cp.start()
+    rows[...] = jnp.transpose(jnp.concatenate([gex[...]] * 4, axis=0))[0:8]
+    for a, b in zip(ins, outs):
+        a.wait()
+        b.start()
+    for cp in outs:
+        cp.wait()
+
+
+def run_leave(arrays, gex):
+    shapes = [jax.ShapeDtypeStruct(a.shape, a.dtype) for a in arrays]
+    return pl.pallas_call(
+        leave_kernel,
+        out_shape=(*shapes, jax.ShapeDtypeStruct((8, 128), F32)),
+        in_specs=[ANY] * 8 + [VM],
+        out_specs=(ANY,) * 8 + (VM,),
+        scratch_shapes=[
+            *(pltpu.VMEM(a.shape, a.dtype) for a in arrays),
+            pltpu.SemaphoreType.DMA((8,)), pltpu.SemaphoreType.DMA((8,)),
+        ],
+        compiler_params=pltpu.CompilerParams(vmem_limit_bytes=63 * MIB),
+    )(*arrays, gex)
 
 
 def fused_device(
@@ -1433,14 +1499,14 @@
         lengths, tokens, cotangent, table.reshape(1, 384),
         w_qkv, w_out, small, w_in, w_expert_in, w_down, w_expert_out,
     )
-    block, gsum, gl, gde, xe, dgi, dgd = run_ff(
-        lengths, nt_all, wmix.reshape(1024, 128), s2, g_all, wi_all, wd_all
-    )
-    gtok, gqkv, gwo, gex, gdd, gwi, gwe = run_back(
-        lengths, tokens, s2, n1, qkv, lse, att, gsum, gl, g_all, nt_all, pack_all, dgi, dgd, xe
-    )
+    gsum, gl, *rest = run_ff(nt_all, wmix.reshape(1024, 128), g_all, wi_all, wd_all)
+    block, gtok, gqkv, gwo, gex, gdd, gde, gwi, gwe = run_back(
+        lengths, tokens, s2, n1, qkv, lse, att, gsum, gl, g_all, nt_all, pack_all, *rest
+    )
+    *big, rows = run_leave((block, gtok, gqkv, gwo, gwi, gdd, gwe, gde), gex)
+    block, gtok, gqkv, gwo, gwi, gdd, gwe, gde = big
     return (
-        block, gtok, gqkv, gwo, gex[:, 2], gwi, gdd, gwe, gde.reshape(2, 128, 1024), gex[:, 0:2], gex[:, 3],
+        block, gtok, gqkv, gwo, rows[2, 0:32], gwi, gdd, gwe, gde, rows[0:2, 0:32].T, rows[3, 0:32],
     )
 
 

time: 318 us -> 304 us (0.956)
  local copies, waits for them, and re-layouts: 11.3 us -> 3.81 us
  Pallas kernels: 303 us -> 297 us
    pallas_call x1, Pallas kernels: 119 us -> 108 us  [run_enter(): pl.pallas_call(enter_kernel, out_shape=(sd((384, 3072), BF), sd((384, 128...]
    unnamed x25 -> x0, local copies, waits for them, and re-layouts: 8.45 us -> none
    pallas_call x2 -> x3, Pallas kernels: 184 us -> 188 us  [the longest x1 109 us: run_ff(): pl.pallas_call(ff_kernel, out_shape=(sd((384, 1024), F32), sd((384, 128),...]
where the time goes in v4:
time: 304 us
  Pallas kernels  297 us (98%)
  local copies, waits for them, and re-layouts  3.81 us (1%)
    pallas_call x1, Pallas kernels, run_ff(): pl.pallas_call(ff_kernel, out_shape=(sd((384, 1024), F32), sd((384, 128),...  109 us
    pallas_call x1, Pallas kernels, run_enter(): pl.pallas_call(enter_kernel, out_shape=(sd((384, 3072), BF), sd((384, 128...  108 us
    pallas_call x1, Pallas kernels, run_back(): pl.pallas_call(back_kernel, out_shape=(sd((384, 1024), BF), sd((384, 1024...  72.9 us
    pallas_call x1, Pallas kernels, run_leave(): pl.pallas_call(leave_kernel, out_shape=(*shapes, jax.ShapeDtypeStruct((8,...  6.47 us

profile of v4, /device:TPU:0, one launch (start us, length us, event | category | flops | bytes accessed | tf_op | source)
XLA Modules:
  0.0 303.8 jit_solution(10146906538620895681)
XLA Ops:
  1.3 0.7 slice_bitcast_fusion.4
  2.0 0.7 select_convert_fusion
  2.7 0.6 reshape.50.tab
  3.3 1.4 select_select_fusion.small
  4.7 108.5 %shard_map.221 = (bf16[384,3072]{1,0:T(8,128)(2,1)}, f32[384,128]{1,0:T(8,128)}, bf16[384,1024]{1,0:T(8,128)(2,1)}, f32[384,1024]{1,0:T(8,128)}, bf16[384,1024]{...) custom-call(s32[1]{0:T(128)S(6)} %copy.25.len_ref, ...), custom_call_target="tpu_custom_call" | custom-call | tf_op jit(solution)/shard_map/pallas_call | solution.py:693
  113.1 108.8 %shard_map.222 = (f32[384,1024]{1,0:T(8,128)}, f32[384,128]{1,0:T(8,128)}, bf16[384,1024]{1,0:T(8,128)(2,1)}, bf16[384,1024]{1,0:T(8,128)(2,1)}, bf16[2,256,512]...) custom-call(bf16[8,384,1024]{2,1,0:T(8,128)(2,1)} %get-tuple-element, ...), custom_call_target="tpu_custom_call" | custom-call | tf_op jit(solution)/shard_map/pallas_call | solution.py:1076
  222.0 72.9 %shard_map.223 = (bf16[384,1024]{1,0:T(8,128)(2,1)}, f32[384,1024]{1,0:T(8,128)}, f32[32,3072]{1,0:T(8,128)}, f32[32,1024]{1,0:T(8,128)}, f32[32,128]{1,0:T(8,12...) custom-call(s32[1]{0:T(128)S(6)} %copy.25.len_ref, ...), custom_call_target="tpu_custom_call" | custom-call | tf_op jit(solution)/shard_map/pallas_call | solution.py:1431
  294.8 6.5 %shard_map.224 = (bf16[384,1024]{1,0:T(8,128)(2,1)}, f32[384,1024]{1,0:T(8,128)}, f32[32,3072]{1,0:T(8,128)}, f32[32,1024]{1,0:T(8,128)}, f32[32,4096]{1,0:T(8,1...) custom-call(bf16[384,1024]{1,0:T(8,128)(2,1)} %get-tuple-element.71.refs_0_, ...), custom_call_target="tpu_custom_call" | custom-call | tf_op jit(solution)/shard_map/pallas_call | solution.py:1476
  301.3 1.2 slice_bitcast_fusion
  302.5 1.3 slice_bitcast_fusion.1
  (2 shorter events, 0.0 us)

commit v5 on v4

--- a/solution.py
+++ b/solution.py
@@ -563,10 +563,6 @@
                 ).wait_recv()
             out_a.relay()
             in_a.ship()
-        if k == 4:
-            store(gt, g_all.at[t])
-            for i, p in enumerate((d1, d2, sib)):
-                go(rcopy(gt, g_all.at[t], gs.at[i], gr.at[t], P_.dev(p)))
         if 1 <= k <= 4:
             s = slot(k - 1, d1)
             landed(s)
@@ -579,12 +575,14 @@
             s = slot(k - 2, dd)
             landed(s)
             fwd(s, 27 + k - 2, sib)
-    out_b.relay()
     in_b.ship()
     stream = tok[...].astype(F32)
     for k in range(4):
         for p in (own, d1, d2, dd):
             landed(slot(k, P_.flip(p)))
+    store(gt, g_all.at[t])
+    for i, p in enumerate((d1, d2, sib)):
+        go(rcopy(gt, g_all.at[t], gs.at[i], gr.at[t], P_.dev(p)))
     store(pack_v, pack_all)
     store(pack_v.at[:, :, EX : EX + 128], wmix_o)
 
@@ -616,7 +614,6 @@
 
     g_landed, g_pass = plane(gt, g_all, gs, gr)
     n_landed, n_pass = plane(nt, nt_all, ts, tr)
-    g_pass(d1, (4, sib))
 
     allowed = masks(len_ref[0])
     lane = lax.broadcasted_iota(jnp.int32, (384, 128), 1)
@@ -638,11 +635,6 @@
         att[:, pl.ds(pl.multiple_of(p * 128, 128), 128)] = jnp.where(
             lane < 64, outs[0], outs[1]
         ).astype(BF)
-
-        @pl.when(p == 4)
-        def _():
-            in_a.relay()
-
         return carry
 
     lax.fori_loop(0, 8, pair_step, 0)
@@ -657,6 +649,9 @@
     store(nt, nt_all.at[t])
     for i, p in enumerate((d1, d2, sib)):
         go(rcopy(nt, nt_all.at[t], ts.at[i], tr.at[t], P_.dev(p)))
+    out_b.relay()
+    in_a.relay()
+    g_pass(d1, (4, sib))
     g_pass(d2, (5, sib))
     in_b.relay()
     n_pass(d1, (4, sib))

time: 304 us -> 295 us (0.970)
  Pallas kernels: 297 us -> 287 us
    pallas_call x1, Pallas kernels: 108 us -> 98.6 us  [run_enter(): pl.pallas_call(enter_kernel, out_shape=(sd((384, 3072), BF), sd((384, 128...]
where the time goes in v5:
time: 295 us; the launch traced here: 294 us
  Pallas kernels  287 us (97%)
  local copies, waits for them, and re-layouts  3.81 us (1%)
    pallas_call x1, Pallas kernels, run_ff(): pl.pallas_call(ff_kernel, out_shape=(sd((384, 1024), F32), sd((384, 128),...  108 us
    pallas_call x1, Pallas kernels, run_enter(): pl.pallas_call(enter_kernel, out_shape=(sd((384, 3072), BF), sd((384, 128...  98.6 us
    pallas_call x1, Pallas kernels, run_back(): pl.pallas_call(back_kernel, out_shape=(sd((384, 1024), BF), sd((384, 1024...  73.8 us
    pallas_call x1, Pallas kernels, run_leave(): pl.pallas_call(leave_kernel, out_shape=(*shapes, jax.ShapeDtypeStruct((8,...  6.47 us

profile of v5, /device:TPU:0, one launch (start us, length us, event | category | flops | bytes accessed | tf_op | source)
XLA Modules:
  0.0 293.9 jit_solution(7799499564563916062)
XLA Ops:
  1.3 0.7 slice_bitcast_fusion.4
  2.0 0.7 select_convert_fusion
  2.7 0.6 reshape.50.tab
  3.3 1.4 select_select_fusion.small
  4.7 98.6 %shard_map.221 = (bf16[384,3072]{1,0:T(8,128)(2,1)}, f32[384,128]{1,0:T(8,128)}, bf16[384,1024]{1,0:T(8,128)(2,1)}, f32[384,1024]{1,0:T(8,128)}, bf16[384,1024]{...) custom-call(s32[1]{0:T(128)S(6)} %copy.25.len_ref, ...), custom_call_target="tpu_custom_call" | custom-call | tf_op jit(solution)/shard_map/pallas_call | solution.py:688
  103.2 107.8 %shard_map.222 = (f32[384,1024]{1,0:T(8,128)}, f32[384,128]{1,0:T(8,128)}, bf16[384,1024]{1,0:T(8,128)(2,1)}, bf16[384,1024]{1,0:T(8,128)(2,1)}, bf16[2,256,512]...) custom-call(bf16[8,384,1024]{2,1,0:T(8,128)(2,1)} %get-tuple-element, ...), custom_call_target="tpu_custom_call" | custom-call | tf_op jit(solution)/shard_map/pallas_call | solution.py:1071
  211.1 73.8 %shard_map.223 = (bf16[384,1024]{1,0:T(8,128)(2,1)}, f32[384,1024]{1,0:T(8,128)}, f32[32,3072]{1,0:T(8,128)}, f32[32,1024]{1,0:T(8,128)}, f32[32,128]{1,0:T(8,12...) custom-call(s32[1]{0:T(128)S(6)} %copy.25.len_ref, ...), custom_call_target="tpu_custom_call" | custom-call | tf_op jit(solution)/shard_map/pallas_call | solution.py:1426
  284.9 6.5 %shard_map.224 = (bf16[384,1024]{1,0:T(8,128)(2,1)}, f32[384,1024]{1,0:T(8,128)}, f32[32,3072]{1,0:T(8,128)}, f32[32,1024]{1,0:T(8,128)}, f32[32,4096]{1,0:T(8,1...) custom-call(bf16[384,1024]{1,0:T(8,128)(2,1)} %get-tuple-element.71.refs_0_, ...), custom_call_target="tpu_custom_call" | custom-call | tf_op jit(solution)/shard_map/pallas_call | solution.py:1471
  291.4 1.2 slice_bitcast_fusion
  292.6 1.3 slice_bitcast_fusion.1
  (2 shorter events, 0.0 us)

commit v6 on v5

--- a/solution.py
+++ b/solution.py
@@ -473,7 +473,10 @@
     others = P_.plane_others()
     pack = pack_v.at[b]
     pack_v[b, :, 0:3072] = w_qkv[...]
-    pack_v[b, :, EX : EX + 128] = small[...]
+    pick = (
+        lax.broadcasted_iota(jnp.int32, (4, 128), 1) == lax.broadcasted_iota(jnp.int32, (4, 128), 0)
+    ).astype(BF)
+    pack_v[b, :, EX : EX + 128] = dot_tn(small[...], pick).astype(BF)
     pack_v[b, :, WO : WO + 1024] = w_out[...]
     meet([P_.dev(p) for p in others] + [P_.dev(own, zz) for zz in P_.zk[1:]])
     sends = []
@@ -1486,10 +1489,7 @@
     w_expert_in, w_expert_out, w_mix, gain_two,
 ):
     table = jnp.where(slot_ids >= 0, expert_ids * CAP + slot_ids, -1).astype(F32)
-    lane = jnp.arange(128, dtype=jnp.int32)[None, :]
-    small = jnp.zeros((32, 128), BF)
-    for k, col in enumerate((w_mix[:, 0], w_mix[:, 1], gain_one, gain_two)):
-        small = jnp.where(lane == k, col[:, None], small)
+    small = jnp.concatenate([w_mix.T, gain_one[None], gain_two[None]], axis=0)
     qkv, lse, att, s2, n1, wmix, pack_all, wi_all, wd_all, g_all, nt_all = run_enter(
         lengths, tokens, cotangent, table.reshape(1, 384),
         w_qkv, w_out, small, w_in, w_expert_in, w_down, w_expert_out,

time: 295 us -> 294 us (level)
  no operation moved by 1% of the time
where the time goes in v6:
time: 294 us; the launch traced here: 293 us
  Pallas kernels  287 us (98%)
  local copies, waits for them, and re-layouts  3.08 us (1%)
    pallas_call x1, Pallas kernels, run_ff(): pl.pallas_call(ff_kernel, out_shape=(sd((384, 1024), F32), sd((384, 128),...  108 us
    pallas_call x1, Pallas kernels, run_enter(): pl.pallas_call(enter_kernel, out_shape=(sd((384, 3072), BF), sd((384, 128...  98.7 us
    pallas_call x1, Pallas kernels, run_back(): pl.pallas_call(back_kernel, out_shape=(sd((384, 1024), BF), sd((384, 1024...  73.6 us
    pallas_call x1, Pallas kernels, run_leave(): pl.pallas_call(leave_kernel, out_shape=(*shapes, jax.ShapeDtypeStruct((8,...  6.48 us

profile of v6, /device:TPU:0, one launch (start us, length us, event | category | flops | bytes accessed | tf_op | source)
XLA Modules:
  0.0 293.1 jit_solution(17229210838241549162)
XLA Ops:
  1.3 1.3 pad_maximum_fusion.small
  2.5 0.7 select_convert_fusion
  3.3 0.6 reshape.28.tab
  3.8 98.7 %shard_map.221 = (bf16[384,3072]{1,0:T(8,128)(2,1)}, f32[384,128]{1,0:T(8,128)}, bf16[384,1024]{1,0:T(8,128)(2,1)}, f32[384,1024]{1,0:T(8,128)}, bf16[384,1024]{...) custom-call(s32[1]{0:T(128)S(6)} %copy.25.len_ref, ...), custom_call_target="tpu_custom_call" | custom-call | tf_op jit(solution)/shard_map/pallas_call | solution.py:691
  102.5 107.9 %shard_map.222 = (f32[384,1024]{1,0:T(8,128)}, f32[384,128]{1,0:T(8,128)}, bf16[384,1024]{1,0:T(8,128)(2,1)}, bf16[384,1024]{1,0:T(8,128)(2,1)}, bf16[2,256,512]...) custom-call(bf16[8,384,1024]{2,1,0:T(8,128)(2,1)} %get-tuple-element, ...), custom_call_target="tpu_custom_call" | custom-call | tf_op jit(solution)/shard_map/pallas_call | solution.py:1074
  210.4 73.6 %shard_map.223 = (bf16[384,1024]{1,0:T(8,128)(2,1)}, f32[384,1024]{1,0:T(8,128)}, f32[32,3072]{1,0:T(8,128)}, f32[32,1024]{1,0:T(8,128)}, f32[32,128]{1,0:T(8,12...) custom-call(s32[1]{0:T(128)S(6)} %copy.25.len_ref, ...), custom_call_target="tpu_custom_call" | custom-call | tf_op jit(solution)/shard_map/pallas_call | solution.py:1429
  284.1 6.5 %shard_map.224 = (bf16[384,1024]{1,0:T(8,128)(2,1)}, f32[384,1024]{1,0:T(8,128)}, f32[32,3072]{1,0:T(8,128)}, f32[32,1024]{1,0:T(8,128)}, f32[32,4096]{1,0:T(8,1...) custom-call(bf16[384,1024]{1,0:T(8,128)(2,1)} %get-tuple-element.71.refs_0_, ...), custom_call_target="tpu_custom_call" | custom-call | tf_op jit(solution)/shard_map/pallas_call | solution.py:1474
  290.6 1.2 slice_bitcast_fusion
  291.8 1.3 slice_bitcast_fusion.1
